TPU v7x, 256 devices: a whole 4x4x8 slice. The times are simulated.
256 devices in a mesh: ang: 32 (over z, y), rad: 8 (over x, core).
Axes of the slice: x: 4, y: 4, z: 8, core: 2. Of those that a mesh axis runs over, the one named last changes fastest.
Arguments:
- field: bfloat16 [27, 128, 65536], P(None, 'rad', 'ang'), may hold values from -6 to 6
- velocity: bfloat16 [3, 128, 65536], P(None, 'rad', 'ang'), may hold values from -6 to 6
- send_cells: int32 [32, 32, 128], P('ang'), may hold values from 0 to 1791
- block_size: int32 [32, 32], P('ang'), may hold values from 0 to 128, as said below
- donor_slot: int32 [4, 8192], P(None, 'ang'), may hold values from 0 to 4095, as said below
- intersection_weight: float32 [4, 8192], P(None, 'ang'), may hold values from 0.05 to 0.6
- block_inverse: float32 [8, 16, 16], replicated
- lower_coupling: float32 [7], replicated, may hold values from -0.45 to -0.3
- upper_coupling: float32 [7], replicated, may hold values from -0.45 to -0.3
Outputs:
- solution: bfloat16 [27, 128, 65536], P(None, 'rad', 'ang')
Inputs may be any that keep to these rules, and one draw needn't show every extreme that they name: `block_size`: only tiles of the other panel send to a tile: each tile receives live lists from 2 to 8 tiles of the other panel, at least one of them with all 128 slots live; one tile receives full lists from 8 tiles. `donor_slot`: every donor names a live slot, j < block_size[q, s]; the four donors of a ghost cell lie in one donor tile of its recipient or in two of them.
All inputs are finite; a program needn't handle non-finite values.
Results may differ from a plain program's by a relative error of at most 0.003.
Values may be sent and summed in bfloat16 or wider, within the bound.
No kernel may reach another device: no remote copies, remote signals or barrier semaphores. Data moves between devices by JAX's collectives and lax.ppermute only.
A program may use at most 128 MiB of HBM per device.

v0:
```python
import jax
import jax.numpy as jnp
from jax import lax
from jax.sharding import PartitionSpec as P

induction = 0.5
highest = lax.Precision.HIGHEST


def cross_source(field, velocity):
    shape = field.shape
    groups = field.reshape((shape[0] // 3, 3) + shape[1:])
    first = velocity[1] * groups[:, 2] - velocity[2] * groups[:, 1]
    second = velocity[2] * groups[:, 0] - velocity[0] * groups[:, 2]
    third = velocity[0] * groups[:, 1] - velocity[1] * groups[:, 0]
    crossed = jnp.stack([first, second, third], axis=1).reshape(shape)
    return field + induction * crossed


def alternate(even_part, odd_part):
    return jnp.stack([even_part, odd_part], axis=1).reshape(-1)


def interface_matrix(block_inverse, lower_coupling, upper_coupling):
    blocks = block_inverse.shape[0]
    nothing = jnp.zeros((1,), jnp.float32)
    upper = jnp.concatenate([upper_coupling, nothing])
    lower = jnp.concatenate([nothing, lower_coupling])
    right = block_inverse[:, :, -1] * upper[:, None]
    left = block_inverse[:, :, 0] * lower[:, None]
    zero_vector = jnp.zeros((blocks,), jnp.float32)
    size = 2 * blocks
    ahead_two = alternate(right[:, 0], zero_vector)
    ahead_one = alternate(zero_vector, right[:, -1])
    behind_one = alternate(left[:, 0], zero_vector)
    behind_two = alternate(zero_vector, left[:, -1])
    matrix = jnp.eye(size, dtype=jnp.float32)
    matrix = matrix + jnp.diag(ahead_two[: size - 2], 2) + jnp.diag(ahead_one[: size - 1], 1)
    matrix = matrix + jnp.diag(behind_one[1:], -1) + jnp.diag(behind_two[2:], -2)
    return (matrix, right, left)


def invert_small(matrix):
    size = matrix.shape[0]
    identity = jnp.eye(size, dtype=jnp.float32)
    positions = jnp.arange(size, dtype=jnp.int32)

    def pivot_step(pivot_row, state):
        work_left, work_right = state
        row_left = lax.dynamic_slice_in_dim(work_left, pivot_row, 1, 0)
        row_right = lax.dynamic_slice_in_dim(work_right, pivot_row, 1, 0)
        pivot = lax.dynamic_slice_in_dim(row_left, pivot_row, 1, 1)
        row_left = row_left / pivot
        row_right = row_right / pivot
        column = lax.dynamic_slice_in_dim(work_left, pivot_row, 1, 1)
        onehot = (positions == pivot_row)[:, None]
        factor = jnp.where(onehot, 0.0, column)
        work_left = jnp.where(onehot, row_left, work_left - factor * row_left)
        work_right = jnp.where(onehot, row_right, work_right - factor * row_right)
        return (work_left, work_right)

    return lax.fori_loop(0, size, pivot_step, (matrix, identity))[1]


def shards(
    field,
    velocity,
    send_cells,
    block_size,
    donor_slot,
    intersection_weight,
    block_inverse,
    lower_coupling,
    upper_coupling,
):
    channels, block_depth, tile_cells = field.shape
    tile_count = send_cells.shape[1]
    capacity = send_cells.shape[2]
    ghosts = donor_slot.shape[1]
    inner = tile_cells - ghosts
    cells = send_cells[0].reshape(tile_count * capacity)
    live = (jnp.arange(capacity, dtype=jnp.int32)[None, :] < block_size[0][:, None]).reshape(
        tile_count * capacity
    )
    slots = donor_slot.reshape(4 * ghosts)
    interior = cross_source(
        field[:, :, :inner].astype(jnp.float32), velocity[:, :, :inner].astype(jnp.float32)
    )
    packed = jnp.where(live[None, None, :], jnp.take(interior, cells, axis=2), 0.0)
    packed = packed.reshape(channels, block_depth, tile_count, capacity)
    donors = lax.all_to_all(
        packed.astype(jnp.bfloat16), "ang", split_axis=2, concat_axis=2, tiled=True
    ).astype(packed.dtype)
    flat = donors.reshape(donors.shape[0], donors.shape[1], tile_count * capacity)
    picked = jnp.take(flat, slots, axis=2).reshape(donors.shape[0], donors.shape[1], 4, ghosts)
    ghost = jnp.sum(picked * intersection_weight[None, None], axis=2)
    filled = jnp.concatenate([interior, ghost], axis=2)
    block_index = lax.axis_index("rad")
    own_inverse = lax.dynamic_index_in_dim(block_inverse, block_index, 0, keepdims=False)
    spread = jnp.einsum("ij,cja->cia", own_inverse, filled, precision=highest)
    edges = jnp.stack([spread[:, 0, :], spread[:, -1, :]], axis=0)
    matrix, right, left = interface_matrix(block_inverse, lower_coupling, upper_coupling)
    blocks = block_inverse.shape[0]
    size = 2 * blocks
    inverse = invert_small(matrix)
    parity = alternate(jnp.ones((blocks,), jnp.float32), jnp.zeros((blocks,), jnp.float32))
    select = jnp.diag(parity[: size - 2], 2) + jnp.diag((1.0 - parity)[2:], -2)
    needed = jnp.dot(select, inverse, precision=highest)
    own_rows = lax.dynamic_slice_in_dim(needed, 2 * block_index, 2, 0)
    piece = lax.all_gather(edges, "rad", axis=0, tiled=True)
    weights_part = lax.slice_in_dim(own_rows, 0, piece.shape[0], axis=1)
    coupled = jnp.zeros_like(edges) + jnp.einsum(
        "pq,qca->pca", weights_part, piece, precision=highest
    )
    spike_right = lax.dynamic_index_in_dim(right, block_index, 0, keepdims=False)
    spike_left = lax.dynamic_index_in_dim(left, block_index, 0, keepdims=False)
    result = (
        spread
        - spike_right[None, :, None] * coupled[0][:, None, :]
        - spike_left[None, :, None] * coupled[1][:, None, :]
    )
    return result.astype(jnp.bfloat16)


def solution(mesh):
    in_specs = (
        P(None, "rad", "ang"),
        P(None, "rad", "ang"),
        P("ang", None, None),
        P("ang", None),
        P(None, "ang"),
        P(None, "ang"),
        P(),
        P(),
        P(),
    )
    out_specs = P(None, "rad", "ang")
    return jax.shard_map(shards, mesh=mesh, in_specs=in_specs, out_specs=out_specs, check_vma=False)
```

profile of v0, /device:TPU:33, one launch (start us, length us, event | category | flops | bytes accessed | tf_op | source)
XLA Modules:
  0.0 281.6 jit_solution(5292276408711413930)
XLA Ops:
  6.5 0.9 slice_convert_fusion.1
  7.5 1.7 slice_convert_fusion
  10.0 1.2 copy-done.2
  11.6 10.4 %copy.15 = bf16[27,16,1792]{0,1,2:T(8,128)(2,1)} copy(f32[27,16,1792]{2,1,0:T(8,128)S(1)} %bitcast_add_fusion) | data formatting | bytes 4644864 | tf_op jit(solution)/shard_map/add | solution.py:17
  22.1 35.0 %gather_fusion = bf16[4096,27,16]{1,2,0:T(8,128)(2,1)} fusion(bf16[27,16,1792]{0,1,2:T(8,128)(2,1)} %copy.15, s32[4096]{0:T(1024)S(1)} %broadcast_clamp_fusion), kind=kCustom, calls=%fused_computation | custom fusion | bytes 7094272 | tf_op jit(solution)/shard_map/jit(_take)/gather | solution.py:89
  57.0 19.9 %copy.16 = bf16[27,16,32,128]{3,1,0,2:T(8,128)(2,1)} copy(bf16[27,16,32,128]{0,1,3,2:T(8,128)(2,1)} %bitcast.71) | data formatting | bytes 7077888 | tf_op jit(solution)/shard_map/jit(_take)/gather | solution.py:89
  77.0 5.4 %select_convert_fusion = bf16[27,16,32,128]{3,1,0,2:T(8,128)(2,1)} fusion(bf16[27,16,32,128]{3,1,0,2:T(8,128)(2,1)} %copy.16, pred[32,128]{1,0:T(8,128)(4,1)S(1)} %get-tuple-element.163, pred[32,128]{1,0:T(8,128)(4,1)S(1)} %get-tuple-element.162), kind=kLoop, calls=%fused_computation.14 | loop fusion | flops 3538944 | bytes 7086080 | tf_op jit(solution)/shard_map/convert_element_type | solution.py:92
  82.4 11.0 %all-to-all-start = ((bf16[27,16,32,128]{3,1,0,2:T(8,128)(2,1)}), bf16[27,16,32,128]{3,1,0,2:T(8,128)(2,1)}, u32[]{:S(2)}, u32[]{:S(2)}) async-start(bf16[27,16,32,128]{3,1,0,2:T(8,128)(2,1)} %select_convert_fusion), calls=%async_computation | async-start | bytes 7077888 | tf_op jit(solution)/shard_map/all_to_all | solution.py:91
  95.9 76.3 %all-to-all-done = bf16[27,16,32,128]{3,1,0,2:T(8,128)(2,1)} async-done(((bf16[27,16,32,128]{3,1,0,2:T(8,128)(2,1)}), bf16[27,16,32,128]{3,1,0,2:T(8,128)(2,1)}, u32[]{:S(2)}, u32[]{:S(2)}) %all-to-all-start) | async-done | bytes 3538976 | tf_op jit(solution)/shard_map/all_to_all | solution.py:91
  172.2 19.4 %copy.17 = f32[27,16,32,128]{0,1,3,2:T(8,128)} copy(bf16[27,16,32,128]{3,1,0,2:T(8,128)(2,1)} %all-to-all-done) | data formatting | bytes 10616832 | tf_op jit(solution)/shard_map/reshape | solution.py:94
  191.6 20.0 %gather_fusion.1 = f32[1024,27,16]{1,2,0:T(8,128)} fusion(f32[27,16,4096]{0,1,2:T(8,128)} %bitcast.70, s32[1024]{0:T(1024)S(1)} %broadcast_clamp_fusion.1), kind=kCustom, calls=%fused_computation.1 | custom fusion | bytes 3543040 | tf_op jit(solution)/shard_map/jit(_take)/gather | solution.py:95
  211.7 8.4 %multiply_reduce_fusion = f32[27,16,256]{0,1,2:T(8,128)} fusion(f32[27,16,4,256]{0,1,3,2:T(8,128)} %bitcast.73, f32[4,256]{1,0:T(4,128)S(1)} %copy-done.6, pred[4,256]{1,0:T(4,128)(4,1)S(1)} %compare_and_fusion.1), kind=kLoop, calls=%fused_computation.13 | loop fusion | flops 1216512 | bytes 2216960 | tf_op jit(solution)/shard_map/reduce_sum | solution.py:96
  220.0 2.7 copy.18
  222.7 4.9 %fusion.11 = f32[27,16,2048]{2,1,0:T(8,128)S(1)} fusion(f32[27,16,256]{2,1,0:T(8,128)S(1)} %copy.18, f32[27,16,1792]{2,1,0:T(8,128)S(1)} %bitcast_add_fusion, f32[8,16,16]{2,1,0:T(8,128)} %param.17, s32[]{:T(128)S(6)} %select_n.138), kind=kOutput, calls=%fused_computation.24 | convolution fusion | flops 170754048 | bytes 7086084 | tf_op jit(solution)/shard_map/ij,cja->cia/dot_general | solution.py:100
  227.6 1.7 copy-done
  230.1 1.1 copy.21
  231.2 26.5 %while.19 = (s32[]{:T(128)}, f32[16,16]{0,1:T(8,128)S(1)}, f32[16,16]{0,1:T(8,128)S(1)}, s32[]{:T(128)}, s32[]{:T(128)}, /*index=5*/s32[]{:T(128)}) while((s32[]{:T(128)}, f32[16,16]{0,1:T(8,128)S(1)}, f32[16,16]{0,1:T(8,128)S(1)}, s32[]{:T(128)}, s32[]{:T(128)}, /*index=5*/s32[]{:T(128)}) %tuple.60), condition=%wide.region_2.3_spmd.clone, body=%wide.region_1.2_spmd.clone.sunk | while | flops 1619 | bytes 5837 | solution.py:62
  231.9 1.2 fusion.47
  233.9 0.9 fusion.47
  235.5 0.9 fusion.47
  237.1 0.9 fusion.47
  238.7 0.9 fusion.47
  240.4 0.9 fusion.47
  242.0 0.9 fusion.47
  243.6 0.9 fusion.47
  245.2 0.9 fusion.47
  255.0 0.9 fusion.47
  256.6 0.9 fusion.47
  257.7 0.9 fusion.19
  258.6 7.9 %all-gather.2.cloned.1.call-done = f32[16,27,2048]{2,1,0:T(8,128)} async-done(((f32[2,27,2048]{2,1,0:T(8,128)}), f32[16,27,2048]{2,1,0:T(8,128)}) %all-gather.2.cloned.1.call-update) | async-done | bytes 3538960 | tf_op jit(solution)/shard_map/all_gather | solution.py:110
  266.5 5.8 %fusion.9 = f32[2,27,2048]{2,0,1:T(2,128)S(1)} fusion(f32[16,27,2048]{2,1,0:T(8,128)} %all-gather.2.cloned.1.call-done, f32[16,16]{1,0:T(8,128)S(1)} %fusion.19, s32[]{:T(128)S(6)} %select_n.145), kind=kOutput, calls=%fused_computation.19 | convolution fusion | flops 21233664 | bytes 3982340 | tf_op jit(solution)/shard_map/pq,qca->pca/dot_general | solution.py:112
  272.9 1.9 subtract_convert_fusion
  (142 shorter events, 21.2 us)
Async XLA Ops:
  9.7 1.5 copy-start.2
  11.6 10.4 %copy-start.4 = (s32[1,32,128]{2,1,0:T(8,128)S(1)}, s32[1,32,128]{2,1,0:T(8,128)}, u32[]{:S(2)}) copy-start(s32[1,32,128]{2,1,0:T(8,128)} %param.13) | copy-start | bytes 49156
  57.0 19.9 %copy-start.12 = (s32[1,32]{1,0:T(1,128)S(1)}, s32[1,32]{1,0:T(1,128)}, u32[]{:S(2)}) copy-start(s32[1,32]{1,0:T(1,128)} %param.14) | copy-start | bytes 388
  82.4 11.3 %copy-start.5 = (s32[4,256]{1,0:T(4,128)S(1)}, s32[4,256]{1,0:T(4,128)}, u32[]{:S(2)}) copy-start(s32[4,256]{1,0:T(4,128)} %param.15) | copy-start | bytes 12292
  82.4 11.3 %copy-start.3 = (f32[8,16,16]{2,1,0:T(8,128)S(1)}, f32[8,16,16]{2,1,0:T(8,128)}, u32[]{:S(2)}) copy-start(f32[8,16,16]{2,1,0:T(8,128)} %param.17) | copy-start | bytes 24580
  82.4 11.6 %copy-start.14 = (f32[7]{0:T(128)S(1)}, f32[7]{0:T(128)}, u32[]{:S(2)}) copy-start(f32[7]{0:T(128)} %param.18) | copy-start | bytes 88
  82.4 11.9 %copy-start.15 = (f32[7]{0:T(128)S(1)}, f32[7]{0:T(128)}, u32[]{:S(2)}) copy-start(f32[7]{0:T(128)} %param.19) | copy-start | bytes 88
  82.4 12.1 %copy-start.13 = (pred[2]{0:T(512)(128)(4,1)S(1)}, pred[2]{0:T(512)(128)(4,1)}, u32[]{:S(2)}) copy-start(pred[2]{0:T(512)(128)(4,1)} %constant.175.clone.1) | copy-start | bytes 10
  82.4 12.6 %copy-start.11 = (pred[8,2]{1,0:T(8,128)(4,1)S(1)}, pred[8,2]{1,0:T(8,128)(4,1)}, u32[]{:S(2)}) copy-start(pred[8,2]{1,0:T(8,128)(4,1)} %constant.177.clone.1) | copy-start | bytes 52
  82.4 89.8 %all-to-all-start = ((bf16[27,16,32,128]{3,1,0,2:T(8,128)(2,1)}), bf16[27,16,32,128]{3,1,0,2:T(8,128)(2,1)}, u32[]{:S(2)}, u32[]{:S(2)}) async-start(bf16[27,16,32,128]{3,1,0,2:T(8,128)(2,1)} %select_convert_fusion), calls=%async_computation | async-start | bytes 7077888 | tf_op jit(solution)/shard_map/all_to_all | solution.py:91
  93.4 173.1 %all-gather.2.cloned.1.call-start = ((), (), s32[]{:S(2)}) async-start(), calls=%async_computation.1 | async-start | bytes 4718592 | tf_op jit(solution)/shard_map/all_gather | solution.py:110
  95.2 96.4 %copy-start.9 = (s32[16]{0:T(128)}, s32[16]{0:T(128)S(1)}, u32[]{:S(2)}) copy-start(s32[16]{0:T(128)S(1)} %get-tuple-element.166) | copy-start | bytes 196
  95.2 96.4 %copy-start.10 = (s32[16]{0:T(128)}, s32[16]{0:T(128)S(1)}, u32[]{:S(2)}) copy-start(s32[16]{0:T(128)S(1)} %get-tuple-element.167) | copy-start | bytes 196
  191.6 20.1 %copy-start.6 = (f32[4,256]{1,0:T(4,128)S(1)}, f32[4,256]{1,0:T(4,128)}, u32[]{:S(2)}) copy-start(f32[4,256]{1,0:T(4,128)} %param.16) | copy-start | bytes 12292
  227.6 1.7 copy-start
  231.2 41.6 %copy-start.1 = (f32[27,16,2048]{2,1,0:T(8,128)S(1)}, f32[27,16,2048]{2,1,0:T(8,128)}, u32[]{:S(2)}) copy-start(f32[27,16,2048]{2,1,0:T(8,128)} %copy-done) | copy-start | bytes 10616836
  258.6 14.2 %copy-start.7 = (f32[16]{0:T(128)S(1)}, f32[16]{0:T(128)}, u32[]{:S(2)}) copy-start(f32[16]{0:T(128)} %get-tuple-element.164) | copy-start | bytes 196
  258.6 14.2 %copy-start.8 = (f32[16]{0:T(128)S(1)}, f32[16]{0:T(128)}, u32[]{:S(2)}) copy-start(f32[16]{0:T(128)} %get-tuple-element.165) | copy-start | bytes 196
Sparse Core Ops, SparseCore 0:
  231.3 35.1 all-gather.1
where the time goes:
time: 285 us; the launch traced here: 282 us
  local copies, waits for them, and re-layouts  124 us (44%)
  waiting for transfers between devices  84.2 us (30%)
  other arithmetic  36.1 us (13%)
  between operations  13.7 us (5%)
  matrix products  11.5 us (4%)
  starting transfers between devices  11.2 us (4%)
    all_to_all x1, waiting for transfers between devices, shards(): lax.all_to_all(packed.astype(jnp.bfloat16), 'ang', split_axis=2, concat_a...  76.3 us
    gather x2, local copies, waits for them, and re-layouts, shards(): jnp.take(interior, cells, axis=2)  54.8 us
    gather x1, local copies, waits for them, and re-layouts, shards(): jnp.take(flat, slots, axis=2)  20 us
    reshape x1, local copies, waits for them, and re-layouts, shards(): donors.reshape(donors.shape[0], donors.shape[1], tile_count * capacity)  19.4 us
    div x16, other arithmetic, pivot_step(): row_left = row_left / pivot  14.2 us
    all_to_all x1, starting transfers between devices, shards(): lax.all_to_all(packed.astype(jnp.bfloat16), 'ang', split_axis=2, concat_a...  11 us
    dynamic_slice x16, local copies, waits for them, and re-layouts, pivot_step(): pivot = lax.dynamic_slice_in_dim(row_left, pivot_row, 1, 1)  10.4 us
    add x1, local copies, waits for them, and re-layouts, cross_source(): return field + induction * crossed  10.4 us
  transfers between devices with their start and end apart: 2, of which 2 were waited for; matrix products, arithmetic and copies ran while one was open for 10% of the time, Pallas kernels for 0%

commit v1 on v0

v1 whole, which is shorter than its diff:
```python
import jax
import jax.numpy as jnp
from jax import lax
from jax.experimental import pallas as pl
from jax.experimental.pallas import tpu as pltpu
from jax.sharding import PartitionSpec as P

f32 = jnp.float32
bf16 = jnp.bfloat16
highest = lax.Precision.HIGHEST
induction = 0.5

CHANNELS = 27
DEPTH = 16
ROWS = CHANNELS * DEPTH
CELLS = 2048
RIM = 256
INNER = CELLS - RIM
CAP = 128
TILES = 32
BLOCKS = 8
PARTS = 3
PART_ROWS = ROWS // PARTS
EDGE = 64
GROUP = 8
VMEM_LIMIT = 48 * 1024 * 1024

SERVES = ((3, 1, 2, 0), (2, 0, 3, 1))


def params():
    return pltpu.CompilerParams(vmem_limit_bytes=VMEM_LIMIT)


def iota(shape, axis):
    return lax.broadcasted_iota(jnp.int32, shape, axis)


def split(value):
    high = value.astype(bf16)
    return high, (value - high.astype(f32)).astype(bf16)


def dot(left, right):
    return jnp.dot(left, right, preferred_element_type=f32)


def spread_kernel(place, field, velocity, block_inverse, spread, rounded, high_mat, low_mat):
    @pl.when(pl.program_id(0) == 0)
    def _():
        own = block_inverse[place[1]]
        size = PART_ROWS
        rows = (iota((size, DEPTH), 0) % DEPTH == iota((size, DEPTH), 1)).astype(f32)
        columns = (iota((DEPTH, size), 1) % DEPTH == iota((DEPTH, size), 0)).astype(f32)
        tiled = jnp.dot(jnp.dot(rows, own, precision=highest), columns, precision=highest)
        same = iota((size, size), 0) // DEPTH == iota((size, size), 1) // DEPTH
        high, low = split(jnp.where(same, tiled, 0.0))
        high_mat[...] = high
        low_mat[...] = low

    flow = [velocity[DEPTH * i : DEPTH * (i + 1), :INNER].astype(f32) for i in range(3)]
    parts = []
    for m in range(PART_ROWS // (3 * DEPTH)):
        f = [
            field[DEPTH * (3 * m + i) : DEPTH * (3 * m + i + 1), :INNER].astype(f32)
            for i in range(3)
        ]
        for i in range(3):
            j, k = (i + 1) % 3, (i + 2) % 3
            parts.append(f[i] + induction * (flow[j] * f[k] - flow[k] * f[j]))
    source_high, source_low = split(jnp.concatenate(parts, axis=0))
    result = dot(high_mat[...], source_high) + dot(high_mat[...], source_low)
    result = result + dot(low_mat[...], source_high)
    spread[...] = result
    rounded[...] = result.astype(bf16)


def edge_select():
    row, column = iota((EDGE, ROWS), 0), iota((EDGE, ROWS), 1)
    wanted = (row % 32) * DEPTH + (row // 32) * (DEPTH - 1)
    return ((row % 32 < CHANNELS) & (column == wanted)).astype(f32).astype(bf16)


def list_kernel(place, block_size, cells, rounded, lists, edges):
    step = pl.program_id(0)
    row = place[0] // 4
    panel, half = row // 4, (row // 2) % 2
    member, y = step // 4, step % 4
    served = (3 - 2 * member - half, 2 - 2 * member + half)
    wanted = []
    for m in range(2):
        tile = (4 * (1 - panel) + served[m]) * 4 + y
        listed = cells[0, pl.ds(tile, 1), :]
        wanted.append(jnp.where(iota((1, CAP), 1) < block_size[0, tile], listed, -1))
    wanted = jnp.concatenate(wanted, axis=1)
    total = jnp.zeros((ROWS, 2 * CAP), f32)
    for first in range(0, INNER, 256):
        hot = (iota((256, 2 * CAP), 0) + first == wanted).astype(f32).astype(bf16)
        total = total + dot(rounded[:, first : first + 256], hot)
    lists[0] = total.astype(bf16)

    start = pl.multiple_of(jnp.minimum(step, INNER // 256 - 1) * 256, 256)
    edges[0] = dot(edge_select(), rounded[:, pl.ds(start, 256)]).astype(bf16)


def weight_kernel(place, first, second, weights):
    base = (place[0] // GROUP) * (GROUP * CAP)
    for m, meta in enumerate((first, second)):
        slots = meta[0:4, :].astype(jnp.int32) - base
        for t in range(GROUP):
            position = iota((CAP, RIM), 0) + t * CAP
            value = jnp.zeros((CAP, RIM), f32)
            for d in range(4):
                value = value + jnp.where(slots[d : d + 1, :] == position, meta[4 + d : 5 + d, :], 0.0)
            high, low = split(value)
            weights[m, t * CAP : (t + 1) * CAP, :RIM] = high
            weights[m, t * CAP : (t + 1) * CAP, RIM:] = low


def setup_kernel(place, lower, upper, corner, block_inverse, needed, spikes):
    size = 2 * BLOCKS
    shape = (size, 128)
    row, lane = iota(shape, 0), iota(shape, 1)
    work = ((row == lane) | (row + size == lane)).astype(f32)
    for k in range(BLOCKS):
        for b in range(2):
            i = b * (DEPTH - 1)
            here = row == 2 * k + b
            if k < BLOCKS - 1:
                value = corner[k, i, DEPTH - 1] * upper[k]
                work = jnp.where(here & (lane == 2 * k + 2), value, work)
            if k > 0:
                value = corner[k, i, 0] * lower[k - 1]
                work = jnp.where(here & (lane == 2 * k - 1), value, work)
    for p in range(size):
        column = jnp.sum(jnp.where(lane == p, work, 0.0), axis=1, keepdims=True)
        chosen = work[p : p + 1, :] / column[p : p + 1, :]
        work = jnp.where(row == p, chosen, work - column * chosen)
    up = jnp.concatenate([work[2:, :], jnp.zeros((2, 128), f32)], axis=0)
    down = jnp.concatenate([jnp.zeros((2, 128), f32), work[:-2, :]], axis=0)
    needed[...] = jnp.where(row % 2 == 0, up, down)

    k = place[1]
    ahead = jnp.where(k < BLOCKS - 1, upper[jnp.minimum(k, BLOCKS - 2)], 0.0)
    behind = jnp.where(k > 0, lower[jnp.maximum(k - 1, 0)], 0.0)
    rows = (iota((ROWS, DEPTH), 0) % DEPTH == iota((ROWS, DEPTH), 1)).astype(f32)
    tiled = jnp.dot(rows, block_inverse[k], precision=highest)
    right, left = tiled[:, DEPTH - 1 :] * ahead, tiled[:, :1] * behind
    channel, lane = iota((ROWS, 128), 0) // DEPTH, iota((ROWS, 128), 1)
    full = jnp.where(lane % 64 == channel, right, 0.0)
    full = full + jnp.where(lane % 64 == channel + 32, left, 0.0)
    high, low = split(full)
    spikes[...] = jnp.where(lane < 64, high.astype(f32), low.astype(f32)).astype(bf16)


def partial_kernel(lists, weights, first, second, first_edges, second_edges):
    for m, (partial, edges) in enumerate(((first, first_edges), (second, second_edges))):
        values = [lists[t, :, m * CAP : (m + 1) * CAP] for t in range(GROUP)]
        both = dot(jnp.concatenate(values, axis=1), weights[m])
        result = (both[:, :RIM] + both[:, RIM:]).astype(bf16)
        partial[...] = result
        edges[...] = dot(edge_select(), result).astype(bf16)


def join_kernel(whole, first, second, edges):
    edges[0] = (first[...].astype(f32) + second[...].astype(f32)).astype(bf16)


def solve_kernel(needed, edges, coupled):
    values = []
    for k in range(BLOCKS):
        for b in range(2):
            values.append(edges[k, 32 * b : 32 * b + 32, :].astype(f32))
    for k in range(BLOCKS):
        for b in range(2):
            total = needed[2 * k + b, 2 * BLOCKS] * values[0]
            for q in range(1, 2 * BLOCKS):
                total = total + needed[2 * k + b, 2 * BLOCKS + q] * values[q]
            coupled[k, 32 * b : 32 * b + 32, :] = total.astype(bf16)


def finish_kernel(spread, first, second, spikes, coupled, result):
    twice = jnp.concatenate([coupled[0], coupled[0]], axis=0)
    correction = dot(spikes[...], twice)

    @pl.when(pl.program_id(0) < INNER // 256)
    def _():
        result[...] = (spread[...] - correction).astype(bf16)

    @pl.when(pl.program_id(0) == INNER // 256)
    def _():
        ghost = first[...].astype(f32) + second[...].astype(f32)
        result[...] = (ghost - correction).astype(bf16)


SMEM = pl.BlockSpec(memory_space=pltpu.SMEM)


def whole(shape):
    return pl.BlockSpec(shape, lambda i: (0,) * len(shape))


def crossing(m, backwards):
    pairs = []
    for z in range(8):
        panel, i = divmod(z, 4)
        target = 4 * (1 - panel) + SERVES[m][i]
        for y in range(4):
            pair = (z * 4 + y, target * 4 + y)
            pairs.append(pair[::-1] if backwards else pair)
    return pairs


def shards(
    field,
    velocity,
    send_cells,
    block_size,
    donor_slot,
    intersection_weight,
    block_inverse,
    lower_coupling,
    upper_coupling,
):
    field = field.reshape(ROWS, CELLS)
    velocity = velocity.reshape(3 * DEPTH, CELLS)
    place = jnp.stack([lax.axis_index("ang"), lax.axis_index("rad")]).astype(jnp.int32)
    groups = [list(range(g * GROUP, (g + 1) * GROUP)) for g in range(TILES // GROUP)]

    meta = jnp.concatenate([donor_slot.astype(f32), intersection_weight], axis=0)
    metas = [lax.ppermute(meta, "ang", crossing(m, True)) for m in range(2)]

    spread, rounded = pl.pallas_call(
        spread_kernel,
        grid=(PARTS,),
        in_specs=[
            SMEM,
            pl.BlockSpec((PART_ROWS, CELLS), lambda i: (i, 0)),
            whole((3 * DEPTH, CELLS)),
            whole((BLOCKS, DEPTH, DEPTH)),
        ],
        out_specs=[
            pl.BlockSpec((PART_ROWS, INNER), lambda i: (i, 0)),
            pl.BlockSpec((PART_ROWS, INNER), lambda i: (i, 0)),
        ],
        out_shape=[
            jax.ShapeDtypeStruct((ROWS, INNER), f32),
            jax.ShapeDtypeStruct((ROWS, INNER), bf16),
        ],
        scratch_shapes=[pltpu.VMEM((PART_ROWS, PART_ROWS), bf16)] * 2,
        compiler_params=params(),
        name="spread",
    )(place, field, velocity, block_inverse)

    lists, edges = pl.pallas_call(
        list_kernel,
        grid=(GROUP,),
        in_specs=[SMEM, SMEM, whole((1, TILES, CAP)), whole((ROWS, INNER))],
        out_specs=[
            pl.BlockSpec((1, ROWS, 2 * CAP), lambda i: (i, 0, 0)),
            pl.BlockSpec((1, EDGE, 256), lambda i: (i, 0, 0)),
        ],
        out_shape=[
            jax.ShapeDtypeStruct((GROUP, ROWS, 2 * CAP), bf16),
            jax.ShapeDtypeStruct((GROUP, EDGE, 256), bf16),
        ],
        compiler_params=params(),
        name="lists",
    )(place, block_size, send_cells, rounded)

    donors = lax.all_to_all(lists, "ang", 0, 0, axis_index_groups=groups)

    weights = pl.pallas_call(
        weight_kernel,
        in_specs=[SMEM, pl.BlockSpec(memory_space=pltpu.VMEM), pl.BlockSpec(memory_space=pltpu.VMEM)],
        out_specs=pl.BlockSpec(memory_space=pltpu.VMEM),
        out_shape=jax.ShapeDtypeStruct((2, GROUP * CAP, 2 * RIM), bf16),
        compiler_params=params(),
        name="weights",
    )(place, *metas)

    needed, spikes = pl.pallas_call(
        setup_kernel,
        in_specs=[SMEM, SMEM, SMEM, SMEM, pl.BlockSpec(memory_space=pltpu.VMEM)],
        out_specs=[pl.BlockSpec(memory_space=pltpu.VMEM)] * 2,
        out_shape=[
            jax.ShapeDtypeStruct((2 * BLOCKS, 128), f32),
            jax.ShapeDtypeStruct((ROWS, 128), bf16),
        ],
        compiler_params=params(),
        name="setup",
    )(place, lower_coupling, upper_coupling, block_inverse, block_inverse)

    outs = pl.pallas_call(
        partial_kernel,
        in_specs=[pl.BlockSpec(memory_space=pltpu.VMEM)] * 2,
        out_specs=[pl.BlockSpec(memory_space=pltpu.VMEM)] * 4,
        out_shape=[jax.ShapeDtypeStruct((ROWS, RIM), bf16)] * 2
        + [jax.ShapeDtypeStruct((EDGE, RIM), bf16)] * 2,
        compiler_params=params(),
        name="partial",
    )(donors, weights)

    ghost_edges = [lax.ppermute(outs[2 + m], "ang", crossing(m, False)) for m in range(2)]
    ghosts = [lax.ppermute(outs[m], "ang", crossing(m, False)) for m in range(2)]

    edges = pl.pallas_call(
        join_kernel,
        grid=(1,),
        in_specs=[pl.BlockSpec(memory_space=pl.ANY), whole((EDGE, RIM)), whole((EDGE, RIM))],
        out_specs=pl.BlockSpec((1, EDGE, 256), lambda i: (GROUP - 1, 0, 0)),
        out_shape=jax.ShapeDtypeStruct((GROUP, EDGE, 256), bf16),
        input_output_aliases={0: 0},
        compiler_params=params(),
        name="join",
    )(edges, *ghost_edges)

    edges = lax.all_to_all(edges, "rad", 0, 0)
    coupled = pl.pallas_call(
        solve_kernel,
        in_specs=[SMEM, pl.BlockSpec(memory_space=pltpu.VMEM)],
        out_specs=pl.BlockSpec(memory_space=pltpu.VMEM),
        out_shape=jax.ShapeDtypeStruct((BLOCKS, EDGE, 256), bf16),
        compiler_params=params(),
        name="solve",
    )(needed, edges)
    coupled = lax.all_to_all(coupled, "rad", 0, 0)

    result = pl.pallas_call(
        finish_kernel,
        grid=(CELLS // 256,),
        in_specs=[
            pl.BlockSpec((ROWS, 256), lambda i: (0, jnp.minimum(i, INNER // 256 - 1))),
            whole((ROWS, RIM)),
            whole((ROWS, RIM)),
            whole((ROWS, 128)),
            pl.BlockSpec((1, EDGE, 256), lambda i: (i, 0, 0)),
        ],
        out_specs=pl.BlockSpec((ROWS, 256), lambda i: (0, i)),
        out_shape=jax.ShapeDtypeStruct((ROWS, CELLS), bf16),
        compiler_params=params(),
        name="finish",
    )(spread, *ghosts, spikes, coupled)
    return result.reshape(CHANNELS, DEPTH, CELLS)


def solution(mesh):
    in_specs = (
        P(None, "rad", "ang"),
        P(None, "rad", "ang"),
        P("ang", None, None),
        P("ang", None),
        P(None, "ang"),
        P(None, "ang"),
        P(),
        P(),
        P(),
    )
    out_specs = P(None, "rad", "ang")
    return jax.shard_map(shards, mesh=mesh, in_specs=in_specs, out_specs=out_specs, check_vma=False)
```

time: 285 us -> 107 us (0.38)
  local copies, waits for them, and re-layouts: 124 us -> 5.15 us
  waiting for transfers between devices: 84.2 us -> 45 us
  other arithmetic: 36.1 us -> 0.09 us
  Pallas kernels: 0 us -> 26.1 us
  starting transfers between devices: 11.2 us -> 29.9 us
  between operations: 13.7 us -> 0.1 us
  matrix products: 11.5 us -> 0 us
    gather x3 -> x0, local copies, waits for them, and re-layouts: 74.9 us -> none  [the longest x2 54.8 us: shards(): jnp.take(interior, cells, axis=2)]
    all_to_all x1 -> x3, waiting for transfers between devices: 76.3 us -> 3.43 us  [the longest x1 3.43 us: shards(): edges = lax.all_to_all(edges, 'rad', 0, 0)]
    ppermute x0 -> x6, waiting for transfers between devices: none -> 41.6 us  [the longest x2 18.8 us: shards(): metas = [lax.ppermute(meta, 'ang', crossing(m, True)) for m in range(2)]]
    pallas_call x0 -> x8, Pallas kernels: none -> 26.1 us  [the longest x1 6.48 us: shards(): pl.pallas_call(list_kernel, grid=(GROUP,), in_specs=[SMEM, SMEM, whole((1...]
    reshape x2 -> x0, local copies, waits for them, and re-layouts: 19.5 us -> none  [the longest x1 19.4 us: shards(): donors.reshape(donors.shape[0], donors.shape[1], tile_count * capacity)]
    div x16 -> x0, other arithmetic: 14.2 us -> none  [pivot_step(): row_left = row_left / pivot]
    ppermute x0 -> x6, starting transfers between devices: none -> 12.8 us  [the longest x2 6.1 us: shards(): metas = [lax.ppermute(meta, 'ang', crossing(m, True)) for m in range(2)]]
    dot_general x3 -> x0, matrix products: 11.5 us -> none  [the longest x1 5.78 us: shards(): jnp.einsum('pq,qca->pca', weights_part, piece, precision=highest)]
  transfers between devices with their start and end apart: 2 -> 9, of which waited for: 2 -> 5; matrix products, arithmetic and copies ran while one was open for 10% -> 0% of each run, Pallas kernels for 0% -> 4%
where the time goes in v1:
time: 107 us; the launch traced here: 106 us
  waiting for transfers between devices  45 us (42%)
  starting transfers between devices  29.9 us (28%)
  Pallas kernels  26.1 us (24%)
  local copies, waits for them, and re-layouts  5.15 us (5%)
    ppermute x2, waiting for transfers between devices, shards(): metas = [lax.ppermute(meta, 'ang', crossing(m, True)) for m in range(2)]  18.8 us
    ppermute x2, waiting for transfers between devices, shards(): lax.ppermute(outs[m], 'ang', crossing(m, False))  18.4 us
    all_to_all x1, starting transfers between devices, shards(): edges = lax.all_to_all(edges, 'rad', 0, 0)  7.29 us
    pallas_call x1, Pallas kernels, shards(): pl.pallas_call(list_kernel, grid=(GROUP,), in_specs=[SMEM, SMEM, whole((1...  6.48 us
    ppermute x2, starting transfers between devices, shards(): metas = [lax.ppermute(meta, 'ang', crossing(m, True)) for m in range(2)]  6.1 us
    all_to_all x1, starting transfers between devices, shards(): donors = lax.all_to_all(lists, 'ang', 0, 0, axis_index_groups=groups)  5.51 us
    unnamed x22, local copies, waits for them, and re-layouts  5.15 us
    pallas_call x1, Pallas kernels, shards(): pl.pallas_call(spread_kernel, grid=(PARTS,), in_specs=[SMEM, pl.BlockSpec...  4.52 us
  transfers between devices with their start and end apart: 9, of which 5 were waited for; matrix products, arithmetic and copies ran while one was open for 0% of the time, Pallas kernels for 4%

profile of v1, /device:TPU:33, one launch (start us, length us, event | category | flops | bytes accessed | tf_op | source)
XLA Modules:
  0.0 106.4 jit_solution(5212758007414303784)
XLA Ops:
  0.0 0.1 pad_add_fusion.place
  0.1 1.5 %copy-done.1 = bf16[27,16,2048]{2,1,0:T(8,128)(2,1)S(1)} copy-done((bf16[27,16,2048]{2,1,0:T(8,128)(2,1)S(1)}, bf16[27,16,2048]{2,1,0:T(8,128)(2,1)}, u32[]{:S(2)}) %copy-start.1) | copy-done | bytes 1769496
  1.6 0.8 copy-done.2
  2.4 0.9 copy-done.4
  3.3 4.5 %spread.1 = (f32[432,1792]{1,0:T(8,128)}, bf16[432,1792]{1,0:T(8,128)(2,1)S(1)}) custom-call(s32[2]{0:T(128)S(1)} %pad_add_fusion.place, bf16[432,2048]{1,0:T(8,128)(2,1)S(1)} %bitcast.5, bf16[48,2048]{1,0:T(8,128)(2,1)S(1)} %bitcast.6, f32[8,16,16]{2,1,0:T(8,128)S(1)} %copy-done.2), custom_call_target="tpu_custom_call" | custom-call | tf_op jit(solution)/shard_map/spread/pallas_call | solution.py:233
  7.8 6.5 %lists.1 = (bf16[8,432,256]{2,1,0:T(8,128)(2,1)}, bf16[8,64,256]{2,1,0:T(8,128)(2,1)}) custom-call(s32[2]{0:T(128)S(1)} %pad_add_fusion.place, s32[1,32]{1,0:T(1,128)S(1)} %copy-done.6, s32[1,32,128]{2,1,0:T(8,128)S(1)} %copy-done.5, bf16[432,1792]{1,0:T(8,128)(2,1)S(1)} %get-tuple-element.16.rounded), custom_call_target="tpu_custom_call" | custom-call | tf_op jit(solution)/shard_map/lists/pallas_call | solution.py:255
  14.3 5.5 %all-to-all-start = ((bf16[8,432,256]{2,1,0:T(8,128)(2,1)}), bf16[8,432,256]{2,1,0:T(8,128)(2,1)}, u32[]{:S(2)}, u32[]{:S(2)}) async-start(bf16[8,432,256]{2,1,0:T(8,128)(2,1)} %get-tuple-element.17), calls=%async_computation | async-start | bytes 3538944 | tf_op jit(solution)/shard_map/all_to_all | solution.py:271
  19.9 6.1 %collective-permute-start = (f32[8,256]{1,0:T(8,128)S(1)}, f32[8,256]{1,0:T(8,128)S(1)}, u32[]{:S(2)}, u32[]{:S(2)}) collective-permute-start(f32[8,256]{1,0:T(8,128)S(1)} %pad_maximum_fusion), channel_id=1, source_target_pairs={{224,0},{232,8},{240,16},{248,24},{160,32},{168,40},{176,48},{184,... | collective-permute-start | bytes 24584 | tf_op jit(solution)/shard_map/ppermute | solution.py:231
  26.0 0.0 collective-permute-start.1
  26.0 18.8 %collective-permute-done.first = f32[8,256]{1,0:T(8,128)S(1)} collective-permute-done((f32[8,256]{1,0:T(8,128)S(1)}, f32[8,256]{1,0:T(8,128)S(1)}, u32[]{:S(2)}, u32[]{:S(2)}) %collective-permute-start) | collective-permute-done | bytes 8224 | tf_op jit(solution)/shard_map/ppermute | solution.py:231
  44.8 0.0 collective-permute-done.1.second
  44.8 1.6 %weights.1 = bf16[2,1024,512]{2,1,0:T(8,128)(2,1)S(1)} custom-call(s32[2]{0:T(128)S(1)} %pad_add_fusion.place, f32[8,256]{1,0:T(8,128)S(1)} %collective-permute-done.first, f32[8,256]{1,0:T(8,128)S(1)} %collective-permute-done.1.second), custom_call_target="tpu_custom_call" | custom-call | tf_op jit(solution)/shard_map/weights/pallas_call | solution.py:273
  46.4 0.0 copy-start.3
  46.4 0.0 copy-start.7
  46.4 0.0 copy-start.8
  46.4 0.0 all-to-all-done.lists
  46.4 3.7 %partial.1 = (bf16[432,256]{1,0:T(8,128)(2,1)S(1)}, bf16[432,256]{1,0:T(8,128)(2,1)S(1)}, bf16[64,256]{1,0:T(8,128)(2,1)S(1)}, bf16[64,256]{1,0:T(8,128)(2,1)S(1)}) custom-call(bf16[8,432,256]{2,1,0:T(8,128)(2,1)} %all-to-all-done.lists, bf16[2,1024,512]{2,1,0:T(8,128)(2,1)S(1)} %weights.1), custom_call_target="tpu_custom_call" | custom-call | tf_op jit(solution)/shard_map/partial/pallas_call | solution.py:294
  50.2 1.9 %collective-permute-start.4 = (bf16[64,256]{1,0:T(8,128)(2,1)S(1)}, bf16[64,256]{1,0:T(8,128)(2,1)S(1)}, u32[]{:S(2)}, u32[]{:S(2)}) collective-permute-start(bf16[64,256]{1,0:T(8,128)(2,1)S(1)} %get-tuple-element.23), channel_id=1, source_target_pairs={{0,224},{8,232},{16,240},{24,248},{32,160},{40,168},{48,176},{56,1... | collective-permute-start | bytes 98312 | tf_op jit(solution)/shard_map/ppermute | solution.py:304
  52.1 1.0 collective-permute-start.5
  53.1 4.3 %collective-permute-done.4.first = bf16[64,256]{1,0:T(8,128)(2,1)S(1)} collective-permute-done((bf16[64,256]{1,0:T(8,128)(2,1)S(1)}, bf16[64,256]{1,0:T(8,128)(2,1)S(1)}, u32[]{:S(2)}, u32[]{:S(2)}) %collective-permute-start.4) | collective-permute-done | bytes 32800 | tf_op jit(solution)/shard_map/ppermute | solution.py:304
  57.5 0.0 collective-permute-done.5.second
  57.5 0.6 join.1
  58.1 7.3 %all-to-all-start.1 = ((bf16[8,64,256]{2,1,0:T(8,128)(2,1)}), bf16[8,64,256]{2,1,0:T(8,128)(2,1)S(1)}, u32[]{:S(2)}, u32[]{:S(2)}) async-start(bf16[8,64,256]{2,1,0:T(8,128)(2,1)} %join.1), calls=%async_computation.1 | async-start | bytes 524288 | tf_op jit(solution)/shard_map/all_to_all | solution.py:318
  65.4 3.1 %setup.1 = (f32[16,128]{1,0:T(8,128)S(1)}, bf16[432,128]{1,0:T(8,128)(2,1)S(1)}) custom-call(s32[2]{0:T(128)S(1)} %pad_add_fusion.place, f32[7]{0:T(128)S(1)} %copy-done.7, f32[7]{0:T(128)S(1)} %copy-done.8, f32[8,16,16]{2,1,0:T(8,128)S(1)} %copy-done.3, f32[8,16,16]{2,1,0:T(8,128)S(1)} %copy-done.3), custom_call_target="tpu_custom_call" | custom-call | tf_op jit(solution)/shard_map/setup/pallas_call | solution.py:282
  68.5 3.4 %all-to-all-done.1.edges = bf16[8,64,256]{2,1,0:T(8,128)(2,1)S(1)} async-done(((bf16[8,64,256]{2,1,0:T(8,128)(2,1)}), bf16[8,64,256]{2,1,0:T(8,128)(2,1)S(1)}, u32[]{:S(2)}, u32[]{:S(2)}) %all-to-all-start.1) | async-done | bytes 262176 | tf_op jit(solution)/shard_map/all_to_all | solution.py:318
  71.9 2.0 %solve.1 = bf16[8,64,256]{2,1,0:T(8,128)(2,1)} custom-call(f32[16,128]{1,0:T(8,128)S(1)} %get-tuple-element.21.needed, bf16[8,64,256]{2,1,0:T(8,128)(2,1)S(1)} %all-to-all-done.1.edges), custom_call_target="tpu_custom_call" | custom-call | tf_op jit(solution)/shard_map/solve/pallas_call | solution.py:319
  73.8 4.4 %all-to-all-start.2 = ((bf16[8,64,256]{2,1,0:T(8,128)(2,1)}), bf16[8,64,256]{2,1,0:T(8,128)(2,1)S(1)}, u32[]{:S(2)}, u32[]{:S(2)}) async-start(bf16[8,64,256]{2,1,0:T(8,128)(2,1)} %solve.1), calls=%async_computation.2 | async-start | bytes 524288 | tf_op jit(solution)/shard_map/all_to_all | solution.py:327
  78.2 3.7 %collective-permute-start.2 = (bf16[432,256]{1,0:T(8,128)(2,1)S(1)}, bf16[432,256]{1,0:T(8,128)(2,1)S(1)}, u32[]{:S(2)}, u32[]{:S(2)}) collective-permute-start(bf16[432,256]{1,0:T(8,128)(2,1)S(1)} %get-tuple-element.18), channel_id=1, source_target_pairs={{0,224},{8,232},{16,240},{24,248},{32,160},{40,168},{48,176},{56,1... | collective-permute-start | bytes 663560 | tf_op jit(solution)/shard_map/ppermute | solution.py:305
  81.9 11.8 %collective-permute-done.2.first = bf16[432,256]{1,0:T(8,128)(2,1)S(1)} collective-permute-done((bf16[432,256]{1,0:T(8,128)(2,1)S(1)}, bf16[432,256]{1,0:T(8,128)(2,1)S(1)}, u32[]{:S(2)}, u32[]{:S(2)}) %collective-permute-start.2) | collective-permute-done | bytes 221216 | tf_op jit(solution)/shard_map/ppermute | solution.py:305
  93.7 6.6 %collective-permute-done.3.second = bf16[432,256]{1,0:T(8,128)(2,1)S(1)} collective-permute-done((bf16[432,256]{1,0:T(8,128)(2,1)S(1)}, bf16[432,256]{1,0:T(8,128)(2,1)S(1)}, u32[]{:S(2)}, u32[]{:S(2)}) %collective-permute-start.3) | collective-permute-done | bytes 221216 | tf_op jit(solution)/shard_map/ppermute | solution.py:305
  100.4 1.9 %copy-done = f32[432,1792]{1,0:T(8,128)S(1)} copy-done((f32[432,1792]{1,0:T(8,128)S(1)}, f32[432,1792]{1,0:T(8,128)}, u32[]{:S(2)}) %copy-start) | copy-done | bytes 3096600
  102.2 4.2 %finish.1 = bf16[432,2048]{1,0:T(8,128)(2,1)} custom-call(f32[432,1792]{1,0:T(8,128)S(1)} %copy-done, bf16[432,256]{1,0:T(8,128)(2,1)S(1)} %collective-permute-done.2.first, bf16[432,256]{1,0:T(8,128)(2,1)S(1)} %collective-permute-done.3.second, bf16[432,128]{1,0:T(8,128)(2,1)S(1)} %get-tuple-element.20.spikes, bf16[8,64,256]{2,1,0:T(8,128)(2,1)S(1)} %all-to-all-done.2.coupled), custom_call_target="tpu_custom_call" | custom-call | tf_op jit(solution)/shard_map/finish/pallas_call | solution.py:329
  (19 shorter events, 0.0 us)
Async XLA Ops:
  0.0 7.8 %copy-start.6 = (s32[1,32]{1,0:T(1,128)S(1)}, s32[1,32]{1,0:T(1,128)}, u32[]{:S(2)}) copy-start(s32[1,32]{1,0:T(1,128)} %block_size.1) | copy-start | bytes 388
  0.0 7.8 %copy-start.5 = (s32[1,32,128]{2,1,0:T(8,128)S(1)}, s32[1,32,128]{2,1,0:T(8,128)}, u32[]{:S(2)}) copy-start(s32[1,32,128]{2,1,0:T(8,128)} %cells.1) | copy-start | bytes 49156
  0.1 1.5 %copy-start.1 = (bf16[27,16,2048]{2,1,0:T(8,128)(2,1)S(1)}, bf16[27,16,2048]{2,1,0:T(8,128)(2,1)}, u32[]{:S(2)}) copy-start(bf16[27,16,2048]{2,1,0:T(8,128)(2,1)} %param.9) | copy-start | bytes 5308420
  1.6 0.8 copy-start.2
  2.4 0.9 copy-start.4
  14.3 5.5 %copy-start.9 = (s32[4,256]{1,0:T(4,128)S(1)}, s32[4,256]{1,0:T(4,128)}, u32[]{:S(2)}) copy-start(s32[4,256]{1,0:T(4,128)} %param.13) | copy-start | bytes 12292
  14.3 5.5 %copy-start.10 = (f32[4,256]{1,0:T(4,128)S(1)}, f32[4,256]{1,0:T(4,128)}, u32[]{:S(2)}) copy-start(f32[4,256]{1,0:T(4,128)} %param.14) | copy-start | bytes 12292
  14.3 32.1 %all-to-all-start = ((bf16[8,432,256]{2,1,0:T(8,128)(2,1)}), bf16[8,432,256]{2,1,0:T(8,128)(2,1)}, u32[]{:S(2)}, u32[]{:S(2)}) async-start(bf16[8,432,256]{2,1,0:T(8,128)(2,1)} %get-tuple-element.17), calls=%async_computation | async-start | bytes 3538944 | tf_op jit(solution)/shard_map/all_to_all | solution.py:271
  19.9 24.9 %collective-permute-start = (f32[8,256]{1,0:T(8,128)S(1)}, f32[8,256]{1,0:T(8,128)S(1)}, u32[]{:S(2)}, u32[]{:S(2)}) collective-permute-start(f32[8,256]{1,0:T(8,128)S(1)} %pad_maximum_fusion), channel_id=1, source_target_pairs={{224,0},{232,8},{240,16},{248,24},{160,32},{168,40},{176,48},{184,... | collective-permute-start | bytes 24584 | tf_op jit(solution)/shard_map/ppermute | solution.py:231
  26.0 18.8 %collective-permute-start.1 = (f32[8,256]{1,0:T(8,128)S(1)}, f32[8,256]{1,0:T(8,128)S(1)}, u32[]{:S(2)}, u32[]{:S(2)}) collective-permute-start(f32[8,256]{1,0:T(8,128)S(1)} %pad_maximum_fusion), channel_id=1, source_target_pairs={{192,0},{200,8},{208,16},{216,24},{128,32},{136,40},{144,48},{152,... | collective-permute-start | bytes 24584 | tf_op jit(solution)/shard_map/ppermute | solution.py:231
  46.4 19.0 %copy-start.3 = (f32[8,16,16]{2,1,0:T(8,128)S(1)}, f32[8,16,16]{2,1,0:T(8,128)}, u32[]{:S(2)}) copy-start(f32[8,16,16]{2,1,0:T(8,128)} %block_inverse.3) | copy-start | bytes 24580
  46.4 19.0 %copy-start.7 = (f32[7]{0:T(128)S(1)}, f32[7]{0:T(128)}, u32[]{:S(2)}) copy-start(f32[7]{0:T(128)} %lower.1) | copy-start | bytes 88
  46.4 19.0 %copy-start.8 = (f32[7]{0:T(128)S(1)}, f32[7]{0:T(128)}, u32[]{:S(2)}) copy-start(f32[7]{0:T(128)} %upper.1) | copy-start | bytes 88
  50.2 7.3 %collective-permute-start.4 = (bf16[64,256]{1,0:T(8,128)(2,1)S(1)}, bf16[64,256]{1,0:T(8,128)(2,1)S(1)}, u32[]{:S(2)}, u32[]{:S(2)}) collective-permute-start(bf16[64,256]{1,0:T(8,128)(2,1)S(1)} %get-tuple-element.23), channel_id=1, source_target_pairs={{0,224},{8,232},{16,240},{24,248},{32,160},{40,168},{48,176},{56,1... | collective-permute-start | bytes 98312 | tf_op jit(solution)/shard_map/ppermute | solution.py:304
  52.1 5.3 %collective-permute-start.5 = (bf16[64,256]{1,0:T(8,128)(2,1)S(1)}, bf16[64,256]{1,0:T(8,128)(2,1)S(1)}, u32[]{:S(2)}, u32[]{:S(2)}) collective-permute-start(bf16[64,256]{1,0:T(8,128)(2,1)S(1)} %get-tuple-element.24), channel_id=1, source_target_pairs={{0,192},{8,200},{16,208},{24,216},{32,128},{40,136},{48,144},{56,1... | collective-permute-start | bytes 98312 | tf_op jit(solution)/shard_map/ppermute | solution.py:304
  58.1 13.8 %all-to-all-start.1 = ((bf16[8,64,256]{2,1,0:T(8,128)(2,1)}), bf16[8,64,256]{2,1,0:T(8,128)(2,1)S(1)}, u32[]{:S(2)}, u32[]{:S(2)}) async-start(bf16[8,64,256]{2,1,0:T(8,128)(2,1)} %join.1), calls=%async_computation.1 | async-start | bytes 524288 | tf_op jit(solution)/shard_map/all_to_all | solution.py:318
  73.8 26.5 %all-to-all-start.2 = ((bf16[8,64,256]{2,1,0:T(8,128)(2,1)}), bf16[8,64,256]{2,1,0:T(8,128)(2,1)S(1)}, u32[]{:S(2)}, u32[]{:S(2)}) async-start(bf16[8,64,256]{2,1,0:T(8,128)(2,1)} %solve.1), calls=%async_computation.2 | async-start | bytes 524288 | tf_op jit(solution)/shard_map/all_to_all | solution.py:327
  78.2 15.5 %collective-permute-start.2 = (bf16[432,256]{1,0:T(8,128)(2,1)S(1)}, bf16[432,256]{1,0:T(8,128)(2,1)S(1)}, u32[]{:S(2)}, u32[]{:S(2)}) collective-permute-start(bf16[432,256]{1,0:T(8,128)(2,1)S(1)} %get-tuple-element.18), channel_id=1, source_target_pairs={{0,224},{8,232},{16,240},{24,248},{32,160},{40,168},{48,176},{56,1... | collective-permute-start | bytes 663560 | tf_op jit(solution)/shard_map/ppermute | solution.py:305
  81.9 18.4 %collective-permute-start.3 = (bf16[432,256]{1,0:T(8,128)(2,1)S(1)}, bf16[432,256]{1,0:T(8,128)(2,1)S(1)}, u32[]{:S(2)}, u32[]{:S(2)}) collective-permute-start(bf16[432,256]{1,0:T(8,128)(2,1)S(1)} %get-tuple-element.19), channel_id=1, source_target_pairs={{0,192},{8,200},{16,208},{24,216},{32,128},{40,136},{48,144},{56,1... | collective-permute-start | bytes 663560 | tf_op jit(solution)/shard_map/ppermute | solution.py:305
  100.4 1.9 %copy-start = (f32[432,1792]{1,0:T(8,128)S(1)}, f32[432,1792]{1,0:T(8,128)}, u32[]{:S(2)}) copy-start(f32[432,1792]{1,0:T(8,128)} %get-tuple-element.15.spread) | copy-start | bytes 9289732

commit v2 on v1

--- a/solution.py
+++ b/solution.py
@@ -23,13 +23,13 @@
 PART_ROWS = ROWS // PARTS
 EDGE = 64
 GROUP = 8
-VMEM_LIMIT = 48 * 1024 * 1024
+EARLY = 160
 
 SERVES = ((3, 1, 2, 0), (2, 0, 3, 1))
 
 
-def params():
-    return pltpu.CompilerParams(vmem_limit_bytes=VMEM_LIMIT)
+def params(mebibytes):
+    return pltpu.CompilerParams(vmem_limit_bytes=mebibytes * 1024 * 1024)
 
 
 def iota(shape, axis):
@@ -81,40 +81,42 @@
     return ((row % 32 < CHANNELS) & (column == wanted)).astype(f32).astype(bf16)
 
 
-def list_kernel(place, block_size, cells, rounded, lists, edges):
-    step = pl.program_id(0)
-    row = place[0] // 4
+def list_kernel(place, block_size, cells, rounded, *outs):
+    row, y = place[0] // 4, place[0] % 4
     panel, half = row // 4, (row // 2) % 2
-    member, y = step // 4, step % 4
-    served = (3 - 2 * member - half, 2 - 2 * member + half)
-    wanted = []
-    for m in range(2):
-        tile = (4 * (1 - panel) + served[m]) * 4 + y
-        listed = cells[0, pl.ds(tile, 1), :]
-        wanted.append(jnp.where(iota((1, CAP), 1) < block_size[0, tile], listed, -1))
-    wanted = jnp.concatenate(wanted, axis=1)
-    total = jnp.zeros((ROWS, 2 * CAP), f32)
-    for first in range(0, INNER, 256):
-        hot = (iota((256, 2 * CAP), 0) + first == wanted).astype(f32).astype(bf16)
-        total = total + dot(rounded[:, first : first + 256], hot)
-    lists[0] = total.astype(bf16)
-
-    start = pl.multiple_of(jnp.minimum(step, INNER // 256 - 1) * 256, 256)
-    edges[0] = dot(edge_select(), rounded[:, pl.ds(start, 256)]).astype(bf16)
+    for r in range(GROUP):
+        member = (row + r // 4) % 2
+        served = (3 - 2 * member - half, 2 - 2 * member + half)
+        wanted = []
+        for m in range(2):
+            tile = (4 * (1 - panel) + served[m]) * 4 + (y + r) % 4
+            listed = cells[0, pl.ds(tile, 1), :]
+            wanted.append(jnp.where(iota((1, CAP), 1) < block_size[0, tile], listed, -1))
+        wanted = jnp.concatenate(wanted, axis=1)
+        total = jnp.zeros((ROWS, 2 * CAP), f32)
+        for first in range(0, INNER, 256):
+            hot = (iota((256, 2 * CAP), 0) + first == wanted).astype(f32).astype(bf16)
+            total = total + dot(rounded[:, first : first + 256], hot)
+        outs[r][...] = total.astype(bf16)
+
+    for j in range(BLOCKS):
+        first = min(j, INNER // 256 - 1) * 256
+        outs[GROUP][j] = dot(edge_select(), rounded[:, first : first + 256]).astype(bf16)
 
 
 def weight_kernel(place, first, second, weights):
-    base = (place[0] // GROUP) * (GROUP * CAP)
+    row, y = place[0] // 4, place[0] % 4
     for m, meta in enumerate((first, second)):
-        slots = meta[0:4, :].astype(jnp.int32) - base
-        for t in range(GROUP):
-            position = iota((CAP, RIM), 0) + t * CAP
+        slots = meta[0:4, :].astype(jnp.int32)
+        for r in range(GROUP):
+            tile = (row // 2 * 2 + (row + r // 4) % 2) * 4 + (y + 4 - r % 4) % 4
+            position = iota((CAP, RIM), 0) + tile * CAP
             value = jnp.zeros((CAP, RIM), f32)
             for d in range(4):
                 value = value + jnp.where(slots[d : d + 1, :] == position, meta[4 + d : 5 + d, :], 0.0)
             high, low = split(value)
-            weights[m, t * CAP : (t + 1) * CAP, :RIM] = high
-            weights[m, t * CAP : (t + 1) * CAP, RIM:] = low
+            weights[m, r * CAP : (r + 1) * CAP, :RIM] = high
+            weights[m, r * CAP : (r + 1) * CAP, RIM:] = low
 
 
 def setup_kernel(place, lower, upper, corner, block_inverse, needed, spikes):
@@ -153,17 +155,19 @@
     spikes[...] = jnp.where(lane < 64, high.astype(f32), low.astype(f32)).astype(bf16)
 
 
-def partial_kernel(lists, weights, first, second, first_edges, second_edges):
-    for m, (partial, edges) in enumerate(((first, first_edges), (second, second_edges))):
-        values = [lists[t, :, m * CAP : (m + 1) * CAP] for t in range(GROUP)]
+def partial_kernel(weights, *refs):
+    lists, outs = refs[:GROUP], refs[GROUP:]
+    for m in range(2):
+        values = [lists[r][:, m * CAP : (m + 1) * CAP] for r in range(GROUP)]
         both = dot(jnp.concatenate(values, axis=1), weights[m])
         result = (both[:, :RIM] + both[:, RIM:]).astype(bf16)
-        partial[...] = result
-        edges[...] = dot(edge_select(), result).astype(bf16)
-
-
-def join_kernel(whole, first, second, edges):
-    edges[0] = (first[...].astype(f32) + second[...].astype(f32)).astype(bf16)
+        outs[m][:EDGE, :] = dot(edge_select(), result).astype(bf16)
+        outs[m][EDGE:, :] = result[:EARLY, :]
+        outs[2 + m][...] = result[EARLY:, :]
+
+
+def join_kernel(first, second, edges):
+    edges[...] = (first[:EDGE, :].astype(f32) + second[:EDGE, :].astype(f32)).astype(bf16)
 
 
 def solve_kernel(needed, edges, coupled):
@@ -179,18 +183,31 @@
             coupled[k, 32 * b : 32 * b + 32, :] = total.astype(bf16)
 
 
-def finish_kernel(spread, first, second, spikes, coupled, result):
+def finish_kernel(spread, spikes, coupled, result):
     twice = jnp.concatenate([coupled[0], coupled[0]], axis=0)
-    correction = dot(spikes[...], twice)
-
-    @pl.when(pl.program_id(0) < INNER // 256)
-    def _():
-        result[...] = (spread[...] - correction).astype(bf16)
-
-    @pl.when(pl.program_id(0) == INNER // 256)
-    def _():
-        ghost = first[...].astype(f32) + second[...].astype(f32)
-        result[...] = (ghost - correction).astype(bf16)
+    result[...] = (spread[...] - dot(spikes[...], twice)).astype(bf16)
+
+
+def ghost_kernel(place, needed, whole, *refs):
+    del whole
+    early, late, edges, (spikes, result) = refs[:2], refs[2:4], refs[4:12], refs[12:]
+    own = place[1]
+    halves = []
+    for p in range(2):
+        total = jnp.zeros((32, RIM), f32)
+        for shift in range(BLOCKS):
+            k = (own + BLOCKS - shift) % BLOCKS
+            for b in range(2):
+                factor = needed[2 * own + p, 2 * BLOCKS + 2 * k + b]
+                total = total + factor * edges[shift][32 * b : 32 * b + 32, :].astype(f32)
+        halves.append(total)
+    high, low = split(jnp.concatenate(halves, axis=0))
+    both = jnp.concatenate([high, high], axis=0)
+    correction = dot(spikes[...], both) + dot(spikes[:, :EDGE], low)
+    ghost = early[0][EDGE:, :].astype(f32) + early[1][EDGE:, :].astype(f32)
+    result[:EARLY, :] = (ghost - correction[:EARLY, :]).astype(bf16)
+    ghost = late[0][...].astype(f32) + late[1][...].astype(f32)
+    result[EARLY:, :] = (ghost - correction[EARLY:, :]).astype(bf16)
 
 
 SMEM = pl.BlockSpec(memory_space=pltpu.SMEM)
@@ -208,6 +225,15 @@
         for y in range(4):
             pair = (z * 4 + y, target * 4 + y)
             pairs.append(pair[::-1] if backwards else pair)
+    return pairs
+
+
+def neighbours(r):
+    pairs = []
+    for z in range(8):
+        for y in range(4):
+            target = z // 2 * 2 + (z + r // 4) % 2
+            pairs.append((z * 4 + y, target * 4 + (y + r) % 4))
     return pairs
 
 
@@ -225,7 +251,6 @@
     field = field.reshape(ROWS, CELLS)
     velocity = velocity.reshape(3 * DEPTH, CELLS)
     place = jnp.stack([lax.axis_index("ang"), lax.axis_index("rad")]).astype(jnp.int32)
-    groups = [list(range(g * GROUP, (g + 1) * GROUP)) for g in range(TILES // GROUP)]
 
     meta = jnp.concatenate([donor_slot.astype(f32), intersection_weight], axis=0)
     metas = [lax.ppermute(meta, "ang", crossing(m, True)) for m in range(2)]
@@ -248,34 +273,28 @@
             jax.ShapeDtypeStruct((ROWS, INNER), bf16),
         ],
         scratch_shapes=[pltpu.VMEM((PART_ROWS, PART_ROWS), bf16)] * 2,
-        compiler_params=params(),
+        compiler_params=params(14),
         name="spread",
     )(place, field, velocity, block_inverse)
 
-    lists, edges = pl.pallas_call(
+    *lists, edges = pl.pallas_call(
         list_kernel,
-        grid=(GROUP,),
-        in_specs=[SMEM, SMEM, whole((1, TILES, CAP)), whole((ROWS, INNER))],
-        out_specs=[
-            pl.BlockSpec((1, ROWS, 2 * CAP), lambda i: (i, 0, 0)),
-            pl.BlockSpec((1, EDGE, 256), lambda i: (i, 0, 0)),
-        ],
-        out_shape=[
-            jax.ShapeDtypeStruct((GROUP, ROWS, 2 * CAP), bf16),
-            jax.ShapeDtypeStruct((GROUP, EDGE, 256), bf16),
-        ],
-        compiler_params=params(),
+        in_specs=[SMEM, SMEM] + [pl.BlockSpec(memory_space=pltpu.VMEM)] * 2,
+        out_specs=[pl.BlockSpec(memory_space=pltpu.VMEM)] * (GROUP + 1),
+        out_shape=[jax.ShapeDtypeStruct((ROWS, 2 * CAP), bf16)] * GROUP
+        + [jax.ShapeDtypeStruct((BLOCKS, EDGE, 256), bf16)],
+        compiler_params=params(14),
         name="lists",
     )(place, block_size, send_cells, rounded)
 
-    donors = lax.all_to_all(lists, "ang", 0, 0, axis_index_groups=groups)
+    donors = lists[:1] + [lax.ppermute(lists[r], "ang", neighbours(r)) for r in range(1, GROUP)]
 
     weights = pl.pallas_call(
         weight_kernel,
         in_specs=[SMEM, pl.BlockSpec(memory_space=pltpu.VMEM), pl.BlockSpec(memory_space=pltpu.VMEM)],
         out_specs=pl.BlockSpec(memory_space=pltpu.VMEM),
         out_shape=jax.ShapeDtypeStruct((2, GROUP * CAP, 2 * RIM), bf16),
-        compiler_params=params(),
+        compiler_params=params(8),
         name="weights",
     )(place, *metas)
 
@@ -287,60 +306,75 @@
             jax.ShapeDtypeStruct((2 * BLOCKS, 128), f32),
             jax.ShapeDtypeStruct((ROWS, 128), bf16),
         ],
-        compiler_params=params(),
+        compiler_params=params(4),
         name="setup",
     )(place, lower_coupling, upper_coupling, block_inverse, block_inverse)
 
-    outs = pl.pallas_call(
-        partial_kernel,
-        in_specs=[pl.BlockSpec(memory_space=pltpu.VMEM)] * 2,
-        out_specs=[pl.BlockSpec(memory_space=pltpu.VMEM)] * 4,
-        out_shape=[jax.ShapeDtypeStruct((ROWS, RIM), bf16)] * 2
-        + [jax.ShapeDtypeStruct((EDGE, RIM), bf16)] * 2,
-        compiler_params=params(),
-        name="partial",
-    )(donors, weights)
-
-    ghost_edges = [lax.ppermute(outs[2 + m], "ang", crossing(m, False)) for m in range(2)]
-    ghosts = [lax.ppermute(outs[m], "ang", crossing(m, False)) for m in range(2)]
-
-    edges = pl.pallas_call(
-        join_kernel,
-        grid=(1,),
-        in_specs=[pl.BlockSpec(memory_space=pl.ANY), whole((EDGE, RIM)), whole((EDGE, RIM))],
-        out_specs=pl.BlockSpec((1, EDGE, 256), lambda i: (GROUP - 1, 0, 0)),
-        out_shape=jax.ShapeDtypeStruct((GROUP, EDGE, 256), bf16),
-        input_output_aliases={0: 0},
-        compiler_params=params(),
-        name="join",
-    )(edges, *ghost_edges)
-
-    edges = lax.all_to_all(edges, "rad", 0, 0)
+    exchanged = lax.all_to_all(edges, "rad", 0, 0)
     coupled = pl.pallas_call(
         solve_kernel,
         in_specs=[SMEM, pl.BlockSpec(memory_space=pltpu.VMEM)],
         out_specs=pl.BlockSpec(memory_space=pltpu.VMEM),
         out_shape=jax.ShapeDtypeStruct((BLOCKS, EDGE, 256), bf16),
-        compiler_params=params(),
+        compiler_params=params(4),
         name="solve",
-    )(needed, edges)
+    )(needed, exchanged)
     coupled = lax.all_to_all(coupled, "rad", 0, 0)
 
     result = pl.pallas_call(
         finish_kernel,
-        grid=(CELLS // 256,),
+        grid=(INNER // 256,),
         in_specs=[
-            pl.BlockSpec((ROWS, 256), lambda i: (0, jnp.minimum(i, INNER // 256 - 1))),
-            whole((ROWS, RIM)),
-            whole((ROWS, RIM)),
+            pl.BlockSpec((ROWS, 256), lambda i: (0, i)),
             whole((ROWS, 128)),
             pl.BlockSpec((1, EDGE, 256), lambda i: (i, 0, 0)),
         ],
         out_specs=pl.BlockSpec((ROWS, 256), lambda i: (0, i)),
         out_shape=jax.ShapeDtypeStruct((ROWS, CELLS), bf16),
-        compiler_params=params(),
+        compiler_params=params(6),
         name="finish",
-    )(spread, *ghosts, spikes, coupled)
+    )(spread, spikes, coupled)
+
+    outs = pl.pallas_call(
+        partial_kernel,
+        in_specs=[pl.BlockSpec(memory_space=pltpu.VMEM)] * (GROUP + 1),
+        out_specs=[pl.BlockSpec(memory_space=pltpu.VMEM)] * 4,
+        out_shape=[jax.ShapeDtypeStruct((EDGE + EARLY, RIM), bf16)] * 2
+        + [jax.ShapeDtypeStruct((ROWS - EARLY, RIM), bf16)] * 2,
+        compiler_params=params(14),
+        name="partial",
+    )(weights, *donors)
+
+    early = [lax.ppermute(outs[m], "ang", crossing(m, False)) for m in range(2)]
+    late = [lax.ppermute(outs[2 + m], "ang", crossing(m, False)) for m in range(2)]
+
+    ghost_edges = pl.pallas_call(
+        join_kernel,
+        in_specs=[pl.BlockSpec(memory_space=pltpu.VMEM)] * 2,
+        out_specs=pl.BlockSpec(memory_space=pltpu.VMEM),
+        out_shape=jax.ShapeDtypeStruct((EDGE, RIM), bf16),
+        compiler_params=params(2),
+        name="join",
+    )(*early)
+    all_edges = [ghost_edges] + [
+        lax.ppermute(ghost_edges, "rad", [(k, (k + shift) % BLOCKS) for k in range(BLOCKS)])
+        for shift in range(1, BLOCKS)
+    ]
+
+    result = pl.pallas_call(
+        ghost_kernel,
+        grid=(1,),
+        in_specs=[SMEM, SMEM, pl.BlockSpec(memory_space=pl.ANY)]
+        + [whole((EDGE + EARLY, RIM))] * 2
+        + [whole((ROWS - EARLY, RIM))] * 2
+        + [whole((EDGE, RIM))] * BLOCKS
+        + [whole((ROWS, 128))],
+        out_specs=pl.BlockSpec((ROWS, RIM), lambda i: (0, INNER // RIM)),
+        out_shape=jax.ShapeDtypeStruct((ROWS, CELLS), bf16),
+        input_output_aliases={2: 0},
+        compiler_params=params(8),
+        name="ghosts",
+    )(place, needed, result, *early, *late, *all_edges, spikes)
     return result.reshape(CHANNELS, DEPTH, CELLS)
 
 

time: 107 us -> 97.7 us (0.913)
  waiting for transfers between devices: 45 us -> 15.9 us
  starting transfers between devices: 29.9 us -> 46.5 us
  local copies, waits for them, and re-layouts: 5.15 us -> 11.6 us
  Pallas kernels: 26.1 us -> 22.8 us
    ppermute x2 -> x16, starting transfers between devices: 3.73 us -> 24 us  [the longest x7 10.9 us: shards(): lax.ppermute(ghost_edges, 'rad', [(k, (k + shift) % BLOCKS) for k in rang...]
    ppermute x2, waiting for transfers between devices: 18.8 us -> 4.17 us  [shards(): metas = [lax.ppermute(meta, 'ang', crossing(m, True)) for m in range(2)]]
    all_to_all x2 -> x1, starting transfers between devices: 12.8 us -> 5.53 us  [shards(): exchanged = lax.all_to_all(edges, 'rad', 0, 0)]
    ppermute x2 -> x16, waiting for transfers between devices: 18.4 us -> 11.7 us  [the longest x2 11.7 us: shards(): early = [lax.ppermute(outs[m], 'ang', crossing(m, False)) for m in range(2)]]
    unnamed x22 -> x60, local copies, waits for them, and re-layouts: 5.15 us -> 11.6 us
    ppermute x2, waiting for transfers between devices: 4.32 us -> 0.01 us  [shards(): lax.ppermute(outs[2 + m], 'ang', crossing(m, False))]
    all_to_all x2 -> x1, waiting for transfers between devices: 3.43 us -> 0.01 us  [shards(): exchanged = lax.all_to_all(edges, 'rad', 0, 0)]
    all_to_all x1, starting transfers between devices: 4.35 us -> 6.8 us  [shards(): coupled = lax.all_to_all(coupled, 'rad', 0, 0)]
  transfers between devices with their start and end apart: 9 -> 22, of which waited for: 5 -> 3; matrix products, arithmetic and copies ran while one was open for 0% -> 0% of each run, Pallas kernels for 4% -> 14%
where the time goes in v2:
time: 97.7 us; the launch traced here: 97.1 us
  starting transfers between devices  46.5 us (48%)
  Pallas kernels  22.8 us (23%)
  waiting for transfers between devices  15.9 us (16%)
  local copies, waits for them, and re-layouts  11.6 us (12%)
    ppermute x2, waiting for transfers between devices, shards(): early = [lax.ppermute(outs[m], 'ang', crossing(m, False)) for m in range(2)]  11.7 us
    unnamed x60, local copies, waits for them, and re-layouts  11.6 us
    ppermute x7, starting transfers between devices, shards(): lax.ppermute(ghost_edges, 'rad', [(k, (k + shift) % BLOCKS) for k in rang...  10.9 us
    ppermute x7, starting transfers between devices, shards(): lax.ppermute(lists[r], 'ang', neighbours(r))  9.02 us
    all_to_all x1, starting transfers between devices, shards(): coupled = lax.all_to_all(coupled, 'rad', 0, 0)  6.8 us
    ppermute x2, starting transfers between devices, shards(): metas = [lax.ppermute(meta, 'ang', crossing(m, True)) for m in range(2)]  6.1 us
    all_to_all x1, starting transfers between devices, shards(): exchanged = lax.all_to_all(edges, 'rad', 0, 0)  5.53 us
    pallas_call x1, Pallas kernels, shards(): pl.pallas_call(list_kernel, in_specs=[SMEM, SMEM] + [pl.BlockSpec(memory_...  4.22 us
  transfers between devices with their start and end apart: 22, of which 3 were waited for; matrix products, arithmetic and copies ran while one was open for 0% of the time, Pallas kernels for 14%

profile of v2, /device:TPU:33, one launch (start us, length us, event | category | flops | bytes accessed | tf_op | source)
XLA Modules:
  0.0 97.1 jit_solution(3273908402364139628)
XLA Ops:
  0.1 1.5 %copy-done = bf16[27,16,2048]{2,1,0:T(8,128)(2,1)S(1)} copy-done((bf16[27,16,2048]{2,1,0:T(8,128)(2,1)S(1)}, bf16[27,16,2048]{2,1,0:T(8,128)(2,1)}, u32[]{:S(2)}) %copy-start) | copy-done | bytes 1769496
  1.6 0.8 copy-done.2
  2.4 0.9 copy-done.12
  3.3 3.3 %spread.1 = (f32[432,1792]{1,0:T(8,128)S(1)}, bf16[432,1792]{1,0:T(8,128)(2,1)S(1)}) custom-call(s32[2]{0:T(128)S(1)} %pad_add_fusion.place, bf16[432,2048]{1,0:T(8,128)(2,1)S(1)} %bitcast.5, bf16[48,2048]{1,0:T(8,128)(2,1)S(1)} %bitcast.6, f32[8,16,16]{2,1,0:T(8,128)S(1)} %copy-done.2), custom_call_target="tpu_custom_call" | custom-call | tf_op jit(solution)/shard_map/spread/pallas_call | solution.py:258
  6.7 4.2 %lists.1 = (bf16[432,256]{1,0:T(8,128)(2,1)S(1)}, bf16[432,256]{1,0:T(8,128)(2,1)}, bf16[432,256]{1,0:T(8,128)(2,1)}, bf16[432,256]{1,0:T(8,128)(2,1)S(1)}, bf16...) custom-call(s32[2]{0:T(128)S(1)} %pad_add_fusion.place, ...), custom_call_target="tpu_custom_call" | custom-call | tf_op jit(solution)/shard_map/lists/pallas_call | solution.py:280
  11.6 0.7 copy-done.10
  12.3 0.7 copy-done.24
  15.1 1.3 %collective-permute-start.2 = (bf16[432,256]{1,0:T(8,128)(2,1)}, bf16[432,256]{1,0:T(8,128)(2,1)}, u32[]{:S(2)}, u32[]{:S(2)}) collective-permute-start(bf16[432,256]{1,0:T(8,128)(2,1)} %get-tuple-element.28), channel_id=1, source_target_pairs={{0,8},{8,16},{16,24},{24,0},{32,40},{40,48},{48,56},{56,32},{64,72... | collective-permute-start | bytes 663560 | tf_op jit(solution)/shard_map/ppermute | solution.py:290
  16.4 2.6 %collective-permute-start.3 = (bf16[432,256]{1,0:T(8,128)(2,1)}, bf16[432,256]{1,0:T(8,128)(2,1)}, u32[]{:S(2)}, u32[]{:S(2)}) collective-permute-start(bf16[432,256]{1,0:T(8,128)(2,1)} %get-tuple-element.29), channel_id=1, source_target_pairs={{0,16},{8,24},{16,0},{24,8},{32,48},{40,56},{48,32},{56,40},{64,80... | collective-permute-start | bytes 663560 | tf_op jit(solution)/shard_map/ppermute | solution.py:290
  19.0 5.5 %all-to-all-start = ((bf16[8,64,256]{2,1,0:T(8,128)(2,1)}), bf16[8,64,256]{2,1,0:T(8,128)(2,1)S(1)}, u32[]{:S(2)}, u32[]{:S(2)}) async-start(bf16[8,64,256]{2,1,0:T(8,128)(2,1)} %copy-done.9), calls=%async_computation | async-start | bytes 524288 | tf_op jit(solution)/shard_map/all_to_all | solution.py:313
  24.6 6.1 %collective-permute-start = (f32[8,256]{1,0:T(8,128)S(1)}, f32[8,256]{1,0:T(8,128)S(1)}, u32[]{:S(2)}, u32[]{:S(2)}) collective-permute-start(f32[8,256]{1,0:T(8,128)S(1)} %pad_maximum_fusion), channel_id=1, source_target_pairs={{224,0},{232,8},{240,16},{248,24},{160,32},{168,40},{176,48},{184,... | collective-permute-start | bytes 24584 | tf_op jit(solution)/shard_map/ppermute | solution.py:256
  30.7 1.1 %collective-permute-start.4 = (bf16[432,256]{1,0:T(8,128)(2,1)}, bf16[432,256]{1,0:T(8,128)(2,1)}, u32[]{:S(2)}, u32[]{:S(2)}) collective-permute-start(bf16[432,256]{1,0:T(8,128)(2,1)} %copy-done.27), channel_id=1, source_target_pairs={{0,24},{8,0},{16,8},{24,16},{32,56},{40,32},{48,40},{56,48},{64,88... | collective-permute-start | bytes 663560 | tf_op jit(solution)/shard_map/ppermute | solution.py:290
  32.1 4.2 %collective-permute-done.1.second = f32[8,256]{1,0:T(8,128)S(1)} collective-permute-done((f32[8,256]{1,0:T(8,128)S(1)}, f32[8,256]{1,0:T(8,128)S(1)}, u32[]{:S(2)}, u32[]{:S(2)}) %collective-permute-start.1) | collective-permute-done | bytes 8224 | tf_op jit(solution)/shard_map/ppermute | solution.py:256
  36.3 3.1 %collective-permute-start.7 = (bf16[432,256]{1,0:T(8,128)(2,1)}, bf16[432,256]{1,0:T(8,128)(2,1)}, u32[]{:S(2)}, u32[]{:S(2)}) collective-permute-start(bf16[432,256]{1,0:T(8,128)(2,1)} %copy-done.24), channel_id=1, source_target_pairs={{0,48},{8,56},{16,32},{24,40},{32,16},{40,24},{48,0},{56,8},{64,11... | collective-permute-start | bytes 663560 | tf_op jit(solution)/shard_map/ppermute | solution.py:290
  40.0 3.0 %setup.1 = (f32[16,128]{1,0:T(8,128)S(1)}, bf16[432,128]{1,0:T(8,128)(2,1)S(1)}) custom-call(s32[2]{0:T(128)S(1)} %pad_add_fusion.place, f32[7]{0:T(128)S(1)} %copy-done.21, f32[7]{0:T(128)S(1)} %copy-done.22, f32[8,16,16]{2,1,0:T(8,128)S(1)} %copy-done.3, f32[8,16,16]{2,1,0:T(8,128)S(1)} %copy-done.3), custom_call_target="tpu_custom_call" | custom-call | tf_op jit(solution)/shard_map/setup/pallas_call | solution.py:301
  43.7 1.3 %solve.1 = bf16[8,64,256]{2,1,0:T(8,128)(2,1)S(1)} custom-call(f32[16,128]{1,0:T(8,128)S(1)} %get-tuple-element.22.needed, bf16[8,64,256]{2,1,0:T(8,128)(2,1)S(1)} %all-to-all-done.edges), custom_call_target="tpu_custom_call" | custom-call | tf_op jit(solution)/shard_map/solve/pallas_call | solution.py:314
  45.6 6.8 %all-to-all-start.1 = ((bf16[8,64,256]{2,1,0:T(8,128)(2,1)}), bf16[8,64,256]{2,1,0:T(8,128)(2,1)S(1)}, u32[]{:S(2)}, u32[]{:S(2)}) async-start(bf16[8,64,256]{2,1,0:T(8,128)(2,1)} %copy-done.1), calls=%async_computation.1 | async-start | bytes 524288 | tf_op jit(solution)/shard_map/all_to_all | solution.py:322
  52.4 1.6 %weights.1 = bf16[2,1024,512]{2,1,0:T(8,128)(2,1)S(1)} custom-call(s32[2]{0:T(128)S(1)} %pad_add_fusion.place, f32[8,256]{1,0:T(8,128)S(1)} %collective-permute-done.first, f32[8,256]{1,0:T(8,128)S(1)} %collective-permute-done.1.second), custom_call_target="tpu_custom_call" | custom-call | tf_op jit(solution)/shard_map/weights/pallas_call | solution.py:292
  54.1 3.7 %partial.1 = (bf16[224,256]{1,0:T(8,128)(2,1)S(1)}, bf16[224,256]{1,0:T(8,128)(2,1)S(1)}, bf16[272,256]{1,0:T(8,128)(2,1)S(1)}, bf16[272,256]{1,0:T(8,128)(2,1)S(1)}) custom-call(bf16[2,1024,512]{2,1,0:T(8,128)(2,1)S(1)} %weights.1, bf16[432,256]{1,0:T(8,128)(2,1)S(1)} %copy-done.11, bf16[432,256]{1,0:T(8,128)(2,1)} %collective-permute-done.2.refs_1_, ...), custom_call_target="tpu_custom_call" | custom-call | tf_op jit(solution)/shard_map/partial/pallas_call | solution.py:338
  57.8 2.4 %collective-permute-start.9 = (bf16[224,256]{1,0:T(8,128)(2,1)S(1)}, bf16[224,256]{1,0:T(8,128)(2,1)S(1)}, u32[]{:S(2)}, u32[]{:S(2)}) collective-permute-start(bf16[224,256]{1,0:T(8,128)(2,1)S(1)} %get-tuple-element.35), channel_id=1, source_target_pairs={{0,224},{8,232},{16,240},{24,248},{32,160},{40,168},{48,176},{56,1... | collective-permute-start | bytes 344072 | tf_op jit(solution)/shard_map/ppermute | solution.py:348
  60.2 1.6 %collective-permute-start.10 = (bf16[224,256]{1,0:T(8,128)(2,1)S(1)}, bf16[224,256]{1,0:T(8,128)(2,1)S(1)}, u32[]{:S(2)}, u32[]{:S(2)}) collective-permute-start(bf16[224,256]{1,0:T(8,128)(2,1)S(1)} %get-tuple-element.36), channel_id=1, source_target_pairs={{0,192},{8,200},{16,208},{24,216},{32,128},{40,136},{48,144},{56,1... | collective-permute-start | bytes 344072 | tf_op jit(solution)/shard_map/ppermute | solution.py:348
  61.9 2.9 %collective-permute-start.11 = (bf16[272,256]{1,0:T(8,128)(2,1)S(1)}, bf16[272,256]{1,0:T(8,128)(2,1)S(1)}, u32[]{:S(2)}, u32[]{:S(2)}) collective-permute-start(bf16[272,256]{1,0:T(8,128)(2,1)S(1)} %get-tuple-element.37), channel_id=1, source_target_pairs={{0,224},{8,232},{16,240},{24,248},{32,160},{40,168},{48,176},{56,1... | collective-permute-start | bytes 417800 | tf_op jit(solution)/shard_map/ppermute | solution.py:349
  64.8 1.2 %collective-permute-start.12 = (bf16[272,256]{1,0:T(8,128)(2,1)S(1)}, bf16[272,256]{1,0:T(8,128)(2,1)S(1)}, u32[]{:S(2)}, u32[]{:S(2)}) collective-permute-start(bf16[272,256]{1,0:T(8,128)(2,1)S(1)} %get-tuple-element.38), channel_id=1, source_target_pairs={{0,192},{8,200},{16,208},{24,216},{32,128},{40,136},{48,144},{56,1... | collective-permute-start | bytes 417800 | tf_op jit(solution)/shard_map/ppermute | solution.py:349
  66.3 11.4 %collective-permute-done.10.second.refs_1_ = bf16[224,256]{1,0:T(8,128)(2,1)S(1)} collective-permute-done((bf16[224,256]{1,0:T(8,128)(2,1)S(1)}, bf16[224,256]{1,0:T(8,128)(2,1)S(1)}, u32[]{:S(2)}, u32[]{:S(2)}) %collective-permute-start.10) | collective-permute-done | bytes 114720 | tf_op jit(solution)/shard_map/ppermute | solution.py:348
  77.7 3.3 %collective-permute-start.13 = (bf16[64,256]{1,0:T(8,128)(2,1)S(1)}, bf16[64,256]{1,0:T(8,128)(2,1)S(1)}, u32[]{:S(2)}, u32[]{:S(2)}) collective-permute-start(bf16[64,256]{1,0:T(8,128)(2,1)S(1)} %join.1.refs_4_), channel_id=1, source_target_pairs={{0,1},{1,2},{2,3},{3,4},{4,5},{5,6},{6,7},{7,0},{8,9},{9,10},{10,1... | collective-permute-start | bytes 98312 | tf_op jit(solution)/shard_map/ppermute | solution.py:360
  81.0 1.2 %collective-permute-start.14 = (bf16[64,256]{1,0:T(8,128)(2,1)S(1)}, bf16[64,256]{1,0:T(8,128)(2,1)S(1)}, u32[]{:S(2)}, u32[]{:S(2)}) collective-permute-start(bf16[64,256]{1,0:T(8,128)(2,1)S(1)} %join.1.refs_4_), channel_id=1, source_target_pairs={{0,2},{1,3},{2,4},{3,5},{4,6},{5,7},{6,0},{7,1},{8,10},{9,11},{10,... | collective-permute-start | bytes 98312 | tf_op jit(solution)/shard_map/ppermute | solution.py:360
  82.2 1.6 %collective-permute-start.15 = (bf16[64,256]{1,0:T(8,128)(2,1)S(1)}, bf16[64,256]{1,0:T(8,128)(2,1)}, u32[]{:S(2)}, u32[]{:S(2)}) collective-permute-start(bf16[64,256]{1,0:T(8,128)(2,1)S(1)} %join.1.refs_4_), channel_id=1, source_target_pairs={{0,3},{1,4},{2,5},{3,6},{4,7},{5,0},{6,1},{7,2},{8,11},{9,12},{10,... | collective-permute-start | bytes 98312 | tf_op jit(solution)/shard_map/ppermute | solution.py:360
  85.6 2.3 %collective-permute-start.17 = (bf16[64,256]{1,0:T(8,128)(2,1)S(1)}, bf16[64,256]{1,0:T(8,128)(2,1)}, u32[]{:S(2)}, u32[]{:S(2)}) collective-permute-start(bf16[64,256]{1,0:T(8,128)(2,1)S(1)} %join.1.refs_4_), channel_id=1, source_target_pairs={{0,5},{1,6},{2,7},{3,0},{4,1},{5,2},{6,3},{7,4},{8,13},{9,14},{10,... | collective-permute-start | bytes 98312 | tf_op jit(solution)/shard_map/ppermute | solution.py:360
  89.1 1.3 %collective-permute-start.19 = (bf16[64,256]{1,0:T(8,128)(2,1)S(1)}, bf16[64,256]{1,0:T(8,128)(2,1)}, u32[]{:S(2)}, u32[]{:S(2)}) collective-permute-start(bf16[64,256]{1,0:T(8,128)(2,1)S(1)} %join.1.refs_4_), channel_id=1, source_target_pairs={{0,7},{1,0},{2,1},{3,2},{4,3},{5,4},{6,5},{7,6},{8,15},{9,8},{10,9... | collective-permute-start | bytes 98312 | tf_op jit(solution)/shard_map/ppermute | solution.py:360
  90.5 0.9 copy-done.7
  91.4 3.7 %finish.1.whole = bf16[432,2048]{1,0:T(8,128)(2,1)} custom-call(f32[432,1792]{1,0:T(8,128)S(1)} %get-tuple-element.23.spread, bf16[432,128]{1,0:T(8,128)(2,1)S(1)} %copy-done.7, bf16[8,64,256]{2,1,0:T(8,128)(2,1)S(1)} %all-to-all-done.1.coupled), custom_call_target="tpu_custom_call" | custom-call | tf_op jit(solution)/shard_map/finish/pallas_call | solution.py:324
  95.2 1.9 %ghosts.1 = bf16[432,2048]{1,0:T(8,128)(2,1)} custom-call(s32[2]{0:T(128)S(1)} %pad_add_fusion.place, f32[16,128]{1,0:T(8,128)S(1)} %get-tuple-element.22.needed, bf16[432,2048]{1,0:T(8,128)(2,1)} %finish.1.whole, bf16[224,256]{1,0:T(8,128)(2,1)S(1)} %collective-permute-done.9.first.refs_0_, ...), custom_call_target="tpu_custom_call", output_to_operand_aliasing={{}: (2, {})} | custom-call | tf_op jit(solution)/shard_map/ghosts/pallas_call | solution.py:364
  (84 shorter events, 8.5 us)
Async XLA Ops:
  0.0 6.7 %copy-start.20 = (s32[1,32]{1,0:T(1,128)S(1)}, s32[1,32]{1,0:T(1,128)}, u32[]{:S(2)}) copy-start(s32[1,32]{1,0:T(1,128)} %block_size.1) | copy-start | bytes 388
  0.0 6.7 %copy-start.19 = (s32[1,32,128]{2,1,0:T(8,128)S(1)}, s32[1,32,128]{2,1,0:T(8,128)}, u32[]{:S(2)}) copy-start(s32[1,32,128]{2,1,0:T(8,128)} %cells.1) | copy-start | bytes 49156
  3.3 21.2 %copy-start.28 = (s32[4,256]{1,0:T(4,128)S(1)}, s32[4,256]{1,0:T(4,128)}, u32[]{:S(2)}) copy-start(s32[4,256]{1,0:T(4,128)} %param.13) | copy-start | bytes 12292
  3.3 21.2 %copy-start.29 = (f32[4,256]{1,0:T(4,128)S(1)}, f32[4,256]{1,0:T(4,128)}, u32[]{:S(2)}) copy-start(f32[4,256]{1,0:T(4,128)} %param.14) | copy-start | bytes 12292
  3.3 36.6 %copy-start.3 = (f32[8,16,16]{2,1,0:T(8,128)S(1)}, f32[8,16,16]{2,1,0:T(8,128)}, u32[]{:S(2)}) copy-start(f32[8,16,16]{2,1,0:T(8,128)} %block_inverse.3) | copy-start | bytes 24580
  3.3 36.6 %copy-start.21 = (f32[7]{0:T(128)S(1)}, f32[7]{0:T(128)}, u32[]{:S(2)}) copy-start(f32[7]{0:T(128)} %lower.1) | copy-start | bytes 88
  3.3 36.6 %copy-start.22 = (f32[7]{0:T(128)S(1)}, f32[7]{0:T(128)}, u32[]{:S(2)}) copy-start(f32[7]{0:T(128)} %upper.1) | copy-start | bytes 88
  15.1 3.9 %copy-start.23 = (bf16[432,256]{1,0:T(8,128)(2,1)}, bf16[432,256]{1,0:T(8,128)(2,1)S(1)}, u32[]{:S(2)}) copy-start(bf16[432,256]{1,0:T(8,128)(2,1)S(1)} %get-tuple-element.34) | copy-start | bytes 663556
  15.1 21.2 %collective-permute-start.2 = (bf16[432,256]{1,0:T(8,128)(2,1)}, bf16[432,256]{1,0:T(8,128)(2,1)}, u32[]{:S(2)}, u32[]{:S(2)}) collective-permute-start(bf16[432,256]{1,0:T(8,128)(2,1)} %get-tuple-element.28), channel_id=1, source_target_pairs={{0,8},{8,16},{16,24},{24,0},{32,40},{40,48},{48,56},{56,32},{64,72... | collective-permute-start | bytes 663560 | tf_op jit(solution)/shard_map/ppermute | solution.py:290
  16.4 23.1 %collective-permute-start.3 = (bf16[432,256]{1,0:T(8,128)(2,1)}, bf16[432,256]{1,0:T(8,128)(2,1)}, u32[]{:S(2)}, u32[]{:S(2)}) collective-permute-start(bf16[432,256]{1,0:T(8,128)(2,1)} %get-tuple-element.29), channel_id=1, source_target_pairs={{0,16},{8,24},{16,0},{24,8},{32,48},{40,56},{48,32},{56,40},{64,80... | collective-permute-start | bytes 663560 | tf_op jit(solution)/shard_map/ppermute | solution.py:290
  19.0 24.7 %all-to-all-start = ((bf16[8,64,256]{2,1,0:T(8,128)(2,1)}), bf16[8,64,256]{2,1,0:T(8,128)(2,1)S(1)}, u32[]{:S(2)}, u32[]{:S(2)}) async-start(bf16[8,64,256]{2,1,0:T(8,128)(2,1)} %copy-done.9), calls=%async_computation | async-start | bytes 524288 | tf_op jit(solution)/shard_map/all_to_all | solution.py:313
  24.6 7.2 %collective-permute-start = (f32[8,256]{1,0:T(8,128)S(1)}, f32[8,256]{1,0:T(8,128)S(1)}, u32[]{:S(2)}, u32[]{:S(2)}) collective-permute-start(f32[8,256]{1,0:T(8,128)S(1)} %pad_maximum_fusion), channel_id=1, source_target_pairs={{224,0},{232,8},{240,16},{248,24},{160,32},{168,40},{176,48},{184,... | collective-permute-start | bytes 24584 | tf_op jit(solution)/shard_map/ppermute | solution.py:256
  30.7 5.6 %collective-permute-start.1 = (f32[8,256]{1,0:T(8,128)S(1)}, f32[8,256]{1,0:T(8,128)S(1)}, u32[]{:S(2)}, u32[]{:S(2)}) collective-permute-start(f32[8,256]{1,0:T(8,128)S(1)} %pad_maximum_fusion), channel_id=1, source_target_pairs={{192,0},{200,8},{208,16},{216,24},{128,32},{136,40},{144,48},{152,... | collective-permute-start | bytes 24584 | tf_op jit(solution)/shard_map/ppermute | solution.py:256
  30.7 23.4 %collective-permute-start.4 = (bf16[432,256]{1,0:T(8,128)(2,1)}, bf16[432,256]{1,0:T(8,128)(2,1)}, u32[]{:S(2)}, u32[]{:S(2)}) collective-permute-start(bf16[432,256]{1,0:T(8,128)(2,1)} %copy-done.27), channel_id=1, source_target_pairs={{0,24},{8,0},{16,8},{24,16},{32,56},{40,32},{48,40},{56,48},{64,88... | collective-permute-start | bytes 663560 | tf_op jit(solution)/shard_map/ppermute | solution.py:290
  31.7 22.3 %collective-permute-start.5 = (bf16[432,256]{1,0:T(8,128)(2,1)}, bf16[432,256]{1,0:T(8,128)(2,1)}, u32[]{:S(2)}, u32[]{:S(2)}) collective-permute-start(bf16[432,256]{1,0:T(8,128)(2,1)} %copy-done.26), channel_id=1, source_target_pairs={{0,32},{8,40},{16,48},{24,56},{32,0},{40,8},{48,16},{56,24},{64,96... | collective-permute-start | bytes 663560 | tf_op jit(solution)/shard_map/ppermute | solution.py:290
  36.3 17.8 %collective-permute-start.6 = (bf16[432,256]{1,0:T(8,128)(2,1)}, bf16[432,256]{1,0:T(8,128)(2,1)}, u32[]{:S(2)}, u32[]{:S(2)}) collective-permute-start(bf16[432,256]{1,0:T(8,128)(2,1)} %copy-done.25), channel_id=1, source_target_pairs={{0,40},{8,48},{16,56},{24,32},{32,8},{40,16},{48,24},{56,0},{64,10... | collective-permute-start | bytes 663560 | tf_op jit(solution)/shard_map/ppermute | solution.py:290
  36.3 17.8 %collective-permute-start.7 = (bf16[432,256]{1,0:T(8,128)(2,1)}, bf16[432,256]{1,0:T(8,128)(2,1)}, u32[]{:S(2)}, u32[]{:S(2)}) collective-permute-start(bf16[432,256]{1,0:T(8,128)(2,1)} %copy-done.24), channel_id=1, source_target_pairs={{0,48},{8,56},{16,32},{24,40},{32,16},{40,24},{48,0},{56,8},{64,11... | collective-permute-start | bytes 663560 | tf_op jit(solution)/shard_map/ppermute | solution.py:290
  39.4 14.6 %collective-permute-start.8 = (bf16[432,256]{1,0:T(8,128)(2,1)}, bf16[432,256]{1,0:T(8,128)(2,1)}, u32[]{:S(2)}, u32[]{:S(2)}) collective-permute-start(bf16[432,256]{1,0:T(8,128)(2,1)} %copy-done.23), channel_id=1, source_target_pairs={{0,56},{8,32},{16,40},{24,48},{32,24},{40,0},{48,8},{56,16},{64,12... | collective-permute-start | bytes 663560 | tf_op jit(solution)/shard_map/ppermute | solution.py:290
  45.6 44.9 %all-to-all-start.1 = ((bf16[8,64,256]{2,1,0:T(8,128)(2,1)}), bf16[8,64,256]{2,1,0:T(8,128)(2,1)S(1)}, u32[]{:S(2)}, u32[]{:S(2)}) async-start(bf16[8,64,256]{2,1,0:T(8,128)(2,1)} %copy-done.1), calls=%async_computation.1 | async-start | bytes 524288 | tf_op jit(solution)/shard_map/all_to_all | solution.py:322
  57.8 8.5 %collective-permute-start.9 = (bf16[224,256]{1,0:T(8,128)(2,1)S(1)}, bf16[224,256]{1,0:T(8,128)(2,1)S(1)}, u32[]{:S(2)}, u32[]{:S(2)}) collective-permute-start(bf16[224,256]{1,0:T(8,128)(2,1)S(1)} %get-tuple-element.35), channel_id=1, source_target_pairs={{0,224},{8,232},{16,240},{24,248},{32,160},{40,168},{48,176},{56,1... | collective-permute-start | bytes 344072 | tf_op jit(solution)/shard_map/ppermute | solution.py:348
  60.2 17.4 %collective-permute-start.10 = (bf16[224,256]{1,0:T(8,128)(2,1)S(1)}, bf16[224,256]{1,0:T(8,128)(2,1)S(1)}, u32[]{:S(2)}, u32[]{:S(2)}) collective-permute-start(bf16[224,256]{1,0:T(8,128)(2,1)S(1)} %get-tuple-element.36), channel_id=1, source_target_pairs={{0,192},{8,200},{16,208},{24,216},{32,128},{40,136},{48,144},{56,1... | collective-permute-start | bytes 344072 | tf_op jit(solution)/shard_map/ppermute | solution.py:348
  61.9 21.9 %collective-permute-start.11 = (bf16[272,256]{1,0:T(8,128)(2,1)S(1)}, bf16[272,256]{1,0:T(8,128)(2,1)S(1)}, u32[]{:S(2)}, u32[]{:S(2)}) collective-permute-start(bf16[272,256]{1,0:T(8,128)(2,1)S(1)} %get-tuple-element.37), channel_id=1, source_target_pairs={{0,224},{8,232},{16,240},{24,248},{32,160},{40,168},{48,176},{56,1... | collective-permute-start | bytes 417800 | tf_op jit(solution)/shard_map/ppermute | solution.py:349
  64.8 20.2 %collective-permute-start.12 = (bf16[272,256]{1,0:T(8,128)(2,1)S(1)}, bf16[272,256]{1,0:T(8,128)(2,1)S(1)}, u32[]{:S(2)}, u32[]{:S(2)}) collective-permute-start(bf16[272,256]{1,0:T(8,128)(2,1)S(1)} %get-tuple-element.38), channel_id=1, source_target_pairs={{0,192},{8,200},{16,208},{24,216},{32,128},{40,136},{48,144},{56,1... | collective-permute-start | bytes 417800 | tf_op jit(solution)/shard_map/ppermute | solution.py:349
  77.6 10.9 %copy-start.4 = (bf16[224,256]{1,0:T(8,128)(2,1)}, bf16[224,256]{1,0:T(8,128)(2,1)S(1)}, u32[]{:S(2)}) copy-start(bf16[224,256]{1,0:T(8,128)(2,1)S(1)} %collective-permute-done.10.second.refs_1_) | copy-start | bytes 344068
  77.7 10.3 %collective-permute-start.13 = (bf16[64,256]{1,0:T(8,128)(2,1)S(1)}, bf16[64,256]{1,0:T(8,128)(2,1)S(1)}, u32[]{:S(2)}, u32[]{:S(2)}) collective-permute-start(bf16[64,256]{1,0:T(8,128)(2,1)S(1)} %join.1.refs_4_), channel_id=1, source_target_pairs={{0,1},{1,2},{2,3},{3,4},{4,5},{5,6},{6,7},{7,0},{8,9},{9,10},{10,1... | collective-permute-start | bytes 98312 | tf_op jit(solution)/shard_map/ppermute | solution.py:360
  81.0 7.6 %collective-permute-start.14 = (bf16[64,256]{1,0:T(8,128)(2,1)S(1)}, bf16[64,256]{1,0:T(8,128)(2,1)S(1)}, u32[]{:S(2)}, u32[]{:S(2)}) collective-permute-start(bf16[64,256]{1,0:T(8,128)(2,1)S(1)} %join.1.refs_4_), channel_id=1, source_target_pairs={{0,2},{1,3},{2,4},{3,5},{4,6},{5,7},{6,0},{7,1},{8,10},{9,11},{10,... | collective-permute-start | bytes 98312 | tf_op jit(solution)/shard_map/ppermute | solution.py:360
  82.2 13.0 %collective-permute-start.15 = (bf16[64,256]{1,0:T(8,128)(2,1)S(1)}, bf16[64,256]{1,0:T(8,128)(2,1)}, u32[]{:S(2)}, u32[]{:S(2)}) collective-permute-start(bf16[64,256]{1,0:T(8,128)(2,1)S(1)} %join.1.refs_4_), channel_id=1, source_target_pairs={{0,3},{1,4},{2,5},{3,6},{4,7},{5,0},{6,1},{7,2},{8,11},{9,12},{10,... | collective-permute-start | bytes 98312 | tf_op jit(solution)/shard_map/ppermute | solution.py:360
  84.4 10.7 %collective-permute-start.16 = (bf16[64,256]{1,0:T(8,128)(2,1)S(1)}, bf16[64,256]{1,0:T(8,128)(2,1)}, u32[]{:S(2)}, u32[]{:S(2)}) collective-permute-start(bf16[64,256]{1,0:T(8,128)(2,1)S(1)} %join.1.refs_4_), channel_id=1, source_target_pairs={{0,4},{1,5},{2,6},{3,7},{4,0},{5,1},{6,2},{7,3},{8,12},{9,13},{10,... | collective-permute-start | bytes 98312 | tf_op jit(solution)/shard_map/ppermute | solution.py:360
  85.6 9.5 %collective-permute-start.17 = (bf16[64,256]{1,0:T(8,128)(2,1)S(1)}, bf16[64,256]{1,0:T(8,128)(2,1)}, u32[]{:S(2)}, u32[]{:S(2)}) collective-permute-start(bf16[64,256]{1,0:T(8,128)(2,1)S(1)} %join.1.refs_4_), channel_id=1, source_target_pairs={{0,5},{1,6},{2,7},{3,0},{4,1},{5,2},{6,3},{7,4},{8,13},{9,14},{10,... | collective-permute-start | bytes 98312 | tf_op jit(solution)/shard_map/ppermute | solution.py:360
  88.0 7.2 %collective-permute-start.18 = (bf16[64,256]{1,0:T(8,128)(2,1)S(1)}, bf16[64,256]{1,0:T(8,128)(2,1)}, u32[]{:S(2)}, u32[]{:S(2)}) collective-permute-start(bf16[64,256]{1,0:T(8,128)(2,1)S(1)} %join.1.refs_4_), channel_id=1, source_target_pairs={{0,6},{1,7},{2,0},{3,1},{4,2},{5,3},{6,4},{7,5},{8,14},{9,15},{10,... | collective-permute-start | bytes 98312 | tf_op jit(solution)/shard_map/ppermute | solution.py:360
  89.1 6.0 %collective-permute-start.19 = (bf16[64,256]{1,0:T(8,128)(2,1)S(1)}, bf16[64,256]{1,0:T(8,128)(2,1)}, u32[]{:S(2)}, u32[]{:S(2)}) collective-permute-start(bf16[64,256]{1,0:T(8,128)(2,1)S(1)} %join.1.refs_4_), channel_id=1, source_target_pairs={{0,7},{1,0},{2,1},{3,2},{4,3},{5,4},{6,5},{7,6},{8,15},{9,8},{10,9... | collective-permute-start | bytes 98312 | tf_op jit(solution)/shard_map/ppermute | solution.py:360
  91.4 3.8 %copy-start.18 = (bf16[64,256]{1,0:T(8,128)(2,1)S(1)}, bf16[64,256]{1,0:T(8,128)(2,1)}, u32[]{:S(2)}) copy-start(bf16[64,256]{1,0:T(8,128)(2,1)} %copy-done.17) | copy-start | bytes 98308
  (20 other events, 28.4 us)

commit v3 on v1

v3 whole, which is shorter than its diff:
```python
import jax
import jax.numpy as jnp
from jax import lax
from jax.experimental import pallas as pl
from jax.experimental.pallas import tpu as pltpu
from jax.sharding import PartitionSpec as P

f32 = jnp.float32
bf16 = jnp.bfloat16
highest = lax.Precision.HIGHEST
induction = 0.5

CHANNELS = 27
DEPTH = 16
ROWS = CHANNELS * DEPTH
CELLS = 2048
RIM = 256
INNER = CELLS - RIM
CAP = 128
TILES = 32
BLOCKS = 8
PARTS = 3
PART_ROWS = ROWS // PARTS
EDGE = 64
GROUP = 8

SERVES = ((3, 1, 2, 0), (2, 0, 3, 1))


def params(mebibytes):
    return pltpu.CompilerParams(vmem_limit_bytes=mebibytes * 1024 * 1024)


def iota(shape, axis):
    return lax.broadcasted_iota(jnp.int32, shape, axis)


def split(value):
    high = value.astype(bf16)
    return high, (value - high.astype(f32)).astype(bf16)


def dot(left, right):
    return jnp.dot(left, right, preferred_element_type=f32)


def edge_select(rows, channels, first):
    row, column = iota((EDGE, rows), 0), iota((EDGE, rows), 1)
    channel = row % 32 - first
    wanted = channel * DEPTH + (row // 32) * (DEPTH - 1)
    return ((channel >= 0) & (channel < channels) & (column == wanted)).astype(f32).astype(bf16)


def head_kernel(place, block_size, cells_hbm, field_hbm, velocity_hbm, inverse_hbm, *refs):
    spread_hbm, lists_hbm, chunks = refs[0], refs[1], refs[2 : 2 + BLOCKS]
    cells, field, velocity, own, spread, rounded, lists, edges, done, sent = refs[2 + BLOCKS :]
    copies = [
        pltpu.make_async_copy(inverse_hbm.at[place[1]], own, done.at[0]),
        pltpu.make_async_copy(velocity_hbm, velocity, done.at[1]),
    ]
    for part in range(PARTS):
        rows = pl.ds(part * PART_ROWS, PART_ROWS)
        copies.append(pltpu.make_async_copy(field_hbm.at[rows], field.at[rows], done.at[2 + part]))
    copies.append(pltpu.make_async_copy(cells_hbm, cells, done.at[2 + PARTS]))
    for copy in copies:
        copy.start()
    sends = []

    size = PART_ROWS
    rows = (iota((size, DEPTH), 0) % DEPTH == iota((size, DEPTH), 1)).astype(f32)
    columns = (iota((DEPTH, size), 1) % DEPTH == iota((DEPTH, size), 0)).astype(f32)
    same = iota((size, size), 0) // DEPTH == iota((size, size), 1) // DEPTH
    copies[0].wait()
    tiled = jnp.dot(jnp.dot(rows, own[...], precision=highest), columns, precision=highest)
    high_mat, low_mat = split(jnp.where(same, tiled, 0.0))

    copies[1].wait()
    flow = [velocity[DEPTH * i : DEPTH * (i + 1), :INNER].astype(f32) for i in range(3)]
    for part in range(PARTS):
        copies[2 + part].wait()
        sources = []
        for m in range(PART_ROWS // (3 * DEPTH)):
            first = part * PART_ROWS + 3 * m * DEPTH
            f = [
                field[first + DEPTH * i : first + DEPTH * (i + 1), :INNER].astype(f32)
                for i in range(3)
            ]
            for i in range(3):
                j, k = (i + 1) % 3, (i + 2) % 3
                sources.append(f[i] + induction * (flow[j] * f[k] - flow[k] * f[j]))
        source_high, source_low = split(jnp.concatenate(sources, axis=0))
        result = dot(high_mat, source_high) + dot(high_mat, source_low)
        result = result + dot(low_mat, source_high)
        here = slice(part * PART_ROWS, (part + 1) * PART_ROWS)
        spread[here, :] = result
        rounded[here, :] = result.astype(bf16)
        rows = pl.ds(part * PART_ROWS, PART_ROWS)
        sends.append(pltpu.make_async_copy(spread.at[rows], spread_hbm.at[rows], sent.at[part]))
        sends[-1].start()
    edges[:, :INNER] = dot(edge_select(ROWS, CHANNELS, 0), rounded[...]).astype(bf16)
    edges[:, INNER:] = jnp.zeros((EDGE, RIM), bf16)
    for shift in range(BLOCKS):
        first = pl.multiple_of((place[1] + shift) % BLOCKS * 256, 256)
        chunks[shift][...] = edges[:, pl.ds(first, 256)]
    copies[2 + PARTS].wait()

    row = place[0] // 4
    panel, half = row // 4, (row // 2) % 2
    for r in range(GROUP):
        member, y = r // 4, r % 4
        served = (3 - 2 * member - half, 2 - 2 * member + half)
        wanted = []
        for m in range(2):
            tile = (4 * (1 - panel) + served[m]) * 4 + y
            listed = cells[0, pl.ds(tile, 1), :]
            wanted.append(jnp.where(iota((1, CAP), 1) < block_size[0, tile], listed, -1))
        wanted = jnp.concatenate(wanted, axis=1)
        total = jnp.zeros((ROWS, 2 * CAP), f32)
        for first in range(0, INNER, 256):
            hot = (iota((256, 2 * CAP), 0) + first == wanted).astype(f32).astype(bf16)
            total = total + dot(rounded[:, first : first + 256], hot)
        lists[r] = total.astype(bf16)
        sends.append(pltpu.make_async_copy(lists.at[r], lists_hbm.at[r], sent.at[PARTS + r]))
        sends[-1].start()
    for copy in sends:
        copy.wait()


def weight_kernel(place, first, second, weights):
    base = place[0] // GROUP * GROUP
    for m, meta in enumerate((first, second)):
        slots = meta[0:4, :].astype(jnp.int32)
        for r in range(GROUP):
            position = iota((CAP, RIM), 0) + (base + r) * CAP
            value = jnp.zeros((CAP, RIM), f32)
            for d in range(4):
                value = value + jnp.where(slots[d : d + 1, :] == position, meta[4 + d : 5 + d, :], 0.0)
            high, low = split(value)
            weights[m, r * CAP : (r + 1) * CAP, :RIM] = high
            weights[m, r * CAP : (r + 1) * CAP, RIM:] = low


def setup_kernel(place, lower, upper, corner, block_inverse, needed, spikes):
    size = 2 * BLOCKS
    shape = (size, 128)
    row, lane = iota(shape, 0), iota(shape, 1)
    work = ((row == lane) | (row + size == lane)).astype(f32)
    for k in range(BLOCKS):
        for b in range(2):
            i = b * (DEPTH - 1)
            here = row == 2 * k + b
            if k < BLOCKS - 1:
                value = corner[k, i, DEPTH - 1] * upper[k]
                work = jnp.where(here & (lane == 2 * k + 2), value, work)
            if k > 0:
                value = corner[k, i, 0] * lower[k - 1]
                work = jnp.where(here & (lane == 2 * k - 1), value, work)
    for p in range(size):
        column = jnp.sum(jnp.where(lane == p, work, 0.0), axis=1, keepdims=True)
        chosen = work[p : p + 1, :] / column[p : p + 1, :]
        work = jnp.where(row == p, chosen, work - column * chosen)
    up = jnp.concatenate([work[2:, :], jnp.zeros((2, 128), f32)], axis=0)
    down = jnp.concatenate([jnp.zeros((2, 128), f32), work[:-2, :]], axis=0)
    needed[...] = jnp.where(row % 2 == 0, up, down)

    k = place[1]
    ahead = jnp.where(k < BLOCKS - 1, upper[jnp.minimum(k, BLOCKS - 2)], 0.0)
    behind = jnp.where(k > 0, lower[jnp.maximum(k - 1, 0)], 0.0)
    rows = (iota((ROWS, DEPTH), 0) % DEPTH == iota((ROWS, DEPTH), 1)).astype(f32)
    tiled = jnp.dot(rows, block_inverse[k], precision=highest)
    right, left = tiled[:, DEPTH - 1 :] * ahead, tiled[:, :1] * behind
    channel, lane = iota((ROWS, 128), 0) // DEPTH, iota((ROWS, 128), 1)
    full = jnp.where(lane % 64 == channel, right, 0.0)
    full = full + jnp.where(lane % 64 == channel + 32, left, 0.0)
    high, low = split(full)
    spikes[...] = jnp.where(lane < 64, high.astype(f32), low.astype(f32)).astype(bf16)


def partial_kernel(weights, lists, coupled, *outs):
    del coupled
    for m in range(2):
        values = [lists[r, :, m * CAP : (m + 1) * CAP] for r in range(GROUP)]
        both = dot(jnp.concatenate(values, axis=1), weights[m])
        result = (both[:, :RIM] + both[:, RIM:]).astype(bf16)
        outs[m][...] = dot(edge_select(ROWS, CHANNELS, 0), result).astype(bf16)
        outs[2 + m][...] = result


def solve_kernel(place, needed, *refs):
    chunks, coupled = refs[:BLOCKS], refs[BLOCKS]
    values = [chunks[shift][...].astype(f32) for shift in range(BLOCKS)]
    for k in range(BLOCKS):
        for p in range(2):
            total = jnp.zeros((32, 256), f32)
            for shift in range(BLOCKS):
                block = (place[1] + BLOCKS - shift) % BLOCKS
                for b in range(2):
                    factor = needed[2 * k + p, 2 * BLOCKS + 2 * block + b]
                    total = total + factor * values[shift][32 * b : 32 * b + 32, :]
            coupled[k, 32 * p : 32 * p + 32, :] = total.astype(bf16)


def join_kernel(first, second, coupled, moved, edges):
    del moved
    both = (first[...].astype(f32) + second[...].astype(f32)).astype(bf16)
    for k in range(BLOCKS):
        edges[k, :EDGE, :] = coupled[k]
        edges[k, EDGE:, :] = both


def finish_kernel(place, needed, spread, first, second, coupled, spikes, result):
    step = pl.program_id(0)

    @pl.when(step < INNER // 256)
    def _():
        mine = coupled[step, :EDGE, :]
        correction = dot(spikes[...], jnp.concatenate([mine, mine], axis=0))
        result[...] = (spread[...] - correction).astype(bf16)

    @pl.when(step == INNER // 256)
    def _():
        own = place[1]
        halves = []
        for p in range(2):
            total = jnp.zeros((32, RIM), f32)
            for k in range(BLOCKS):
                for b in range(2):
                    factor = needed[2 * own + p, 2 * BLOCKS + 2 * k + b]
                    edge = coupled[k, EDGE + 32 * b : EDGE + 32 * b + 32, :]
                    total = total + factor * edge.astype(f32)
            halves.append(total)
        mine = jnp.concatenate(halves, axis=0).astype(bf16)
        correction = dot(spikes[...], jnp.concatenate([mine, mine], axis=0))
        ghost = first[...].astype(f32) + second[...].astype(f32)
        result[...] = (ghost - correction).astype(bf16)


SMEM = pl.BlockSpec(memory_space=pltpu.SMEM)
VMEM = pl.BlockSpec(memory_space=pltpu.VMEM)
ANY = pl.BlockSpec(memory_space=pl.ANY)


def whole(shape):
    return pl.BlockSpec(shape, lambda i: (0,) * len(shape))


def crossing(m, backwards):
    pairs = []
    for z in range(8):
        panel, i = divmod(z, 4)
        target = 4 * (1 - panel) + SERVES[m][i]
        for y in range(4):
            pair = (z * 4 + y, target * 4 + y)
            pairs.append(pair[::-1] if backwards else pair)
    return pairs


def shards(
    field,
    velocity,
    send_cells,
    block_size,
    donor_slot,
    intersection_weight,
    block_inverse,
    lower_coupling,
    upper_coupling,
):
    field = field.reshape(ROWS, CELLS)
    velocity = velocity.reshape(3 * DEPTH, CELLS)
    place = jnp.stack([lax.axis_index("ang"), lax.axis_index("rad")]).astype(jnp.int32)

    meta = jnp.concatenate([donor_slot.astype(f32), intersection_weight], axis=0)
    metas = [lax.ppermute(meta, "ang", crossing(m, True)) for m in range(2)]

    groups = [list(range(g * GROUP, (g + 1) * GROUP)) for g in range(TILES // GROUP)]
    spread, lists, *chunks = pl.pallas_call(
        head_kernel,
        in_specs=[SMEM, SMEM] + [ANY] * 4,
        out_specs=[ANY] * 2 + [VMEM] * BLOCKS,
        out_shape=[
            jax.ShapeDtypeStruct((ROWS, INNER), f32),
            jax.ShapeDtypeStruct((GROUP, ROWS, 2 * CAP), bf16),
        ]
        + [jax.ShapeDtypeStruct((EDGE, 256), bf16)] * BLOCKS,
        scratch_shapes=[
            pltpu.VMEM((1, TILES, CAP), jnp.int32),
            pltpu.VMEM((ROWS, CELLS), bf16),
            pltpu.VMEM((3 * DEPTH, CELLS), bf16),
            pltpu.VMEM((DEPTH, DEPTH), f32),
            pltpu.VMEM((ROWS, INNER), f32),
            pltpu.VMEM((ROWS, INNER), bf16),
            pltpu.VMEM((GROUP, ROWS, 2 * CAP), bf16),
            pltpu.VMEM((EDGE, CELLS), bf16),
            pltpu.SemaphoreType.DMA((3 + PARTS,)),
            pltpu.SemaphoreType.DMA((PARTS + GROUP,)),
        ],
        compiler_params=params(60),
        name="head",
    )(place, block_size, send_cells, field, velocity, block_inverse)

    donors = lax.all_to_all(lists, "ang", 0, 0, axis_index_groups=groups)
    chunks = chunks[:1] + [
        lax.ppermute(chunks[shift], "rad", [(k, (k + shift) % BLOCKS) for k in range(BLOCKS)])
        for shift in range(1, BLOCKS)
    ]

    weights = pl.pallas_call(
        weight_kernel,
        in_specs=[SMEM, VMEM, VMEM],
        out_specs=VMEM,
        out_shape=jax.ShapeDtypeStruct((2, GROUP * CAP, 2 * RIM), bf16),
        compiler_params=params(8),
        name="weights",
    )(place, *metas)

    needed, spikes = pl.pallas_call(
        setup_kernel,
        in_specs=[SMEM, SMEM, SMEM, SMEM, VMEM],
        out_specs=[VMEM] * 2,
        out_shape=[
            jax.ShapeDtypeStruct((2 * BLOCKS, 128), f32),
            jax.ShapeDtypeStruct((ROWS, 128), bf16),
        ],
        compiler_params=params(4),
        name="setup",
    )(place, lower_coupling, upper_coupling, block_inverse, block_inverse)

    coupled = pl.pallas_call(
        solve_kernel,
        in_specs=[SMEM] * 2 + [VMEM] * BLOCKS,
        out_specs=VMEM,
        out_shape=jax.ShapeDtypeStruct((BLOCKS, EDGE, 256), bf16),
        compiler_params=params(4),
        name="solve",
    )(place, needed, *chunks)

    *first_edges, first, second = pl.pallas_call(
        partial_kernel,
        in_specs=[VMEM] * 2 + [ANY],
        out_specs=[VMEM] * 4,
        out_shape=[jax.ShapeDtypeStruct((EDGE, RIM), bf16)] * 2
        + [jax.ShapeDtypeStruct((ROWS, RIM), bf16)] * 2,
        compiler_params=params(14),
        name="partial",
    )(weights, donors, coupled)

    first_edges = [lax.ppermute(first_edges[m], "ang", crossing(m, False)) for m in range(2)]
    ghosts = [lax.ppermute(value, "ang", crossing(m, False)) for m, value in enumerate((first, second))]

    joined = pl.pallas_call(
        join_kernel,
        in_specs=[VMEM] * 3 + [ANY],
        out_specs=VMEM,
        out_shape=jax.ShapeDtypeStruct((BLOCKS, 2 * EDGE, RIM), bf16),
        compiler_params=params(4),
        name="join",
    )(*first_edges, coupled, ghosts[0])
    joined = lax.all_to_all(joined, "rad", 0, 0)

    result = pl.pallas_call(
        finish_kernel,
        grid=(CELLS // 256,),
        in_specs=[
            SMEM,
            SMEM,
            pl.BlockSpec((ROWS, 256), lambda i: (0, jnp.minimum(i, INNER // 256 - 1))),
            whole((ROWS, RIM)),
            whole((ROWS, RIM)),
            whole((BLOCKS, 2 * EDGE, 256)),
            whole((ROWS, 128)),
        ],
        out_specs=pl.BlockSpec((ROWS, 256), lambda i: (0, i)),
        out_shape=jax.ShapeDtypeStruct((ROWS, CELLS), bf16),
        compiler_params=params(61),
        name="finish",
    )(place, needed, spread, *ghosts, joined, spikes)
    return result.reshape(CHANNELS, DEPTH, CELLS)


def solution(mesh):
    in_specs = (
        P(None, "rad", "ang"),
        P(None, "rad", "ang"),
        P("ang", None, None),
        P("ang", None),
        P(None, "ang"),
        P(None, "ang"),
        P(),
        P(),
        P(),
    )
    out_specs = P(None, "rad", "ang")
    return jax.shard_map(shards, mesh=mesh, in_specs=in_specs, out_specs=out_specs, check_vma=False)
```

time: 107 us -> 99.3 us (0.928)
  waiting for transfers between devices: 45 us -> 32.3 us
  starting transfers between devices: 29.9 us -> 36.1 us
  local copies, waits for them, and re-layouts: 5.15 us -> 1.6 us
  Pallas kernels: 26.1 us -> 27.2 us
    ppermute x4 -> x11, starting transfers between devices: 6.66 us -> 19.7 us  [the longest x7 12.1 us: shards(): lax.ppermute(chunks[shift], 'rad', [(k, (k + shift) % BLOCKS) for k in ra...]
    all_to_all x2 -> x1, starting transfers between devices: 11.6 us -> 4.78 us  [shards(): joined = lax.all_to_all(joined, 'rad', 0, 0)]
    ppermute x2, waiting for transfers between devices: 18.8 us -> 13.4 us  [shards(): metas = [lax.ppermute(meta, 'ang', crossing(m, True)) for m in range(2)]]
    ppermute x4 -> x11, waiting for transfers between devices: 22.8 us -> 18.9 us  [the longest x2 11.5 us: shards(): lax.ppermute(value, 'ang', crossing(m, False))]
    unnamed x22 -> x38, local copies, waits for them, and re-layouts: 5.15 us -> 1.6 us
    all_to_all x2 -> x1, waiting for transfers between devices: 3.43 us -> 0.01 us  [shards(): joined = lax.all_to_all(joined, 'rad', 0, 0)]
    pallas_call x8 -> x7, Pallas kernels: 26.1 us -> 27.2 us  [the longest x1 10 us: shards(): pl.pallas_call(head_kernel, in_specs=[SMEM, SMEM] + [ANY] * 4, out_specs=...]
  transfers between devices with their start and end apart: 9 -> 15, of which waited for: 5 -> 4; matrix products, arithmetic and copies ran while one was open for 0% -> 0% of each run, Pallas kernels for 4% -> 6%
where the time goes in v3:
time: 99.3 us; the launch traced here: 98.1 us
  starting transfers between devices  36.1 us (36%)
  waiting for transfers between devices  32.3 us (33%)
  Pallas kernels  27.2 us (27%)
  local copies, waits for them, and re-layouts  1.6 us (2%)
    ppermute x2, waiting for transfers between devices, shards(): metas = [lax.ppermute(meta, 'ang', crossing(m, True)) for m in range(2)]  13.4 us
    ppermute x7, starting transfers between devices, shards(): lax.ppermute(chunks[shift], 'rad', [(k, (k + shift) % BLOCKS) for k in ra...  12.1 us
    ppermute x2, waiting for transfers between devices, shards(): lax.ppermute(value, 'ang', crossing(m, False))  11.5 us
    pallas_call x1, Pallas kernels, shards(): pl.pallas_call(head_kernel, in_specs=[SMEM, SMEM] + [ANY] * 4, out_specs=...  10 us
    ppermute x2, waiting for transfers between devices, shards(): lax.ppermute(first_edges[m], 'ang', crossing(m, False))  7.35 us
    pallas_call x1, Pallas kernels, shards(): pl.pallas_call(finish_kernel, grid=(CELLS // 256,), in_specs=[SMEM, SMEM,...  6.68 us
    ppermute x2, starting transfers between devices, shards(): metas = [lax.ppermute(meta, 'ang', crossing(m, True)) for m in range(2)]  6.1 us
    all_to_all x1, starting transfers between devices, shards(): donors = lax.all_to_all(lists, 'ang', 0, 0, axis_index_groups=groups)  5.52 us
  transfers between devices with their start and end apart: 15, of which 4 were waited for; matrix products, arithmetic and copies ran while one was open for 0% of the time, Pallas kernels for 6%

profile of v3, /device:TPU:33, one launch (start us, length us, event | category | flops | bytes accessed | tf_op | source)
XLA Modules:
  0.0 98.1 jit_solution(13901994060986374953)
XLA Ops:
  0.0 0.6 pad_add_fusion.place
  0.6 10.0 %head.1 = (f32[432,1792]{1,0:T(8,128)}, bf16[8,432,256]{2,1,0:T(8,128)(2,1)}, bf16[64,256]{1,0:T(8,128)(2,1)}, bf16[64,256]{1,0:T(8,128)(2,1)}, bf16[64,256]{1,0...) custom-call(s32[2]{0:T(128)} %pad_add_fusion.place, ...), custom_call_target="tpu_custom_call" | custom-call | tf_op jit(solution)/shard_map/head/pallas_call | solution.py:277
  10.6 0.0 copy-start.10
  10.6 0.0 copy-start.11
  10.7 0.0 copy-start.1
  10.7 0.0 copy-start.6
  10.7 0.0 copy-start.7
  10.7 5.5 %all-to-all-start = ((bf16[8,432,256]{2,1,0:T(8,128)(2,1)}), bf16[8,432,256]{2,1,0:T(8,128)(2,1)}, u32[]{:S(2)}, u32[]{:S(2)}) async-start(bf16[8,432,256]{2,1,0:T(8,128)(2,1)} %get-tuple-element.23), calls=%async_computation | async-start | bytes 3538944 | tf_op jit(solution)/shard_map/all_to_all | solution.py:302
  16.3 2.3 %collective-permute-start.2 = (bf16[64,256]{1,0:T(8,128)(2,1)S(1)}, bf16[64,256]{1,0:T(8,128)(2,1)S(1)}, u32[]{:S(2)}, u32[]{:S(2)}) collective-permute-start(bf16[64,256]{1,0:T(8,128)(2,1)S(1)} %copy-done.18), channel_id=1, source_target_pairs={{0,1},{1,2},{2,3},{3,4},{4,5},{5,6},{6,7},{7,0},{8,9},{9,10},{10,1... | collective-permute-start | bytes 98312 | tf_op jit(solution)/shard_map/ppermute | solution.py:304
  18.6 1.2 %collective-permute-start.3 = (bf16[64,256]{1,0:T(8,128)(2,1)S(1)}, bf16[64,256]{1,0:T(8,128)(2,1)S(1)}, u32[]{:S(2)}, u32[]{:S(2)}) collective-permute-start(bf16[64,256]{1,0:T(8,128)(2,1)S(1)} %copy-done.17), channel_id=1, source_target_pairs={{0,2},{1,3},{2,4},{3,5},{4,6},{5,7},{6,0},{7,1},{8,10},{9,11},{10,... | collective-permute-start | bytes 98312 | tf_op jit(solution)/shard_map/ppermute | solution.py:304
  19.8 6.1 %collective-permute-start = (f32[8,256]{1,0:T(8,128)S(1)}, f32[8,256]{1,0:T(8,128)S(1)}, u32[]{:S(2)}, u32[]{:S(2)}) collective-permute-start(f32[8,256]{1,0:T(8,128)S(1)} %pad_maximum_fusion), channel_id=1, source_target_pairs={{224,0},{232,8},{240,16},{248,24},{160,32},{168,40},{176,48},{184,... | collective-permute-start | bytes 24584 | tf_op jit(solution)/shard_map/ppermute | solution.py:274
  25.9 1.9 %collective-permute-start.4 = (bf16[64,256]{1,0:T(8,128)(2,1)S(1)}, bf16[64,256]{1,0:T(8,128)(2,1)S(1)}, u32[]{:S(2)}, u32[]{:S(2)}) collective-permute-start(bf16[64,256]{1,0:T(8,128)(2,1)S(1)} %copy-done.16), channel_id=1, source_target_pairs={{0,3},{1,4},{2,5},{3,6},{4,7},{5,0},{6,1},{7,2},{8,11},{9,12},{10,... | collective-permute-start | bytes 98312 | tf_op jit(solution)/shard_map/ppermute | solution.py:304
  27.8 13.4 %collective-permute-done.first = f32[8,256]{1,0:T(8,128)S(1)} collective-permute-done((f32[8,256]{1,0:T(8,128)S(1)}, f32[8,256]{1,0:T(8,128)S(1)}, u32[]{:S(2)}, u32[]{:S(2)}) %collective-permute-start) | collective-permute-done | bytes 8224 | tf_op jit(solution)/shard_map/ppermute | solution.py:274
  41.2 2.8 %collective-permute-start.5 = (bf16[64,256]{1,0:T(8,128)(2,1)S(1)}, bf16[64,256]{1,0:T(8,128)(2,1)S(1)}, u32[]{:S(2)}, u32[]{:S(2)}) collective-permute-start(bf16[64,256]{1,0:T(8,128)(2,1)S(1)} %copy-done.15), channel_id=1, source_target_pairs={{0,4},{1,5},{2,6},{3,7},{4,0},{5,1},{6,2},{7,3},{8,12},{9,13},{10,... | collective-permute-start | bytes 98312 | tf_op jit(solution)/shard_map/ppermute | solution.py:304
  44.0 3.2 %collective-permute-start.6 = (bf16[64,256]{1,0:T(8,128)(2,1)S(1)}, bf16[64,256]{1,0:T(8,128)(2,1)S(1)}, u32[]{:S(2)}, u32[]{:S(2)}) collective-permute-start(bf16[64,256]{1,0:T(8,128)(2,1)S(1)} %copy-done.14), channel_id=1, source_target_pairs={{0,5},{1,6},{2,7},{3,0},{4,1},{5,2},{6,3},{7,4},{8,13},{9,14},{10,... | collective-permute-start | bytes 98312 | tf_op jit(solution)/shard_map/ppermute | solution.py:304
  47.2 0.6 collective-permute-start.8
  47.9 3.0 %setup.1 = (f32[16,128]{1,0:T(8,128)S(1)}, bf16[432,128]{1,0:T(8,128)(2,1)S(1)}) custom-call(s32[2]{0:T(128)S(1)} %copy-done.5, f32[7]{0:T(128)S(1)} %copy-done.6, f32[7]{0:T(128)S(1)} %copy-done.7, f32[8,16,16]{2,1,0:T(8,128)S(1)} %copy-done.1, f32[8,16,16]{2,1,0:T(8,128)S(1)} %copy-done.1), custom_call_target="tpu_custom_call" | custom-call | tf_op jit(solution)/shard_map/setup/pallas_call | solution.py:317
  51.0 0.7 copy-done.2
  51.6 1.6 %weights.1 = bf16[2,1024,512]{2,1,0:T(8,128)(2,1)S(1)} custom-call(s32[2]{0:T(128)S(1)} %copy-done.5, f32[8,256]{1,0:T(8,128)S(1)} %collective-permute-done.first, f32[8,256]{1,0:T(8,128)S(1)} %collective-permute-done.1.second), custom_call_target="tpu_custom_call" | custom-call | tf_op jit(solution)/shard_map/weights/pallas_call | solution.py:308
  53.3 1.3 %solve.1.coupled = bf16[8,64,256]{2,1,0:T(8,128)(2,1)S(1)} custom-call(s32[2]{0:T(128)S(1)} %copy-done.5, f32[16,128]{1,0:T(8,128)S(1)} %get-tuple-element.21.needed, bf16[64,256]{1,0:T(8,128)(2,1)S(1)} %copy-done.4, bf16[64,256]{1,0:T(8,128)(2,1)S(1)} %collective-permute-done.2.refs_1_, bf16[64,256]{1,0:T(8,128)(2,1)S(1)} %collective-permute-done.3.refs_2_, ...), custom_call_target="tpu_custom_call" | custom-call | tf_op jit(solution)/shard_map/solve/pallas_call | solution.py:329
  54.6 3.7 %partial.1 = (bf16[64,256]{1,0:T(8,128)(2,1)S(1)}, bf16[64,256]{1,0:T(8,128)(2,1)S(1)}, bf16[432,256]{1,0:T(8,128)(2,1)S(1)}, bf16[432,256]{1,0:T(8,128)(2,1)S(1)}) custom-call(bf16[2,1024,512]{2,1,0:T(8,128)(2,1)S(1)} %weights.1, bf16[8,432,256]{2,1,0:T(8,128)(2,1)} %all-to-all-done.lists, bf16[8,64,256]{2,1,0:T(8,128)(2,1)S(1)} %solve.1.coupled), custom_call_target="tpu_custom_call" | custom-call | tf_op jit(solution)/shard_map/partial/pallas_call | solution.py:338
  58.4 0.1 collective-permute-start.9
  58.5 5.4 %collective-permute-start.11 = (bf16[64,256]{1,0:T(8,128)(2,1)S(1)}, bf16[64,256]{1,0:T(8,128)(2,1)S(1)}, u32[]{:S(2)}, u32[]{:S(2)}) collective-permute-start(bf16[64,256]{1,0:T(8,128)(2,1)S(1)} %get-tuple-element.34), channel_id=1, source_target_pairs={{0,224},{8,232},{16,240},{24,248},{32,160},{40,168},{48,176},{56,1... | collective-permute-start | bytes 98312 | tf_op jit(solution)/shard_map/ppermute | solution.py:348
  63.8 5.2 %collective-permute-done.11.first = bf16[64,256]{1,0:T(8,128)(2,1)S(1)} collective-permute-done((bf16[64,256]{1,0:T(8,128)(2,1)S(1)}, bf16[64,256]{1,0:T(8,128)(2,1)S(1)}, u32[]{:S(2)}, u32[]{:S(2)}) %collective-permute-start.11) | collective-permute-done | bytes 32800 | tf_op jit(solution)/shard_map/ppermute | solution.py:348
  69.0 2.2 %collective-permute-done.12.second = bf16[64,256]{1,0:T(8,128)(2,1)S(1)} collective-permute-done((bf16[64,256]{1,0:T(8,128)(2,1)S(1)}, bf16[64,256]{1,0:T(8,128)(2,1)S(1)}, u32[]{:S(2)}, u32[]{:S(2)}) %collective-permute-start.12) | collective-permute-done | bytes 32800 | tf_op jit(solution)/shard_map/ppermute | solution.py:348
  71.2 0.9 join.1
  72.0 4.8 %all-to-all-start.1 = ((bf16[8,128,256]{2,1,0:T(8,128)(2,1)}), bf16[8,128,256]{2,1,0:T(8,128)(2,1)S(1)}, u32[]{:S(2)}, u32[]{:S(2)}) async-start(bf16[8,128,256]{2,1,0:T(8,128)(2,1)} %join.1), calls=%async_computation.1 | async-start | bytes 1048576 | tf_op jit(solution)/shard_map/all_to_all | solution.py:359
  76.8 2.2 %collective-permute-start.10 = (bf16[432,256]{1,0:T(8,128)(2,1)S(1)}, bf16[432,256]{1,0:T(8,128)(2,1)S(1)}, u32[]{:S(2)}, u32[]{:S(2)}) collective-permute-start(bf16[432,256]{1,0:T(8,128)(2,1)S(1)} %get-tuple-element.33), channel_id=1, source_target_pairs={{0,192},{8,200},{16,208},{24,216},{32,128},{40,136},{48,144},{56,1... | collective-permute-start | bytes 663560 | tf_op jit(solution)/shard_map/ppermute | solution.py:349
  79.0 11.5 %collective-permute-done.10.second = bf16[432,256]{1,0:T(8,128)(2,1)S(1)} collective-permute-done((bf16[432,256]{1,0:T(8,128)(2,1)S(1)}, bf16[432,256]{1,0:T(8,128)(2,1)S(1)}, u32[]{:S(2)}, u32[]{:S(2)}) %collective-permute-start.10) | collective-permute-done | bytes 221216 | tf_op jit(solution)/shard_map/ppermute | solution.py:349
  90.6 0.7 copy-done.9
  91.2 0.2 copy-done.8
  91.4 6.7 %finish.1 = bf16[432,2048]{1,0:T(8,128)(2,1)} custom-call(s32[2]{0:T(128)} %pad_add_fusion.place, f32[16,128]{1,0:T(8,128)} %copy-done.3, f32[432,1792]{1,0:T(8,128)} %get-tuple-element.22.spread, bf16[432,256]{1,0:T(8,128)(2,1)} %copy-done, bf16[432,256]{1,0:T(8,128)(2,1)} %copy-done.9, bf16[8,128,256]{2,1,0:T(8,128)(2,1)} %copy-done.8, ...), custom_call_target="tpu_custom_call" | custom-call | tf_op jit(solution)/shard_map/finish/pallas_call | solution.py:361
  (46 shorter events, 0.1 us)
Async XLA Ops:
  10.6 5.7 %copy-start.18 = (bf16[64,256]{1,0:T(8,128)(2,1)S(1)}, bf16[64,256]{1,0:T(8,128)(2,1)}, u32[]{:S(2)}) copy-start(bf16[64,256]{1,0:T(8,128)(2,1)} %get-tuple-element.25) | copy-start | bytes 98308
  10.6 8.0 %copy-start.17 = (bf16[64,256]{1,0:T(8,128)(2,1)S(1)}, bf16[64,256]{1,0:T(8,128)(2,1)}, u32[]{:S(2)}) copy-start(bf16[64,256]{1,0:T(8,128)(2,1)} %get-tuple-element.26) | copy-start | bytes 98308
  10.6 9.2 %copy-start.10 = (s32[4,256]{1,0:T(4,128)S(1)}, s32[4,256]{1,0:T(4,128)}, u32[]{:S(2)}) copy-start(s32[4,256]{1,0:T(4,128)} %param.13) | copy-start | bytes 12292
  10.6 9.2 %copy-start.11 = (f32[4,256]{1,0:T(4,128)S(1)}, f32[4,256]{1,0:T(4,128)}, u32[]{:S(2)}) copy-start(f32[4,256]{1,0:T(4,128)} %param.14) | copy-start | bytes 12292
  10.6 15.3 %copy-start.16 = (bf16[64,256]{1,0:T(8,128)(2,1)S(1)}, bf16[64,256]{1,0:T(8,128)(2,1)}, u32[]{:S(2)}) copy-start(bf16[64,256]{1,0:T(8,128)(2,1)} %get-tuple-element.27) | copy-start | bytes 98308
  10.6 30.5 %copy-start.15 = (bf16[64,256]{1,0:T(8,128)(2,1)S(1)}, bf16[64,256]{1,0:T(8,128)(2,1)}, u32[]{:S(2)}) copy-start(bf16[64,256]{1,0:T(8,128)(2,1)} %get-tuple-element.28) | copy-start | bytes 98308
  10.7 33.3 %copy-start.14 = (bf16[64,256]{1,0:T(8,128)(2,1)S(1)}, bf16[64,256]{1,0:T(8,128)(2,1)}, u32[]{:S(2)}) copy-start(bf16[64,256]{1,0:T(8,128)(2,1)} %get-tuple-element.29) | copy-start | bytes 98308
  10.7 36.5 %copy-start.13 = (bf16[64,256]{1,0:T(8,128)(2,1)S(1)}, bf16[64,256]{1,0:T(8,128)(2,1)}, u32[]{:S(2)}) copy-start(bf16[64,256]{1,0:T(8,128)(2,1)} %get-tuple-element.30) | copy-start | bytes 98308
  10.7 36.5 %copy-start.12 = (bf16[64,256]{1,0:T(8,128)(2,1)S(1)}, bf16[64,256]{1,0:T(8,128)(2,1)}, u32[]{:S(2)}) copy-start(bf16[64,256]{1,0:T(8,128)(2,1)} %get-tuple-element.31) | copy-start | bytes 98308
  10.7 37.2 %copy-start.1 = (f32[8,16,16]{2,1,0:T(8,128)S(1)}, f32[8,16,16]{2,1,0:T(8,128)}, u32[]{:S(2)}) copy-start(f32[8,16,16]{2,1,0:T(8,128)} %inverse_hbm.1) | copy-start | bytes 24580
  10.7 37.2 %copy-start.5 = (s32[2]{0:T(128)S(1)}, s32[2]{0:T(128)}, u32[]{:S(2)}) copy-start(s32[2]{0:T(128)} %pad_add_fusion.place) | copy-start | bytes 28
  10.7 37.2 %copy-start.6 = (f32[7]{0:T(128)S(1)}, f32[7]{0:T(128)}, u32[]{:S(2)}) copy-start(f32[7]{0:T(128)} %lower.1) | copy-start | bytes 88
  10.7 37.2 %copy-start.7 = (f32[7]{0:T(128)S(1)}, f32[7]{0:T(128)}, u32[]{:S(2)}) copy-start(f32[7]{0:T(128)} %upper.1) | copy-start | bytes 88
  10.7 43.9 %all-to-all-start = ((bf16[8,432,256]{2,1,0:T(8,128)(2,1)}), bf16[8,432,256]{2,1,0:T(8,128)(2,1)}, u32[]{:S(2)}, u32[]{:S(2)}) async-start(bf16[8,432,256]{2,1,0:T(8,128)(2,1)} %get-tuple-element.23), calls=%async_computation | async-start | bytes 3538944 | tf_op jit(solution)/shard_map/all_to_all | solution.py:302
  16.2 37.0 %copy-start.4 = (bf16[64,256]{1,0:T(8,128)(2,1)S(1)}, bf16[64,256]{1,0:T(8,128)(2,1)}, u32[]{:S(2)}) copy-start(bf16[64,256]{1,0:T(8,128)(2,1)} %get-tuple-element.24.refs_0_) | copy-start | bytes 98308
  16.3 30.9 %collective-permute-start.2 = (bf16[64,256]{1,0:T(8,128)(2,1)S(1)}, bf16[64,256]{1,0:T(8,128)(2,1)S(1)}, u32[]{:S(2)}, u32[]{:S(2)}) collective-permute-start(bf16[64,256]{1,0:T(8,128)(2,1)S(1)} %copy-done.18), channel_id=1, source_target_pairs={{0,1},{1,2},{2,3},{3,4},{4,5},{5,6},{6,7},{7,0},{8,9},{9,10},{10,1... | collective-permute-start | bytes 98312 | tf_op jit(solution)/shard_map/ppermute | solution.py:304
  18.6 28.6 %collective-permute-start.3 = (bf16[64,256]{1,0:T(8,128)(2,1)S(1)}, bf16[64,256]{1,0:T(8,128)(2,1)S(1)}, u32[]{:S(2)}, u32[]{:S(2)}) collective-permute-start(bf16[64,256]{1,0:T(8,128)(2,1)S(1)} %copy-done.17), channel_id=1, source_target_pairs={{0,2},{1,3},{2,4},{3,5},{4,6},{5,7},{6,0},{7,1},{8,10},{9,11},{10,... | collective-permute-start | bytes 98312 | tf_op jit(solution)/shard_map/ppermute | solution.py:304
  19.8 21.4 %collective-permute-start = (f32[8,256]{1,0:T(8,128)S(1)}, f32[8,256]{1,0:T(8,128)S(1)}, u32[]{:S(2)}, u32[]{:S(2)}) collective-permute-start(f32[8,256]{1,0:T(8,128)S(1)} %pad_maximum_fusion), channel_id=1, source_target_pairs={{224,0},{232,8},{240,16},{248,24},{160,32},{168,40},{176,48},{184,... | collective-permute-start | bytes 24584 | tf_op jit(solution)/shard_map/ppermute | solution.py:274
  25.9 18.0 %collective-permute-start.1 = (f32[8,256]{1,0:T(8,128)S(1)}, f32[8,256]{1,0:T(8,128)S(1)}, u32[]{:S(2)}, u32[]{:S(2)}) collective-permute-start(f32[8,256]{1,0:T(8,128)S(1)} %pad_maximum_fusion), channel_id=1, source_target_pairs={{192,0},{200,8},{208,16},{216,24},{128,32},{136,40},{144,48},{152,... | collective-permute-start | bytes 24584 | tf_op jit(solution)/shard_map/ppermute | solution.py:274
  25.9 27.3 %collective-permute-start.4 = (bf16[64,256]{1,0:T(8,128)(2,1)S(1)}, bf16[64,256]{1,0:T(8,128)(2,1)S(1)}, u32[]{:S(2)}, u32[]{:S(2)}) collective-permute-start(bf16[64,256]{1,0:T(8,128)(2,1)S(1)} %copy-done.16), channel_id=1, source_target_pairs={{0,3},{1,4},{2,5},{3,6},{4,7},{5,0},{6,1},{7,2},{8,11},{9,12},{10,... | collective-permute-start | bytes 98312 | tf_op jit(solution)/shard_map/ppermute | solution.py:304
  41.2 12.0 %collective-permute-start.5 = (bf16[64,256]{1,0:T(8,128)(2,1)S(1)}, bf16[64,256]{1,0:T(8,128)(2,1)S(1)}, u32[]{:S(2)}, u32[]{:S(2)}) collective-permute-start(bf16[64,256]{1,0:T(8,128)(2,1)S(1)} %copy-done.15), channel_id=1, source_target_pairs={{0,4},{1,5},{2,6},{3,7},{4,0},{5,1},{6,2},{7,3},{8,12},{9,13},{10,... | collective-permute-start | bytes 98312 | tf_op jit(solution)/shard_map/ppermute | solution.py:304
  44.0 9.3 %collective-permute-start.6 = (bf16[64,256]{1,0:T(8,128)(2,1)S(1)}, bf16[64,256]{1,0:T(8,128)(2,1)S(1)}, u32[]{:S(2)}, u32[]{:S(2)}) collective-permute-start(bf16[64,256]{1,0:T(8,128)(2,1)S(1)} %copy-done.14), channel_id=1, source_target_pairs={{0,5},{1,6},{2,7},{3,0},{4,1},{5,2},{6,3},{7,4},{8,13},{9,14},{10,... | collective-permute-start | bytes 98312 | tf_op jit(solution)/shard_map/ppermute | solution.py:304
  47.2 6.0 %collective-permute-start.7 = (bf16[64,256]{1,0:T(8,128)(2,1)S(1)}, bf16[64,256]{1,0:T(8,128)(2,1)S(1)}, u32[]{:S(2)}, u32[]{:S(2)}) collective-permute-start(bf16[64,256]{1,0:T(8,128)(2,1)S(1)} %copy-done.13), channel_id=1, source_target_pairs={{0,6},{1,7},{2,0},{3,1},{4,2},{5,3},{6,4},{7,5},{8,14},{9,15},{10,... | collective-permute-start | bytes 98312 | tf_op jit(solution)/shard_map/ppermute | solution.py:304
  47.2 6.0 %collective-permute-start.8 = (bf16[64,256]{1,0:T(8,128)(2,1)S(1)}, bf16[64,256]{1,0:T(8,128)(2,1)S(1)}, u32[]{:S(2)}, u32[]{:S(2)}) collective-permute-start(bf16[64,256]{1,0:T(8,128)(2,1)S(1)} %copy-done.12), channel_id=1, source_target_pairs={{0,7},{1,0},{2,1},{3,2},{4,3},{5,4},{6,5},{7,6},{8,15},{9,8},{10,9... | collective-permute-start | bytes 98312 | tf_op jit(solution)/shard_map/ppermute | solution.py:304
  51.6 6.7 %copy-start.3 = (f32[16,128]{1,0:T(8,128)}, f32[16,128]{1,0:T(8,128)S(1)}, u32[]{:S(2)}) copy-start(f32[16,128]{1,0:T(8,128)S(1)} %get-tuple-element.21.needed) | copy-start | bytes 24580
  58.4 12.8 %collective-permute-start.9 = (bf16[432,256]{1,0:T(8,128)(2,1)S(1)}, bf16[432,256]{1,0:T(8,128)(2,1)S(1)}, u32[]{:S(2)}, u32[]{:S(2)}) collective-permute-start(bf16[432,256]{1,0:T(8,128)(2,1)S(1)} %get-tuple-element.32), channel_id=1, source_target_pairs={{0,224},{8,232},{16,240},{24,248},{32,160},{40,168},{48,176},{56,1... | collective-permute-start | bytes 663560 | tf_op jit(solution)/shard_map/ppermute | solution.py:349
  58.5 10.5 %collective-permute-start.11 = (bf16[64,256]{1,0:T(8,128)(2,1)S(1)}, bf16[64,256]{1,0:T(8,128)(2,1)S(1)}, u32[]{:S(2)}, u32[]{:S(2)}) collective-permute-start(bf16[64,256]{1,0:T(8,128)(2,1)S(1)} %get-tuple-element.34), channel_id=1, source_target_pairs={{0,224},{8,232},{16,240},{24,248},{32,160},{40,168},{48,176},{56,1... | collective-permute-start | bytes 98312 | tf_op jit(solution)/shard_map/ppermute | solution.py:348
  63.8 7.4 %collective-permute-start.12 = (bf16[64,256]{1,0:T(8,128)(2,1)S(1)}, bf16[64,256]{1,0:T(8,128)(2,1)S(1)}, u32[]{:S(2)}, u32[]{:S(2)}) collective-permute-start(bf16[64,256]{1,0:T(8,128)(2,1)S(1)} %get-tuple-element.35), channel_id=1, source_target_pairs={{0,192},{8,200},{16,208},{24,216},{32,128},{40,136},{48,144},{56,1... | collective-permute-start | bytes 98312 | tf_op jit(solution)/shard_map/ppermute | solution.py:348
  71.2 19.4 %copy-start = (bf16[432,256]{1,0:T(8,128)(2,1)}, bf16[432,256]{1,0:T(8,128)(2,1)S(1)}, u32[]{:S(2)}) copy-start(bf16[432,256]{1,0:T(8,128)(2,1)S(1)} %collective-permute-done.9.moved.first) | copy-start | bytes 663556
  72.0 18.5 %all-to-all-start.1 = ((bf16[8,128,256]{2,1,0:T(8,128)(2,1)}), bf16[8,128,256]{2,1,0:T(8,128)(2,1)S(1)}, u32[]{:S(2)}, u32[]{:S(2)}) async-start(bf16[8,128,256]{2,1,0:T(8,128)(2,1)} %join.1), calls=%async_computation.1 | async-start | bytes 1048576 | tf_op jit(solution)/shard_map/all_to_all | solution.py:359
  76.8 13.7 %collective-permute-start.10 = (bf16[432,256]{1,0:T(8,128)(2,1)S(1)}, bf16[432,256]{1,0:T(8,128)(2,1)S(1)}, u32[]{:S(2)}, u32[]{:S(2)}) collective-permute-start(bf16[432,256]{1,0:T(8,128)(2,1)S(1)} %get-tuple-element.33), channel_id=1, source_target_pairs={{0,192},{8,200},{16,208},{24,216},{32,128},{40,136},{48,144},{56,1... | collective-permute-start | bytes 663560 | tf_op jit(solution)/shard_map/ppermute | solution.py:349
  90.5 0.9 copy-start.8
  (2 other events, 1.4 us)

commit v4 on v3

--- a/solution.py
+++ b/solution.py
@@ -95,7 +95,8 @@
         spread[here, :] = result
         rounded[here, :] = result.astype(bf16)
         rows = pl.ds(part * PART_ROWS, PART_ROWS)
-        sends.append(pltpu.make_async_copy(spread.at[rows], spread_hbm.at[rows], sent.at[part]))
+        target = spread_hbm.at[rows, pl.ds(0, INNER)]
+        sends.append(pltpu.make_async_copy(spread.at[rows], target, sent.at[part]))
         sends[-1].start()
     edges[:, :INNER] = dot(edge_select(ROWS, CHANNELS, 0), rounded[...]).astype(bf16)
     edges[:, INNER:] = jnp.zeros((EDGE, RIM), bf16)
@@ -126,21 +127,11 @@
         copy.wait()
 
 
-def weight_kernel(place, first, second, weights):
-    base = place[0] // GROUP * GROUP
-    for m, meta in enumerate((first, second)):
-        slots = meta[0:4, :].astype(jnp.int32)
-        for r in range(GROUP):
-            position = iota((CAP, RIM), 0) + (base + r) * CAP
-            value = jnp.zeros((CAP, RIM), f32)
-            for d in range(4):
-                value = value + jnp.where(slots[d : d + 1, :] == position, meta[4 + d : 5 + d, :], 0.0)
-            high, low = split(value)
-            weights[m, r * CAP : (r + 1) * CAP, :RIM] = high
-            weights[m, r * CAP : (r + 1) * CAP, RIM:] = low
-
-
-def setup_kernel(place, lower, upper, corner, block_inverse, needed, spikes):
+def setup_kernel(
+    place, lower, upper, corner, block_inverse, slots, factors, needed, spikes, meta
+):
+    meta[:4, :] = slots[...].astype(f32)
+    meta[4:, :] = factors[...]
     size = 2 * BLOCKS
     shape = (size, 128)
     row, lane = iota(shape, 0), iota(shape, 1)
@@ -176,18 +167,31 @@
     spikes[...] = jnp.where(lane < 64, high.astype(f32), low.astype(f32)).astype(bf16)
 
 
-def partial_kernel(weights, lists, coupled, *outs):
-    del coupled
-    for m in range(2):
-        values = [lists[r, :, m * CAP : (m + 1) * CAP] for r in range(GROUP)]
-        both = dot(jnp.concatenate(values, axis=1), weights[m])
-        result = (both[:, :RIM] + both[:, RIM:]).astype(bf16)
-        outs[m][...] = dot(edge_select(ROWS, CHANNELS, 0), result).astype(bf16)
-        outs[2 + m][...] = result
-
-
-def solve_kernel(place, needed, *refs):
-    chunks, coupled = refs[:BLOCKS], refs[BLOCKS]
+def partial_kernel(place, first_meta, second_meta, lists, coupled, first, second, shared):
+    base = place[0] // GROUP * GROUP
+    shared[:, :EDGE, :] = coupled[...]
+    for m, (meta, partial) in enumerate(((first_meta, first), (second_meta, second))):
+        slots = meta[:4, :].astype(jnp.int32) - base * CAP
+        total = jnp.zeros((ROWS, RIM), f32)
+        for r in range(0, GROUP, 2):
+            position = iota((2 * CAP, RIM), 0) + r * CAP
+            weights = jnp.zeros((2 * CAP, RIM), f32)
+            for d in range(4):
+                hit = slots[d : d + 1, :] == position
+                weights = weights + jnp.where(hit, meta[4 + d : 5 + d, :], 0.0)
+            columns = slice(m * CAP, (m + 1) * CAP)
+            values = jnp.concatenate([lists[r, :, columns], lists[r + 1, :, columns]], axis=1)
+            total = total + dot(values, weights.astype(bf16))
+        result = total.astype(bf16)
+        partial[...] = result
+        edges = dot(edge_select(ROWS, CHANNELS, 0), result).astype(bf16)
+        for k in range(BLOCKS):
+            shared[k, EDGE * (m + 1) : EDGE * (m + 2), :] = edges
+
+
+def solve_kernel(place, needed, meta, *refs):
+    chunks, coupled, passed = refs[:BLOCKS], refs[BLOCKS], refs[BLOCKS + 1]
+    passed[...] = meta[...]
     values = [chunks[shift][...].astype(f32) for shift in range(BLOCKS)]
     for k in range(BLOCKS):
         for p in range(2):
@@ -200,39 +204,34 @@
             coupled[k, 32 * p : 32 * p + 32, :] = total.astype(bf16)
 
 
-def join_kernel(first, second, coupled, moved, edges):
-    del moved
-    both = (first[...].astype(f32) + second[...].astype(f32)).astype(bf16)
-    for k in range(BLOCKS):
-        edges[k, :EDGE, :] = coupled[k]
-        edges[k, EDGE:, :] = both
-
-
-def finish_kernel(place, needed, spread, first, second, coupled, spikes, result):
-    step = pl.program_id(0)
-
-    @pl.when(step < INNER // 256)
-    def _():
-        mine = coupled[step, :EDGE, :]
-        correction = dot(spikes[...], jnp.concatenate([mine, mine], axis=0))
-        result[...] = (spread[...] - correction).astype(bf16)
-
-    @pl.when(step == INNER // 256)
-    def _():
-        own = place[1]
-        halves = []
+def own_kernel(place, needed, shared, *outs):
+    own = place[1]
+    for m in range(2):
         for p in range(2):
             total = jnp.zeros((32, RIM), f32)
             for k in range(BLOCKS):
                 for b in range(2):
                     factor = needed[2 * own + p, 2 * BLOCKS + 2 * k + b]
-                    edge = coupled[k, EDGE + 32 * b : EDGE + 32 * b + 32, :]
-                    total = total + factor * edge.astype(f32)
-            halves.append(total)
-        mine = jnp.concatenate(halves, axis=0).astype(bf16)
-        correction = dot(spikes[...], jnp.concatenate([mine, mine], axis=0))
-        ghost = first[...].astype(f32) + second[...].astype(f32)
-        result[...] = (ghost - correction).astype(bf16)
+                    row = EDGE * (m + 1) + 32 * b
+                    total = total + factor * shared[k, row : row + 32, :].astype(f32)
+            outs[m][32 * p : 32 * p + 32, :] = total.astype(bf16)
+
+
+def finish_kernel(spread, shared, spikes, result):
+    for j in range(2):
+        here = slice(256 * j, 256 * (j + 1))
+        coupled = shared[j, :EDGE, :]
+        correction = dot(spikes[...], jnp.concatenate([coupled, coupled], axis=0))
+        result[:, here] = (spread[:, here] - correction).astype(bf16)
+
+
+def ghost_kernel(whole, first, second, first_coupled, second_coupled, spikes, result):
+    del whole
+    high, low = split(first_coupled[...].astype(f32) + second_coupled[...].astype(f32))
+    correction = dot(spikes[...], jnp.concatenate([high, high], axis=0))
+    correction = correction + dot(spikes[:, :EDGE], low)
+    ghost = first[...].astype(f32) + second[...].astype(f32)
+    result[...] = (ghost - correction).astype(bf16)
 
 
 SMEM = pl.BlockSpec(memory_space=pltpu.SMEM)
@@ -270,16 +269,13 @@
     velocity = velocity.reshape(3 * DEPTH, CELLS)
     place = jnp.stack([lax.axis_index("ang"), lax.axis_index("rad")]).astype(jnp.int32)
 
-    meta = jnp.concatenate([donor_slot.astype(f32), intersection_weight], axis=0)
-    metas = [lax.ppermute(meta, "ang", crossing(m, True)) for m in range(2)]
-
     groups = [list(range(g * GROUP, (g + 1) * GROUP)) for g in range(TILES // GROUP)]
     spread, lists, *chunks = pl.pallas_call(
         head_kernel,
         in_specs=[SMEM, SMEM] + [ANY] * 4,
         out_specs=[ANY] * 2 + [VMEM] * BLOCKS,
         out_shape=[
-            jax.ShapeDtypeStruct((ROWS, INNER), f32),
+            jax.ShapeDtypeStruct((ROWS, CELLS), f32),
             jax.ShapeDtypeStruct((GROUP, ROWS, 2 * CAP), bf16),
         ]
         + [jax.ShapeDtypeStruct((EDGE, 256), bf16)] * BLOCKS,
@@ -305,76 +301,90 @@
         for shift in range(1, BLOCKS)
     ]
 
-    weights = pl.pallas_call(
-        weight_kernel,
-        in_specs=[SMEM, VMEM, VMEM],
-        out_specs=VMEM,
-        out_shape=jax.ShapeDtypeStruct((2, GROUP * CAP, 2 * RIM), bf16),
-        compiler_params=params(8),
-        name="weights",
-    )(place, *metas)
-
-    needed, spikes = pl.pallas_call(
+    needed, spikes, meta = pl.pallas_call(
         setup_kernel,
-        in_specs=[SMEM, SMEM, SMEM, SMEM, VMEM],
-        out_specs=[VMEM] * 2,
+        in_specs=[SMEM, SMEM, SMEM, SMEM] + [VMEM] * 3,
+        out_specs=[VMEM] * 3,
         out_shape=[
             jax.ShapeDtypeStruct((2 * BLOCKS, 128), f32),
             jax.ShapeDtypeStruct((ROWS, 128), bf16),
+            jax.ShapeDtypeStruct((8, RIM), f32),
         ],
         compiler_params=params(4),
         name="setup",
-    )(place, lower_coupling, upper_coupling, block_inverse, block_inverse)
-
-    coupled = pl.pallas_call(
+    )(
+        place,
+        lower_coupling,
+        upper_coupling,
+        block_inverse,
+        block_inverse,
+        donor_slot,
+        intersection_weight,
+    )
+
+    coupled, meta = pl.pallas_call(
         solve_kernel,
-        in_specs=[SMEM] * 2 + [VMEM] * BLOCKS,
-        out_specs=VMEM,
-        out_shape=jax.ShapeDtypeStruct((BLOCKS, EDGE, 256), bf16),
+        in_specs=[SMEM] * 2 + [VMEM] * (BLOCKS + 1),
+        out_specs=[VMEM] * 2,
+        out_shape=[
+            jax.ShapeDtypeStruct((BLOCKS, EDGE, 256), bf16),
+            jax.ShapeDtypeStruct((8, RIM), f32),
+        ],
         compiler_params=params(4),
         name="solve",
-    )(place, needed, *chunks)
-
-    *first_edges, first, second = pl.pallas_call(
+    )(place, needed, meta, *chunks)
+
+    metas = [lax.ppermute(meta, "ang", crossing(m, True)) for m in range(2)]
+    first, second, shared = pl.pallas_call(
         partial_kernel,
-        in_specs=[VMEM] * 2 + [ANY],
-        out_specs=[VMEM] * 4,
-        out_shape=[jax.ShapeDtypeStruct((EDGE, RIM), bf16)] * 2
-        + [jax.ShapeDtypeStruct((ROWS, RIM), bf16)] * 2,
+        in_specs=[SMEM] + [VMEM] * 4,
+        out_specs=[VMEM] * 3,
+        out_shape=[
+            jax.ShapeDtypeStruct((ROWS, RIM), bf16),
+            jax.ShapeDtypeStruct((ROWS, RIM), bf16),
+            jax.ShapeDtypeStruct((BLOCKS, 3 * EDGE, 256), bf16),
+        ],
         compiler_params=params(14),
         name="partial",
-    )(weights, donors, coupled)
-
-    first_edges = [lax.ppermute(first_edges[m], "ang", crossing(m, False)) for m in range(2)]
+    )(place, *metas, donors, coupled)
+
+    shared = lax.all_to_all(shared, "rad", 0, 0)
     ghosts = [lax.ppermute(value, "ang", crossing(m, False)) for m, value in enumerate((first, second))]
 
-    joined = pl.pallas_call(
-        join_kernel,
-        in_specs=[VMEM] * 3 + [ANY],
-        out_specs=VMEM,
-        out_shape=jax.ShapeDtypeStruct((BLOCKS, 2 * EDGE, RIM), bf16),
+    own = pl.pallas_call(
+        own_kernel,
+        in_specs=[SMEM] * 2 + [VMEM],
+        out_specs=[VMEM] * 2,
+        out_shape=[jax.ShapeDtypeStruct((EDGE, RIM), bf16)] * 2,
         compiler_params=params(4),
-        name="join",
-    )(*first_edges, coupled, ghosts[0])
-    joined = lax.all_to_all(joined, "rad", 0, 0)
+        name="own",
+    )(place, needed, shared)
+    own = [lax.ppermute(value, "ang", crossing(m, False)) for m, value in enumerate(own)]
 
     result = pl.pallas_call(
         finish_kernel,
-        grid=(CELLS // 256,),
+        grid=(CELLS // 512,),
         in_specs=[
-            SMEM,
-            SMEM,
-            pl.BlockSpec((ROWS, 256), lambda i: (0, jnp.minimum(i, INNER // 256 - 1))),
-            whole((ROWS, RIM)),
-            whole((ROWS, RIM)),
-            whole((BLOCKS, 2 * EDGE, 256)),
+            pl.BlockSpec((ROWS, 512), lambda i: (0, i)),
+            pl.BlockSpec((2, 3 * EDGE, 256), lambda i: (i, 0, 0)),
             whole((ROWS, 128)),
         ],
-        out_specs=pl.BlockSpec((ROWS, 256), lambda i: (0, i)),
+        out_specs=pl.BlockSpec((ROWS, 512), lambda i: (0, i)),
         out_shape=jax.ShapeDtypeStruct((ROWS, CELLS), bf16),
-        compiler_params=params(61),
+        compiler_params=params(6),
         name="finish",
-    )(place, needed, spread, *ghosts, joined, spikes)
+    )(spread, shared, spikes)
+
+    result = pl.pallas_call(
+        ghost_kernel,
+        grid=(1,),
+        in_specs=[ANY] + [whole((ROWS, RIM))] * 2 + [whole((EDGE, RIM))] * 2 + [whole((ROWS, 128))],
+        out_specs=pl.BlockSpec((ROWS, RIM), lambda i: (0, INNER // RIM)),
+        out_shape=jax.ShapeDtypeStruct((ROWS, CELLS), bf16),
+        input_output_aliases={0: 0},
+        compiler_params=params(6),
+        name="ghosts",
+    )(result, *ghosts, *own, spikes)
     return result.reshape(CHANNELS, DEPTH, CELLS)
 
 

time: 99.3 us -> 76.8 us (0.77)
  waiting for transfers between devices: 32.3 us -> 18.5 us
  Pallas kernels: 27.2 us -> 21.7 us
  starting transfers between devices: 36.1 us -> 32.4 us
    all_to_all x1, waiting for transfers between devices: 0.01 us -> 9.7 us  [shards(): shared = lax.all_to_all(shared, 'rad', 0, 0)]
    ppermute x2 -> x4, waiting for transfers between devices: 11.5 us -> 3.36 us  [shards(): lax.ppermute(value, 'ang', crossing(m, False))]
    ppermute x2, waiting for transfers between devices: 13.4 us -> 5.39 us  [shards(): metas = [lax.ppermute(meta, 'ang', crossing(m, True)) for m in range(2)]]
    ppermute x2 -> x0, waiting for transfers between devices: 7.35 us -> none  [shards(): lax.ppermute(first_edges[m], 'ang', crossing(m, False))]
    pallas_call x6, Pallas kernels: 17.2 us -> 11.7 us  [the longest x1 3.05 us: shards(): pl.pallas_call(setup_kernel, in_specs=[SMEM, SMEM, SMEM, SMEM] + [VMEM] *...]
    ppermute x2 -> x0, starting transfers between devices: 5.36 us -> none  [shards(): lax.ppermute(first_edges[m], 'ang', crossing(m, False))]
    ppermute x2 -> x4, starting transfers between devices: 2.27 us -> 5.27 us  [shards(): lax.ppermute(value, 'ang', crossing(m, False))]
    ppermute x7, starting transfers between devices: 12.1 us -> 9.95 us  [shards(): lax.ppermute(chunks[shift], 'rad', [(k, (k + shift) % BLOCKS) for k in ra...]
  transfers between devices with their start and end apart: 15 -> 15, of which waited for: 4 -> 4; matrix products, arithmetic and copies ran while one was open for 0% -> 0% of each run, Pallas kernels for 6% -> 10%
where the time goes in v4:
time: 76.8 us; the launch traced here: 75.5 us
  starting transfers between devices  32.4 us (42%)
  Pallas kernels  21.7 us (28%)
  waiting for transfers between devices  18.5 us (24%)
  local copies, waits for them, and re-layouts  2.07 us (3%)
    pallas_call x1, Pallas kernels, shards(): pl.pallas_call(head_kernel, in_specs=[SMEM, SMEM] + [ANY] * 4, out_specs=...  9.99 us
    ppermute x7, starting transfers between devices, shards(): lax.ppermute(chunks[shift], 'rad', [(k, (k + shift) % BLOCKS) for k in ra...  9.95 us
    all_to_all x1, waiting for transfers between devices, shards(): shared = lax.all_to_all(shared, 'rad', 0, 0)  9.7 us
    ppermute x2, starting transfers between devices, shards(): metas = [lax.ppermute(meta, 'ang', crossing(m, True)) for m in range(2)]  6.37 us
    all_to_all x1, starting transfers between devices, shards(): donors = lax.all_to_all(lists, 'ang', 0, 0, axis_index_groups=groups)  5.51 us
    ppermute x2, waiting for transfers between devices, shards(): metas = [lax.ppermute(meta, 'ang', crossing(m, True)) for m in range(2)]  5.39 us
    all_to_all x1, starting transfers between devices, shards(): shared = lax.all_to_all(shared, 'rad', 0, 0)  5.33 us
    ppermute x4, starting transfers between devices, shards(): lax.ppermute(value, 'ang', crossing(m, False))  5.27 us
  transfers between devices with their start and end apart: 15, of which 4 were waited for; matrix products, arithmetic and copies ran while one was open for 0% of the time, Pallas kernels for 10%

profile of v4, /device:TPU:33, one launch (start us, length us, event | category | flops | bytes accessed | tf_op | source)
XLA Modules:
  0.0 75.5 jit_solution(14286739677582764989)
XLA Ops:
  0.0 0.7 pad_add_fusion.place
  0.7 10.0 %head.1 = (f32[432,2048]{1,0:T(8,128)}, bf16[8,432,256]{2,1,0:T(8,128)(2,1)}, bf16[64,256]{1,0:T(8,128)(2,1)}, bf16[64,256]{1,0:T(8,128)(2,1)}, bf16[64,256]{1,0...) custom-call(s32[2]{0:T(128)} %pad_add_fusion.place, ...), custom_call_target="tpu_custom_call" | custom-call | tf_op jit(solution)/shard_map/head/pallas_call | solution.py:273
  10.7 0.0 copy-start.1
  10.8 0.0 copy-start.4
  10.8 0.0 copy-start.5
  10.8 0.0 copy-start.6
  10.8 5.5 %all-to-all-start = ((bf16[8,432,256]{2,1,0:T(8,128)(2,1)}), bf16[8,432,256]{2,1,0:T(8,128)(2,1)S(1)}, u32[]{:S(2)}, u32[]{:S(2)}) async-start(bf16[8,432,256]{2,1,0:T(8,128)(2,1)} %get-tuple-element.37), calls=%async_computation | async-start | bytes 3538944 | tf_op jit(solution)/shard_map/all_to_all | solution.py:298
  16.3 2.3 %collective-permute-start = (bf16[64,256]{1,0:T(8,128)(2,1)S(1)}, bf16[64,256]{1,0:T(8,128)(2,1)S(1)}, u32[]{:S(2)}, u32[]{:S(2)}) collective-permute-start(bf16[64,256]{1,0:T(8,128)(2,1)S(1)} %copy-done.14), channel_id=1, source_target_pairs={{0,1},{1,2},{2,3},{3,4},{4,5},{5,6},{6,7},{7,0},{8,9},{9,10},{10,1... | collective-permute-start | bytes 98312 | tf_op jit(solution)/shard_map/ppermute | solution.py:300
  18.7 1.2 %collective-permute-start.1 = (bf16[64,256]{1,0:T(8,128)(2,1)S(1)}, bf16[64,256]{1,0:T(8,128)(2,1)S(1)}, u32[]{:S(2)}, u32[]{:S(2)}) collective-permute-start(bf16[64,256]{1,0:T(8,128)(2,1)S(1)} %copy-done.13), channel_id=1, source_target_pairs={{0,2},{1,3},{2,4},{3,5},{4,6},{5,7},{6,0},{7,1},{8,10},{9,11},{10,... | collective-permute-start | bytes 98312 | tf_op jit(solution)/shard_map/ppermute | solution.py:300
  19.9 1.6 %collective-permute-start.2 = (bf16[64,256]{1,0:T(8,128)(2,1)S(1)}, bf16[64,256]{1,0:T(8,128)(2,1)S(1)}, u32[]{:S(2)}, u32[]{:S(2)}) collective-permute-start(bf16[64,256]{1,0:T(8,128)(2,1)S(1)} %copy-done.12), channel_id=1, source_target_pairs={{0,3},{1,4},{2,5},{3,6},{4,7},{5,0},{6,1},{7,2},{8,11},{9,12},{10,... | collective-permute-start | bytes 98312 | tf_op jit(solution)/shard_map/ppermute | solution.py:300
  21.5 0.5 collective-permute-start.3
  22.0 1.9 %collective-permute-start.4 = (bf16[64,256]{1,0:T(8,128)(2,1)S(1)}, bf16[64,256]{1,0:T(8,128)(2,1)S(1)}, u32[]{:S(2)}, u32[]{:S(2)}) collective-permute-start(bf16[64,256]{1,0:T(8,128)(2,1)S(1)} %copy-done.10), channel_id=1, source_target_pairs={{0,5},{1,6},{2,7},{3,0},{4,1},{5,2},{6,3},{7,4},{8,13},{9,14},{10,... | collective-permute-start | bytes 98312 | tf_op jit(solution)/shard_map/ppermute | solution.py:300
  24.0 0.7 collective-permute-start.5
  24.6 1.7 %collective-permute-start.6 = (bf16[64,256]{1,0:T(8,128)(2,1)S(1)}, bf16[64,256]{1,0:T(8,128)(2,1)S(1)}, u32[]{:S(2)}, u32[]{:S(2)}) collective-permute-start(bf16[64,256]{1,0:T(8,128)(2,1)S(1)} %copy-done.8), channel_id=1, source_target_pairs={{0,7},{1,0},{2,1},{3,2},{4,3},{5,4},{6,5},{7,6},{8,15},{9,8},{10,9... | collective-permute-start | bytes 98312 | tf_op jit(solution)/shard_map/ppermute | solution.py:300
  26.3 3.0 %setup.1 = (f32[16,128]{1,0:T(8,128)S(1)}, bf16[432,128]{1,0:T(8,128)(2,1)S(1)}, f32[8,256]{1,0:T(8,128)S(1)}) custom-call(s32[2]{0:T(128)S(1)} %copy-done.3, f32[7]{0:T(128)S(1)} %copy-done.6, f32[7]{0:T(128)S(1)} %copy-done.7, f32[8,16,16]{2,1,0:T(8,128)S(1)} %copy-done.1, f32[8,16,16]{2,1,0:T(8,128)S(1)} %copy-done.1, s32[4,256]{1,0:T(4,128)S(1)} %copy-done.4, ...), custom_call_target="tpu_custom_call" | custom-call | tf_op jit(solution)/shard_map/setup/pallas_call | solution.py:304
  29.5 1.3 %solve.1 = (bf16[8,64,256]{2,1,0:T(8,128)(2,1)S(1)}, f32[8,256]{1,0:T(8,128)S(1)}) custom-call(s32[2]{0:T(128)S(1)} %copy-done.3, f32[16,128]{1,0:T(8,128)S(1)} %get-tuple-element.26.needed, f32[8,256]{1,0:T(8,128)S(1)} %get-tuple-element.27.meta, bf16[64,256]{1,0:T(8,128)(2,1)S(1)} %copy-done.2, bf16[64,256]{1,0:T(8,128)(2,1)S(1)} %collective-permute-done.refs_1_, ...), custom_call_target="tpu_custom_call" | custom-call | tf_op jit(solution)/shard_map/solve/pallas_call | solution.py:325
  30.8 5.2 %collective-permute-start.8 = (f32[8,256]{1,0:T(8,128)S(1)}, f32[8,256]{1,0:T(8,128)S(1)}, u32[]{:S(2)}, u32[]{:S(2)}) collective-permute-start(f32[8,256]{1,0:T(8,128)S(1)} %get-tuple-element.36), channel_id=1, source_target_pairs={{192,0},{200,8},{208,16},{216,24},{128,32},{136,40},{144,48},{152,... | collective-permute-start | bytes 24584 | tf_op jit(solution)/shard_map/ppermute | solution.py:337
  36.0 1.2 %collective-permute-start.7 = (f32[8,256]{1,0:T(8,128)S(1)}, f32[8,256]{1,0:T(8,128)S(1)}, u32[]{:S(2)}, u32[]{:S(2)}) collective-permute-start(f32[8,256]{1,0:T(8,128)S(1)} %get-tuple-element.36), channel_id=1, source_target_pairs={{224,0},{232,8},{240,16},{248,24},{160,32},{168,40},{176,48},{184,... | collective-permute-start | bytes 24584 | tf_op jit(solution)/shard_map/ppermute | solution.py:337
  37.2 5.4 %collective-permute-done.7.first_meta = f32[8,256]{1,0:T(8,128)S(1)} collective-permute-done((f32[8,256]{1,0:T(8,128)S(1)}, f32[8,256]{1,0:T(8,128)S(1)}, u32[]{:S(2)}, u32[]{:S(2)}) %collective-permute-start.7) | collective-permute-done | bytes 8224 | tf_op jit(solution)/shard_map/ppermute | solution.py:337
  42.6 3.0 %partial.1 = (bf16[432,256]{1,0:T(8,128)(2,1)S(1)}, bf16[432,256]{1,0:T(8,128)(2,1)S(1)}, bf16[8,192,256]{2,1,0:T(8,128)(2,1)}) custom-call(s32[2]{0:T(128)S(1)} %copy-done.3, f32[8,256]{1,0:T(8,128)S(1)} %collective-permute-done.7.first_meta, f32[8,256]{1,0:T(8,128)S(1)} %collective-permute-done.8.second_meta, bf16[8,432,256]{2,1,0:T(8,128)(2,1)S(1)} %all-to-all-done.lists, ...), custom_call_target="tpu_custom_call" | custom-call | tf_op jit(solution)/shard_map/partial/pallas_call | solution.py:338
  45.5 5.3 %all-to-all-start.1 = ((bf16[8,192,256]{2,1,0:T(8,128)(2,1)}), bf16[8,192,256]{2,1,0:T(8,128)(2,1)S(1)}, u32[]{:S(2)}, u32[]{:S(2)}) async-start(bf16[8,192,256]{2,1,0:T(8,128)(2,1)} %get-tuple-element.39), calls=%async_computation.1 | async-start | bytes 1572864 | tf_op jit(solution)/shard_map/all_to_all | solution.py:351
  50.8 2.0 %collective-permute-start.9 = (bf16[432,256]{1,0:T(8,128)(2,1)S(1)}, bf16[432,256]{1,0:T(8,128)(2,1)S(1)}, u32[]{:S(2)}, u32[]{:S(2)}) collective-permute-start(bf16[432,256]{1,0:T(8,128)(2,1)S(1)} %get-tuple-element.41), channel_id=1, source_target_pairs={{0,224},{8,232},{16,240},{24,248},{32,160},{40,168},{48,176},{56,1... | collective-permute-start | bytes 663560 | tf_op jit(solution)/shard_map/ppermute | solution.py:352
  52.8 0.6 collective-permute-start.10
  53.4 9.7 %all-to-all-done.1.shared = bf16[8,192,256]{2,1,0:T(8,128)(2,1)S(1)} async-done(((bf16[8,192,256]{2,1,0:T(8,128)(2,1)}), bf16[8,192,256]{2,1,0:T(8,128)(2,1)S(1)}, u32[]{:S(2)}, u32[]{:S(2)}) %all-to-all-start.1) | async-done | bytes 786464 | tf_op jit(solution)/shard_map/all_to_all | solution.py:351
  63.1 0.9 %own.1 = (bf16[64,256]{1,0:T(8,128)(2,1)S(1)}, bf16[64,256]{1,0:T(8,128)(2,1)S(1)}) custom-call(s32[2]{0:T(128)S(1)} %copy-done.3, f32[16,128]{1,0:T(8,128)S(1)} %get-tuple-element.26.needed, bf16[8,192,256]{2,1,0:T(8,128)(2,1)S(1)} %all-to-all-done.1.shared), custom_call_target="tpu_custom_call" | custom-call | tf_op jit(solution)/shard_map/own/pallas_call | solution.py:354
  64.0 2.0 %collective-permute-start.11 = (bf16[64,256]{1,0:T(8,128)(2,1)S(1)}, bf16[64,256]{1,0:T(8,128)(2,1)S(1)}, u32[]{:S(2)}, u32[]{:S(2)}) collective-permute-start(bf16[64,256]{1,0:T(8,128)(2,1)S(1)} %get-tuple-element.43), channel_id=1, source_target_pairs={{0,224},{8,232},{16,240},{24,248},{32,160},{40,168},{48,176},{56,1... | collective-permute-start | bytes 98312 | tf_op jit(solution)/shard_map/ppermute | solution.py:362
  66.1 0.6 collective-permute-start.12
  66.7 2.0 %copy-done = f32[432,2048]{1,0:T(8,128)S(1)} copy-done((f32[432,2048]{1,0:T(8,128)S(1)}, f32[432,2048]{1,0:T(8,128)}, u32[]{:S(2)}) %copy-start) | copy-done | bytes 3538968
  68.7 2.5 %finish.1.whole = bf16[432,2048]{1,0:T(8,128)(2,1)} custom-call(f32[432,2048]{1,0:T(8,128)S(1)} %copy-done, bf16[8,192,256]{2,1,0:T(8,128)(2,1)S(1)} %all-to-all-done.1.shared, bf16[432,128]{1,0:T(8,128)(2,1)S(1)} %get-tuple-element.40.spikes), custom_call_target="tpu_custom_call" | custom-call | tf_op jit(solution)/shard_map/finish/pallas_call | solution.py:364
  71.2 2.2 %collective-permute-done.10.second = bf16[432,256]{1,0:T(8,128)(2,1)S(1)} collective-permute-done((bf16[432,256]{1,0:T(8,128)(2,1)S(1)}, bf16[432,256]{1,0:T(8,128)(2,1)S(1)}, u32[]{:S(2)}, u32[]{:S(2)}) %collective-permute-start.10) | collective-permute-done | bytes 221216 | tf_op jit(solution)/shard_map/ppermute | solution.py:352
  73.5 1.1 %collective-permute-done.12.second_coupled = bf16[64,256]{1,0:T(8,128)(2,1)S(1)} collective-permute-done((bf16[64,256]{1,0:T(8,128)(2,1)S(1)}, bf16[64,256]{1,0:T(8,128)(2,1)S(1)}, u32[]{:S(2)}, u32[]{:S(2)}) %collective-permute-start.12) | collective-permute-done | bytes 32800 | tf_op jit(solution)/shard_map/ppermute | solution.py:362
  74.6 1.0 %ghosts.1 = bf16[432,2048]{1,0:T(8,128)(2,1)} custom-call(bf16[432,2048]{1,0:T(8,128)(2,1)} %finish.1.whole, bf16[432,256]{1,0:T(8,128)(2,1)S(1)} %collective-permute-done.9.first, bf16[432,256]{1,0:T(8,128)(2,1)S(1)} %collective-permute-done.10.second, bf16[64,256]{1,0:T(8,128)(2,1)S(1)} %collective-permute-done.11.first_coupled, ...), custom_call_target="tpu_custom_call", output_to_operand_aliasing={{}: (0, {})} | custom-call | tf_op jit(solution)/shard_map/ghosts/pallas_call | solution.py:378
  (36 shorter events, 0.1 us)
Async XLA Ops:
  10.7 5.7 %copy-start.14 = (bf16[64,256]{1,0:T(8,128)(2,1)S(1)}, bf16[64,256]{1,0:T(8,128)(2,1)}, u32[]{:S(2)}) copy-start(bf16[64,256]{1,0:T(8,128)(2,1)} %get-tuple-element.29) | copy-start | bytes 98308
  10.7 8.0 %copy-start.13 = (bf16[64,256]{1,0:T(8,128)(2,1)S(1)}, bf16[64,256]{1,0:T(8,128)(2,1)}, u32[]{:S(2)}) copy-start(bf16[64,256]{1,0:T(8,128)(2,1)} %get-tuple-element.30) | copy-start | bytes 98308
  10.7 9.2 %copy-start.12 = (bf16[64,256]{1,0:T(8,128)(2,1)S(1)}, bf16[64,256]{1,0:T(8,128)(2,1)}, u32[]{:S(2)}) copy-start(bf16[64,256]{1,0:T(8,128)(2,1)} %get-tuple-element.31) | copy-start | bytes 98308
  10.7 10.8 %copy-start.11 = (bf16[64,256]{1,0:T(8,128)(2,1)S(1)}, bf16[64,256]{1,0:T(8,128)(2,1)}, u32[]{:S(2)}) copy-start(bf16[64,256]{1,0:T(8,128)(2,1)} %get-tuple-element.32) | copy-start | bytes 98308
  10.7 11.3 %copy-start.10 = (bf16[64,256]{1,0:T(8,128)(2,1)S(1)}, bf16[64,256]{1,0:T(8,128)(2,1)}, u32[]{:S(2)}) copy-start(bf16[64,256]{1,0:T(8,128)(2,1)} %get-tuple-element.33) | copy-start | bytes 98308
  10.7 13.2 %copy-start.9 = (bf16[64,256]{1,0:T(8,128)(2,1)S(1)}, bf16[64,256]{1,0:T(8,128)(2,1)}, u32[]{:S(2)}) copy-start(bf16[64,256]{1,0:T(8,128)(2,1)} %get-tuple-element.34) | copy-start | bytes 98308
  10.7 13.9 %copy-start.8 = (bf16[64,256]{1,0:T(8,128)(2,1)S(1)}, bf16[64,256]{1,0:T(8,128)(2,1)}, u32[]{:S(2)}) copy-start(bf16[64,256]{1,0:T(8,128)(2,1)} %get-tuple-element.35) | copy-start | bytes 98308
  10.7 15.6 %copy-start.1 = (f32[8,16,16]{2,1,0:T(8,128)S(1)}, f32[8,16,16]{2,1,0:T(8,128)}, u32[]{:S(2)}) copy-start(f32[8,16,16]{2,1,0:T(8,128)} %block_inverse.1) | copy-start | bytes 24580
  10.7 15.6 %copy-start.3 = (s32[2]{0:T(128)S(1)}, s32[2]{0:T(128)}, u32[]{:S(2)}) copy-start(s32[2]{0:T(128)} %pad_add_fusion.place) | copy-start | bytes 28
  10.8 15.6 %copy-start.4 = (s32[4,256]{1,0:T(4,128)S(1)}, s32[4,256]{1,0:T(4,128)}, u32[]{:S(2)}) copy-start(s32[4,256]{1,0:T(4,128)} %slots.1) | copy-start | bytes 12292
  10.8 15.5 %copy-start.5 = (f32[4,256]{1,0:T(4,128)S(1)}, f32[4,256]{1,0:T(4,128)}, u32[]{:S(2)}) copy-start(f32[4,256]{1,0:T(4,128)} %factors.1) | copy-start | bytes 12292
  10.8 15.5 %copy-start.6 = (f32[7]{0:T(128)S(1)}, f32[7]{0:T(128)}, u32[]{:S(2)}) copy-start(f32[7]{0:T(128)} %lower.1) | copy-start | bytes 88
  10.8 15.5 %copy-start.7 = (f32[7]{0:T(128)S(1)}, f32[7]{0:T(128)}, u32[]{:S(2)}) copy-start(f32[7]{0:T(128)} %upper.1) | copy-start | bytes 88
  10.8 18.6 %copy-start.2 = (bf16[64,256]{1,0:T(8,128)(2,1)S(1)}, bf16[64,256]{1,0:T(8,128)(2,1)}, u32[]{:S(2)}) copy-start(bf16[64,256]{1,0:T(8,128)(2,1)} %get-tuple-element.28.refs_0_) | copy-start | bytes 98308
  10.8 31.7 %all-to-all-start = ((bf16[8,432,256]{2,1,0:T(8,128)(2,1)}), bf16[8,432,256]{2,1,0:T(8,128)(2,1)S(1)}, u32[]{:S(2)}, u32[]{:S(2)}) async-start(bf16[8,432,256]{2,1,0:T(8,128)(2,1)} %get-tuple-element.37), calls=%async_computation | async-start | bytes 3538944 | tf_op jit(solution)/shard_map/all_to_all | solution.py:298
  16.3 7.6 %collective-permute-start = (bf16[64,256]{1,0:T(8,128)(2,1)S(1)}, bf16[64,256]{1,0:T(8,128)(2,1)S(1)}, u32[]{:S(2)}, u32[]{:S(2)}) collective-permute-start(bf16[64,256]{1,0:T(8,128)(2,1)S(1)} %copy-done.14), channel_id=1, source_target_pairs={{0,1},{1,2},{2,3},{3,4},{4,5},{5,6},{6,7},{7,0},{8,9},{9,10},{10,1... | collective-permute-start | bytes 98312 | tf_op jit(solution)/shard_map/ppermute | solution.py:300
  18.7 6.0 %collective-permute-start.1 = (bf16[64,256]{1,0:T(8,128)(2,1)S(1)}, bf16[64,256]{1,0:T(8,128)(2,1)S(1)}, u32[]{:S(2)}, u32[]{:S(2)}) collective-permute-start(bf16[64,256]{1,0:T(8,128)(2,1)S(1)} %copy-done.13), channel_id=1, source_target_pairs={{0,2},{1,3},{2,4},{3,5},{4,6},{5,7},{6,0},{7,1},{8,10},{9,11},{10,... | collective-permute-start | bytes 98312 | tf_op jit(solution)/shard_map/ppermute | solution.py:300
  19.9 9.5 %collective-permute-start.2 = (bf16[64,256]{1,0:T(8,128)(2,1)S(1)}, bf16[64,256]{1,0:T(8,128)(2,1)S(1)}, u32[]{:S(2)}, u32[]{:S(2)}) collective-permute-start(bf16[64,256]{1,0:T(8,128)(2,1)S(1)} %copy-done.12), channel_id=1, source_target_pairs={{0,3},{1,4},{2,5},{3,6},{4,7},{5,0},{6,1},{7,2},{8,11},{9,12},{10,... | collective-permute-start | bytes 98312 | tf_op jit(solution)/shard_map/ppermute | solution.py:300
  21.5 7.9 %collective-permute-start.3 = (bf16[64,256]{1,0:T(8,128)(2,1)S(1)}, bf16[64,256]{1,0:T(8,128)(2,1)S(1)}, u32[]{:S(2)}, u32[]{:S(2)}) collective-permute-start(bf16[64,256]{1,0:T(8,128)(2,1)S(1)} %copy-done.11), channel_id=1, source_target_pairs={{0,4},{1,5},{2,6},{3,7},{4,0},{5,1},{6,2},{7,3},{8,12},{9,13},{10,... | collective-permute-start | bytes 98312 | tf_op jit(solution)/shard_map/ppermute | solution.py:300
  22.0 7.4 %collective-permute-start.4 = (bf16[64,256]{1,0:T(8,128)(2,1)S(1)}, bf16[64,256]{1,0:T(8,128)(2,1)S(1)}, u32[]{:S(2)}, u32[]{:S(2)}) collective-permute-start(bf16[64,256]{1,0:T(8,128)(2,1)S(1)} %copy-done.10), channel_id=1, source_target_pairs={{0,5},{1,6},{2,7},{3,0},{4,1},{5,2},{6,3},{7,4},{8,13},{9,14},{10,... | collective-permute-start | bytes 98312 | tf_op jit(solution)/shard_map/ppermute | solution.py:300
  24.0 5.5 %collective-permute-start.5 = (bf16[64,256]{1,0:T(8,128)(2,1)S(1)}, bf16[64,256]{1,0:T(8,128)(2,1)S(1)}, u32[]{:S(2)}, u32[]{:S(2)}) collective-permute-start(bf16[64,256]{1,0:T(8,128)(2,1)S(1)} %copy-done.9), channel_id=1, source_target_pairs={{0,6},{1,7},{2,0},{3,1},{4,2},{5,3},{6,4},{7,5},{8,14},{9,15},{10,... | collective-permute-start | bytes 98312 | tf_op jit(solution)/shard_map/ppermute | solution.py:300
  24.6 4.8 %collective-permute-start.6 = (bf16[64,256]{1,0:T(8,128)(2,1)S(1)}, bf16[64,256]{1,0:T(8,128)(2,1)S(1)}, u32[]{:S(2)}, u32[]{:S(2)}) collective-permute-start(bf16[64,256]{1,0:T(8,128)(2,1)S(1)} %copy-done.8), channel_id=1, source_target_pairs={{0,7},{1,0},{2,1},{3,2},{4,3},{5,4},{6,5},{7,6},{8,15},{9,8},{10,9... | collective-permute-start | bytes 98312 | tf_op jit(solution)/shard_map/ppermute | solution.py:300
  30.8 6.4 %collective-permute-start.8 = (f32[8,256]{1,0:T(8,128)S(1)}, f32[8,256]{1,0:T(8,128)S(1)}, u32[]{:S(2)}, u32[]{:S(2)}) collective-permute-start(f32[8,256]{1,0:T(8,128)S(1)} %get-tuple-element.36), channel_id=1, source_target_pairs={{192,0},{200,8},{208,16},{216,24},{128,32},{136,40},{144,48},{152,... | collective-permute-start | bytes 24584 | tf_op jit(solution)/shard_map/ppermute | solution.py:337
  36.0 6.6 %collective-permute-start.7 = (f32[8,256]{1,0:T(8,128)S(1)}, f32[8,256]{1,0:T(8,128)S(1)}, u32[]{:S(2)}, u32[]{:S(2)}) collective-permute-start(f32[8,256]{1,0:T(8,128)S(1)} %get-tuple-element.36), channel_id=1, source_target_pairs={{224,0},{232,8},{240,16},{248,24},{160,32},{168,40},{176,48},{184,... | collective-permute-start | bytes 24584 | tf_op jit(solution)/shard_map/ppermute | solution.py:337
  45.5 17.6 %all-to-all-start.1 = ((bf16[8,192,256]{2,1,0:T(8,128)(2,1)}), bf16[8,192,256]{2,1,0:T(8,128)(2,1)S(1)}, u32[]{:S(2)}, u32[]{:S(2)}) async-start(bf16[8,192,256]{2,1,0:T(8,128)(2,1)} %get-tuple-element.39), calls=%async_computation.1 | async-start | bytes 1572864 | tf_op jit(solution)/shard_map/all_to_all | solution.py:351
  50.8 20.4 %collective-permute-start.9 = (bf16[432,256]{1,0:T(8,128)(2,1)S(1)}, bf16[432,256]{1,0:T(8,128)(2,1)S(1)}, u32[]{:S(2)}, u32[]{:S(2)}) collective-permute-start(bf16[432,256]{1,0:T(8,128)(2,1)S(1)} %get-tuple-element.41), channel_id=1, source_target_pairs={{0,224},{8,232},{16,240},{24,248},{32,160},{40,168},{48,176},{56,1... | collective-permute-start | bytes 663560 | tf_op jit(solution)/shard_map/ppermute | solution.py:352
  52.8 20.7 %collective-permute-start.10 = (bf16[432,256]{1,0:T(8,128)(2,1)S(1)}, bf16[432,256]{1,0:T(8,128)(2,1)S(1)}, u32[]{:S(2)}, u32[]{:S(2)}) collective-permute-start(bf16[432,256]{1,0:T(8,128)(2,1)S(1)} %get-tuple-element.42), channel_id=1, source_target_pairs={{0,192},{8,200},{16,208},{24,216},{32,128},{40,136},{48,144},{56,1... | collective-permute-start | bytes 663560 | tf_op jit(solution)/shard_map/ppermute | solution.py:352
  64.0 9.5 %collective-permute-start.11 = (bf16[64,256]{1,0:T(8,128)(2,1)S(1)}, bf16[64,256]{1,0:T(8,128)(2,1)S(1)}, u32[]{:S(2)}, u32[]{:S(2)}) collective-permute-start(bf16[64,256]{1,0:T(8,128)(2,1)S(1)} %get-tuple-element.43), channel_id=1, source_target_pairs={{0,224},{8,232},{16,240},{24,248},{32,160},{40,168},{48,176},{56,1... | collective-permute-start | bytes 98312 | tf_op jit(solution)/shard_map/ppermute | solution.py:362
  66.1 8.5 %collective-permute-start.12 = (bf16[64,256]{1,0:T(8,128)(2,1)S(1)}, bf16[64,256]{1,0:T(8,128)(2,1)S(1)}, u32[]{:S(2)}, u32[]{:S(2)}) collective-permute-start(bf16[64,256]{1,0:T(8,128)(2,1)S(1)} %get-tuple-element.44), channel_id=1, source_target_pairs={{0,192},{8,200},{16,208},{24,216},{32,128},{40,136},{48,144},{56,1... | collective-permute-start | bytes 98312 | tf_op jit(solution)/shard_map/ppermute | solution.py:362
  66.7 2.0 %copy-start = (f32[432,2048]{1,0:T(8,128)S(1)}, f32[432,2048]{1,0:T(8,128)}, u32[]{:S(2)}) copy-start(f32[432,2048]{1,0:T(8,128)} %get-tuple-element.25.spread) | copy-start | bytes 10616836

commit v5 on v4

--- a/solution.py
+++ b/solution.py
@@ -51,11 +51,11 @@
     return ((channel >= 0) & (channel < channels) & (column == wanted)).astype(f32).astype(bf16)
 
 
-def head_kernel(place, block_size, cells_hbm, field_hbm, velocity_hbm, inverse_hbm, *refs):
+def head_kernel(block_size, cells_hbm, field_hbm, velocity_hbm, inverse_hbm, *refs):
     spread_hbm, lists_hbm, chunks = refs[0], refs[1], refs[2 : 2 + BLOCKS]
     cells, field, velocity, own, spread, rounded, lists, edges, done, sent = refs[2 + BLOCKS :]
     copies = [
-        pltpu.make_async_copy(inverse_hbm.at[place[1]], own, done.at[0]),
+        pltpu.make_async_copy(inverse_hbm.at[lax.axis_index("rad")], own, done.at[0]),
         pltpu.make_async_copy(velocity_hbm, velocity, done.at[1]),
     ]
     for part in range(PARTS):
@@ -73,6 +73,8 @@
     copies[0].wait()
     tiled = jnp.dot(jnp.dot(rows, own[...], precision=highest), columns, precision=highest)
     high_mat, low_mat = split(jnp.where(same, tiled, 0.0))
+    matrix = jnp.concatenate([high_mat.astype(f32), high_mat.astype(f32), low_mat.astype(f32)], axis=1)
+    matrix = matrix.astype(bf16)
 
     copies[1].wait()
     flow = [velocity[DEPTH * i : DEPTH * (i + 1), :INNER].astype(f32) for i in range(3)]
@@ -89,8 +91,7 @@
                 j, k = (i + 1) % 3, (i + 2) % 3
                 sources.append(f[i] + induction * (flow[j] * f[k] - flow[k] * f[j]))
         source_high, source_low = split(jnp.concatenate(sources, axis=0))
-        result = dot(high_mat, source_high) + dot(high_mat, source_low)
-        result = result + dot(low_mat, source_high)
+        result = dot(matrix, jnp.concatenate([source_high, source_low, source_high], axis=0))
         here = slice(part * PART_ROWS, (part + 1) * PART_ROWS)
         spread[here, :] = result
         rounded[here, :] = result.astype(bf16)
@@ -101,11 +102,11 @@
     edges[:, :INNER] = dot(edge_select(ROWS, CHANNELS, 0), rounded[...]).astype(bf16)
     edges[:, INNER:] = jnp.zeros((EDGE, RIM), bf16)
     for shift in range(BLOCKS):
-        first = pl.multiple_of((place[1] + shift) % BLOCKS * 256, 256)
+        first = pl.multiple_of((lax.axis_index("rad") + shift) % BLOCKS * 256, 256)
         chunks[shift][...] = edges[:, pl.ds(first, 256)]
     copies[2 + PARTS].wait()
 
-    row = place[0] // 4
+    row = lax.axis_index("ang") // 4
     panel, half = row // 4, (row // 2) % 2
     for r in range(GROUP):
         member, y = r // 4, r % 4
@@ -116,11 +117,8 @@
             listed = cells[0, pl.ds(tile, 1), :]
             wanted.append(jnp.where(iota((1, CAP), 1) < block_size[0, tile], listed, -1))
         wanted = jnp.concatenate(wanted, axis=1)
-        total = jnp.zeros((ROWS, 2 * CAP), f32)
-        for first in range(0, INNER, 256):
-            hot = (iota((256, 2 * CAP), 0) + first == wanted).astype(f32).astype(bf16)
-            total = total + dot(rounded[:, first : first + 256], hot)
-        lists[r] = total.astype(bf16)
+        hot = (iota((INNER, 2 * CAP), 0) == wanted).astype(f32).astype(bf16)
+        lists[r] = dot(rounded[...], hot).astype(bf16)
         sends.append(pltpu.make_async_copy(lists.at[r], lists_hbm.at[r], sent.at[PARTS + r]))
         sends[-1].start()
     for copy in sends:
@@ -128,7 +126,7 @@
 
 
 def setup_kernel(
-    place, lower, upper, corner, block_inverse, slots, factors, needed, spikes, meta
+    lower, upper, corner, block_inverse, slots, factors, needed, spikes, meta
 ):
     meta[:4, :] = slots[...].astype(f32)
     meta[4:, :] = factors[...]
@@ -154,7 +152,7 @@
     down = jnp.concatenate([jnp.zeros((2, 128), f32), work[:-2, :]], axis=0)
     needed[...] = jnp.where(row % 2 == 0, up, down)
 
-    k = place[1]
+    k = lax.axis_index("rad")
     ahead = jnp.where(k < BLOCKS - 1, upper[jnp.minimum(k, BLOCKS - 2)], 0.0)
     behind = jnp.where(k > 0, lower[jnp.maximum(k - 1, 0)], 0.0)
     rows = (iota((ROWS, DEPTH), 0) % DEPTH == iota((ROWS, DEPTH), 1)).astype(f32)
@@ -167,29 +165,25 @@
     spikes[...] = jnp.where(lane < 64, high.astype(f32), low.astype(f32)).astype(bf16)
 
 
-def partial_kernel(place, first_meta, second_meta, lists, coupled, first, second, shared):
-    base = place[0] // GROUP * GROUP
+def partial_kernel(first_meta, second_meta, lists, coupled, first, second, shared):
+    base = lax.axis_index("ang") // GROUP * GROUP
     shared[:, :EDGE, :] = coupled[...]
     for m, (meta, partial) in enumerate(((first_meta, first), (second_meta, second))):
         slots = meta[:4, :].astype(jnp.int32) - base * CAP
-        total = jnp.zeros((ROWS, RIM), f32)
-        for r in range(0, GROUP, 2):
-            position = iota((2 * CAP, RIM), 0) + r * CAP
-            weights = jnp.zeros((2 * CAP, RIM), f32)
-            for d in range(4):
-                hit = slots[d : d + 1, :] == position
-                weights = weights + jnp.where(hit, meta[4 + d : 5 + d, :], 0.0)
-            columns = slice(m * CAP, (m + 1) * CAP)
-            values = jnp.concatenate([lists[r, :, columns], lists[r + 1, :, columns]], axis=1)
-            total = total + dot(values, weights.astype(bf16))
-        result = total.astype(bf16)
+        position = iota((GROUP * CAP, RIM), 0)
+        weights = jnp.zeros((GROUP * CAP, RIM), f32)
+        for d in range(4):
+            hit = slots[d : d + 1, :] == position
+            weights = weights + jnp.where(hit, meta[4 + d : 5 + d, :], 0.0)
+        values = [lists[r, :, m * CAP : (m + 1) * CAP] for r in range(GROUP)]
+        result = dot(jnp.concatenate(values, axis=1), weights.astype(bf16)).astype(bf16)
         partial[...] = result
         edges = dot(edge_select(ROWS, CHANNELS, 0), result).astype(bf16)
         for k in range(BLOCKS):
             shared[k, EDGE * (m + 1) : EDGE * (m + 2), :] = edges
 
 
-def solve_kernel(place, needed, meta, *refs):
+def solve_kernel(needed, meta, *refs):
     chunks, coupled, passed = refs[:BLOCKS], refs[BLOCKS], refs[BLOCKS + 1]
     passed[...] = meta[...]
     values = [chunks[shift][...].astype(f32) for shift in range(BLOCKS)]
@@ -197,15 +191,15 @@
         for p in range(2):
             total = jnp.zeros((32, 256), f32)
             for shift in range(BLOCKS):
-                block = (place[1] + BLOCKS - shift) % BLOCKS
+                block = (lax.axis_index("rad") + BLOCKS - shift) % BLOCKS
                 for b in range(2):
                     factor = needed[2 * k + p, 2 * BLOCKS + 2 * block + b]
                     total = total + factor * values[shift][32 * b : 32 * b + 32, :]
             coupled[k, 32 * p : 32 * p + 32, :] = total.astype(bf16)
 
 
-def own_kernel(place, needed, shared, *outs):
-    own = place[1]
+def own_kernel(needed, shared, *outs):
+    own = lax.axis_index("rad")
     for m in range(2):
         for p in range(2):
             total = jnp.zeros((32, RIM), f32)
@@ -267,12 +261,11 @@
 ):
     field = field.reshape(ROWS, CELLS)
     velocity = velocity.reshape(3 * DEPTH, CELLS)
-    place = jnp.stack([lax.axis_index("ang"), lax.axis_index("rad")]).astype(jnp.int32)
 
     groups = [list(range(g * GROUP, (g + 1) * GROUP)) for g in range(TILES // GROUP)]
     spread, lists, *chunks = pl.pallas_call(
         head_kernel,
-        in_specs=[SMEM, SMEM] + [ANY] * 4,
+        in_specs=[SMEM] + [ANY] * 4,
         out_specs=[ANY] * 2 + [VMEM] * BLOCKS,
         out_shape=[
             jax.ShapeDtypeStruct((ROWS, CELLS), f32),
@@ -293,7 +286,7 @@
         ],
         compiler_params=params(60),
         name="head",
-    )(place, block_size, send_cells, field, velocity, block_inverse)
+    )(block_size, send_cells, field, velocity, block_inverse)
 
     donors = lax.all_to_all(lists, "ang", 0, 0, axis_index_groups=groups)
     chunks = chunks[:1] + [
@@ -303,7 +296,7 @@
 
     needed, spikes, meta = pl.pallas_call(
         setup_kernel,
-        in_specs=[SMEM, SMEM, SMEM, SMEM] + [VMEM] * 3,
+        in_specs=[SMEM] * 3 + [VMEM] * 3,
         out_specs=[VMEM] * 3,
         out_shape=[
             jax.ShapeDtypeStruct((2 * BLOCKS, 128), f32),
@@ -313,7 +306,6 @@
         compiler_params=params(4),
         name="setup",
     )(
-        place,
         lower_coupling,
         upper_coupling,
         block_inverse,
@@ -324,7 +316,7 @@
 
     coupled, meta = pl.pallas_call(
         solve_kernel,
-        in_specs=[SMEM] * 2 + [VMEM] * (BLOCKS + 1),
+        in_specs=[SMEM] + [VMEM] * (BLOCKS + 1),
         out_specs=[VMEM] * 2,
         out_shape=[
             jax.ShapeDtypeStruct((BLOCKS, EDGE, 256), bf16),
@@ -332,12 +324,12 @@
         ],
         compiler_params=params(4),
         name="solve",
-    )(place, needed, meta, *chunks)
+    )(needed, meta, *chunks)
 
     metas = [lax.ppermute(meta, "ang", crossing(m, True)) for m in range(2)]
     first, second, shared = pl.pallas_call(
         partial_kernel,
-        in_specs=[SMEM] + [VMEM] * 4,
+        in_specs=[VMEM] * 4,
         out_specs=[VMEM] * 3,
         out_shape=[
             jax.ShapeDtypeStruct((ROWS, RIM), bf16),
@@ -346,19 +338,19 @@
         ],
         compiler_params=params(14),
         name="partial",
-    )(place, *metas, donors, coupled)
+    )(*metas, donors, coupled)
 
     shared = lax.all_to_all(shared, "rad", 0, 0)
     ghosts = [lax.ppermute(value, "ang", crossing(m, False)) for m, value in enumerate((first, second))]
 
     own = pl.pallas_call(
         own_kernel,
-        in_specs=[SMEM] * 2 + [VMEM],
+        in_specs=[SMEM, VMEM],
         out_specs=[VMEM] * 2,
         out_shape=[jax.ShapeDtypeStruct((EDGE, RIM), bf16)] * 2,
         compiler_params=params(4),
         name="own",
-    )(place, needed, shared)
+    )(needed, shared)
     own = [lax.ppermute(value, "ang", crossing(m, False)) for m, value in enumerate(own)]
 
     result = pl.pallas_call(

time: 76.8 us -> 74.6 us (0.971)
  Pallas kernels: 21.7 us -> 20.1 us
    pallas_call x5, Pallas kernels: 18.2 us -> 16.6 us  [the longest x1 8.93 us: shards(): pl.pallas_call(head_kernel, in_specs=[SMEM] + [ANY] * 4, out_specs=[ANY]...]
    unnamed x30 -> x28, local copies, waits for them, and re-layouts: 2.07 us -> 2.07 us
  transfers between devices with their start and end apart: 15 -> 15, of which waited for: 4 -> 4; matrix products, arithmetic and copies ran while one was open for 0% -> 0% of each run, Pallas kernels for 10% -> 11%
where the time goes in v5:
time: 74.6 us; the launch traced here: 73.3 us
  starting transfers between devices  32.5 us (44%)
  Pallas kernels  20.1 us (27%)
  waiting for transfers between devices  18.5 us (25%)
  local copies, waits for them, and re-layouts  2.07 us (3%)
    ppermute x7, starting transfers between devices, shards(): lax.ppermute(chunks[shift], 'rad', [(k, (k + shift) % BLOCKS) for k in ra...  9.95 us
    all_to_all x1, waiting for transfers between devices, shards(): shared = lax.all_to_all(shared, 'rad', 0, 0)  9.7 us
    pallas_call x1, Pallas kernels, shards(): pl.pallas_call(head_kernel, in_specs=[SMEM] + [ANY] * 4, out_specs=[ANY]...  8.93 us
    ppermute x2, starting transfers between devices, shards(): metas = [lax.ppermute(meta, 'ang', crossing(m, True)) for m in range(2)]  6.37 us
    all_to_all x1, starting transfers between devices, shards(): donors = lax.all_to_all(lists, 'ang', 0, 0, axis_index_groups=groups)  5.51 us
    ppermute x2, waiting for transfers between devices, shards(): metas = [lax.ppermute(meta, 'ang', crossing(m, True)) for m in range(2)]  5.4 us
    all_to_all x1, starting transfers between devices, shards(): shared = lax.all_to_all(shared, 'rad', 0, 0)  5.38 us
    ppermute x4, starting transfers between devices, shards(): lax.ppermute(value, 'ang', crossing(m, False))  5.27 us
  transfers between devices with their start and end apart: 15, of which 4 were waited for; matrix products, arithmetic and copies ran while one was open for 0% of the time, Pallas kernels for 11%

profile of v5, /device:TPU:33, one launch (start us, length us, event | category | flops | bytes accessed | tf_op | source)
XLA Modules:
  0.0 73.3 jit_solution(6955990831055307377)
XLA Ops:
  0.0 8.9 %head.1 = (f32[432,2048]{1,0:T(8,128)}, bf16[8,432,256]{2,1,0:T(8,128)(2,1)}, bf16[64,256]{1,0:T(8,128)(2,1)}, bf16[64,256]{1,0:T(8,128)(2,1)}, bf16[64,256]{1,0...) custom-call(s32[1,32]{1,0:T(1,128)} %block_size.1, ...), custom_call_target="tpu_custom_call" | custom-call | tf_op jit(solution)/shard_map/head/pallas_call | solution.py:266
  9.0 0.0 copy-start.1
  9.0 0.0 copy-start.3
  9.0 0.0 copy-start.4
  9.0 0.0 copy-start.5
  9.1 0.0 copy-start.6
  9.1 5.5 %all-to-all-start = ((bf16[8,432,256]{2,1,0:T(8,128)(2,1)}), bf16[8,432,256]{2,1,0:T(8,128)(2,1)S(1)}, u32[]{:S(2)}, u32[]{:S(2)}) async-start(bf16[8,432,256]{2,1,0:T(8,128)(2,1)} %get-tuple-element.37), calls=%async_computation | async-start | bytes 3538944 | tf_op jit(solution)/shard_map/all_to_all | solution.py:291
  14.6 2.3 %collective-permute-start = (bf16[64,256]{1,0:T(8,128)(2,1)S(1)}, bf16[64,256]{1,0:T(8,128)(2,1)S(1)}, u32[]{:S(2)}, u32[]{:S(2)}) collective-permute-start(bf16[64,256]{1,0:T(8,128)(2,1)S(1)} %copy-done.13), channel_id=1, source_target_pairs={{0,1},{1,2},{2,3},{3,4},{4,5},{5,6},{6,7},{7,0},{8,9},{9,10},{10,1... | collective-permute-start | bytes 98312 | tf_op jit(solution)/shard_map/ppermute | solution.py:293
  16.9 1.2 %collective-permute-start.1 = (bf16[64,256]{1,0:T(8,128)(2,1)S(1)}, bf16[64,256]{1,0:T(8,128)(2,1)S(1)}, u32[]{:S(2)}, u32[]{:S(2)}) collective-permute-start(bf16[64,256]{1,0:T(8,128)(2,1)S(1)} %copy-done.12), channel_id=1, source_target_pairs={{0,2},{1,3},{2,4},{3,5},{4,6},{5,7},{6,0},{7,1},{8,10},{9,11},{10,... | collective-permute-start | bytes 98312 | tf_op jit(solution)/shard_map/ppermute | solution.py:293
  18.1 1.6 %collective-permute-start.2 = (bf16[64,256]{1,0:T(8,128)(2,1)S(1)}, bf16[64,256]{1,0:T(8,128)(2,1)S(1)}, u32[]{:S(2)}, u32[]{:S(2)}) collective-permute-start(bf16[64,256]{1,0:T(8,128)(2,1)S(1)} %copy-done.11), channel_id=1, source_target_pairs={{0,3},{1,4},{2,5},{3,6},{4,7},{5,0},{6,1},{7,2},{8,11},{9,12},{10,... | collective-permute-start | bytes 98312 | tf_op jit(solution)/shard_map/ppermute | solution.py:293
  19.8 0.5 collective-permute-start.3
  20.3 1.9 %collective-permute-start.4 = (bf16[64,256]{1,0:T(8,128)(2,1)S(1)}, bf16[64,256]{1,0:T(8,128)(2,1)S(1)}, u32[]{:S(2)}, u32[]{:S(2)}) collective-permute-start(bf16[64,256]{1,0:T(8,128)(2,1)S(1)} %copy-done.9), channel_id=1, source_target_pairs={{0,5},{1,6},{2,7},{3,0},{4,1},{5,2},{6,3},{7,4},{8,13},{9,14},{10,... | collective-permute-start | bytes 98312 | tf_op jit(solution)/shard_map/ppermute | solution.py:293
  22.2 0.7 collective-permute-start.5
  22.9 1.7 %collective-permute-start.6 = (bf16[64,256]{1,0:T(8,128)(2,1)S(1)}, bf16[64,256]{1,0:T(8,128)(2,1)S(1)}, u32[]{:S(2)}, u32[]{:S(2)}) collective-permute-start(bf16[64,256]{1,0:T(8,128)(2,1)S(1)} %copy-done.7), channel_id=1, source_target_pairs={{0,7},{1,0},{2,1},{3,2},{4,3},{5,4},{6,5},{7,6},{8,15},{9,8},{10,9... | collective-permute-start | bytes 98312 | tf_op jit(solution)/shard_map/ppermute | solution.py:293
  24.6 3.0 %setup.1 = (f32[16,128]{1,0:T(8,128)S(1)}, bf16[432,128]{1,0:T(8,128)(2,1)S(1)}, f32[8,256]{1,0:T(8,128)S(1)}) custom-call(f32[7]{0:T(128)S(1)} %copy-done.5, f32[7]{0:T(128)S(1)} %copy-done.6, f32[8,16,16]{2,1,0:T(8,128)S(1)} %copy-done.1, f32[8,16,16]{2,1,0:T(8,128)S(1)} %copy-done.1, s32[4,256]{1,0:T(4,128)S(1)} %copy-done.3, f32[4,256]{1,0:T(4,128)S(1)} %copy-done.4), custom_call_target="tpu_custom_call" | custom-call | tf_op jit(solution)/shard_map/setup/pallas_call | solution.py:297
  27.7 1.3 %solve.1 = (bf16[8,64,256]{2,1,0:T(8,128)(2,1)S(1)}, f32[8,256]{1,0:T(8,128)S(1)}) custom-call(f32[16,128]{1,0:T(8,128)S(1)} %get-tuple-element.26.needed, f32[8,256]{1,0:T(8,128)S(1)} %get-tuple-element.27.meta, bf16[64,256]{1,0:T(8,128)(2,1)S(1)} %copy-done.2, bf16[64,256]{1,0:T(8,128)(2,1)S(1)} %collective-permute-done.refs_1_, ...), custom_call_target="tpu_custom_call" | custom-call | tf_op jit(solution)/shard_map/solve/pallas_call | solution.py:317
  29.0 5.2 %collective-permute-start.8 = (f32[8,256]{1,0:T(8,128)S(1)}, f32[8,256]{1,0:T(8,128)S(1)}, u32[]{:S(2)}, u32[]{:S(2)}) collective-permute-start(f32[8,256]{1,0:T(8,128)S(1)} %get-tuple-element.36), channel_id=1, source_target_pairs={{192,0},{200,8},{208,16},{216,24},{128,32},{136,40},{144,48},{152,... | collective-permute-start | bytes 24584 | tf_op jit(solution)/shard_map/ppermute | solution.py:329
  34.2 1.2 %collective-permute-start.7 = (f32[8,256]{1,0:T(8,128)S(1)}, f32[8,256]{1,0:T(8,128)S(1)}, u32[]{:S(2)}, u32[]{:S(2)}) collective-permute-start(f32[8,256]{1,0:T(8,128)S(1)} %get-tuple-element.36), channel_id=1, source_target_pairs={{224,0},{232,8},{240,16},{248,24},{160,32},{168,40},{176,48},{184,... | collective-permute-start | bytes 24584 | tf_op jit(solution)/shard_map/ppermute | solution.py:329
  35.4 5.4 %collective-permute-done.7.first_meta = f32[8,256]{1,0:T(8,128)S(1)} collective-permute-done((f32[8,256]{1,0:T(8,128)S(1)}, f32[8,256]{1,0:T(8,128)S(1)}, u32[]{:S(2)}, u32[]{:S(2)}) %collective-permute-start.7) | collective-permute-done | bytes 8224 | tf_op jit(solution)/shard_map/ppermute | solution.py:329
  40.8 2.5 %partial.1 = (bf16[432,256]{1,0:T(8,128)(2,1)S(1)}, bf16[432,256]{1,0:T(8,128)(2,1)S(1)}, bf16[8,192,256]{2,1,0:T(8,128)(2,1)}) custom-call(f32[8,256]{1,0:T(8,128)S(1)} %collective-permute-done.7.first_meta, f32[8,256]{1,0:T(8,128)S(1)} %collective-permute-done.8.second_meta, bf16[8,432,256]{2,1,0:T(8,128)(2,1)S(1)} %all-to-all-done.lists, ...), custom_call_target="tpu_custom_call" | custom-call | tf_op jit(solution)/shard_map/partial/pallas_call | solution.py:330
  43.2 5.4 %all-to-all-start.1 = ((bf16[8,192,256]{2,1,0:T(8,128)(2,1)}), bf16[8,192,256]{2,1,0:T(8,128)(2,1)S(1)}, u32[]{:S(2)}, u32[]{:S(2)}) async-start(bf16[8,192,256]{2,1,0:T(8,128)(2,1)} %get-tuple-element.39), calls=%async_computation.1 | async-start | bytes 1572864 | tf_op jit(solution)/shard_map/all_to_all | solution.py:343
  48.6 1.9 %collective-permute-start.9 = (bf16[432,256]{1,0:T(8,128)(2,1)S(1)}, bf16[432,256]{1,0:T(8,128)(2,1)S(1)}, u32[]{:S(2)}, u32[]{:S(2)}) collective-permute-start(bf16[432,256]{1,0:T(8,128)(2,1)S(1)} %get-tuple-element.41), channel_id=1, source_target_pairs={{0,224},{8,232},{16,240},{24,248},{32,160},{40,168},{48,176},{56,1... | collective-permute-start | bytes 663560 | tf_op jit(solution)/shard_map/ppermute | solution.py:344
  50.6 0.6 collective-permute-start.10
  51.2 9.7 %all-to-all-done.1.shared = bf16[8,192,256]{2,1,0:T(8,128)(2,1)S(1)} async-done(((bf16[8,192,256]{2,1,0:T(8,128)(2,1)}), bf16[8,192,256]{2,1,0:T(8,128)(2,1)S(1)}, u32[]{:S(2)}, u32[]{:S(2)}) %all-to-all-start.1) | async-done | bytes 786464 | tf_op jit(solution)/shard_map/all_to_all | solution.py:343
  60.9 0.9 %own.1 = (bf16[64,256]{1,0:T(8,128)(2,1)S(1)}, bf16[64,256]{1,0:T(8,128)(2,1)S(1)}) custom-call(f32[16,128]{1,0:T(8,128)S(1)} %get-tuple-element.26.needed, bf16[8,192,256]{2,1,0:T(8,128)(2,1)S(1)} %all-to-all-done.1.shared), custom_call_target="tpu_custom_call" | custom-call | tf_op jit(solution)/shard_map/own/pallas_call | solution.py:346
  61.8 2.0 %collective-permute-start.11 = (bf16[64,256]{1,0:T(8,128)(2,1)S(1)}, bf16[64,256]{1,0:T(8,128)(2,1)S(1)}, u32[]{:S(2)}, u32[]{:S(2)}) collective-permute-start(bf16[64,256]{1,0:T(8,128)(2,1)S(1)} %get-tuple-element.43), channel_id=1, source_target_pairs={{0,224},{8,232},{16,240},{24,248},{32,160},{40,168},{48,176},{56,1... | collective-permute-start | bytes 98312 | tf_op jit(solution)/shard_map/ppermute | solution.py:354
  63.8 0.6 collective-permute-start.12
  64.5 2.0 %copy-done = f32[432,2048]{1,0:T(8,128)S(1)} copy-done((f32[432,2048]{1,0:T(8,128)S(1)}, f32[432,2048]{1,0:T(8,128)}, u32[]{:S(2)}) %copy-start) | copy-done | bytes 3538968
  66.5 2.5 %finish.1.whole = bf16[432,2048]{1,0:T(8,128)(2,1)} custom-call(f32[432,2048]{1,0:T(8,128)S(1)} %copy-done, bf16[8,192,256]{2,1,0:T(8,128)(2,1)S(1)} %all-to-all-done.1.shared, bf16[432,128]{1,0:T(8,128)(2,1)S(1)} %get-tuple-element.40.spikes), custom_call_target="tpu_custom_call" | custom-call | tf_op jit(solution)/shard_map/finish/pallas_call | solution.py:356
  69.0 2.2 %collective-permute-done.10.second = bf16[432,256]{1,0:T(8,128)(2,1)S(1)} collective-permute-done((bf16[432,256]{1,0:T(8,128)(2,1)S(1)}, bf16[432,256]{1,0:T(8,128)(2,1)S(1)}, u32[]{:S(2)}, u32[]{:S(2)}) %collective-permute-start.10) | collective-permute-done | bytes 221216 | tf_op jit(solution)/shard_map/ppermute | solution.py:344
  71.2 1.1 %collective-permute-done.12.second_coupled = bf16[64,256]{1,0:T(8,128)(2,1)S(1)} collective-permute-done((bf16[64,256]{1,0:T(8,128)(2,1)S(1)}, bf16[64,256]{1,0:T(8,128)(2,1)S(1)}, u32[]{:S(2)}, u32[]{:S(2)}) %collective-permute-start.12) | collective-permute-done | bytes 32800 | tf_op jit(solution)/shard_map/ppermute | solution.py:354
  72.4 1.0 %ghosts.1 = bf16[432,2048]{1,0:T(8,128)(2,1)} custom-call(bf16[432,2048]{1,0:T(8,128)(2,1)} %finish.1.whole, bf16[432,256]{1,0:T(8,128)(2,1)S(1)} %collective-permute-done.9.first, bf16[432,256]{1,0:T(8,128)(2,1)S(1)} %collective-permute-done.10.second, bf16[64,256]{1,0:T(8,128)(2,1)S(1)} %collective-permute-done.11.first_coupled, ...), custom_call_target="tpu_custom_call", output_to_operand_aliasing={{}: (0, {})} | custom-call | tf_op jit(solution)/shard_map/ghosts/pallas_call | solution.py:370
  (33 shorter events, 0.1 us)
Async XLA Ops:
  8.9 5.7 %copy-start.13 = (bf16[64,256]{1,0:T(8,128)(2,1)S(1)}, bf16[64,256]{1,0:T(8,128)(2,1)}, u32[]{:S(2)}) copy-start(bf16[64,256]{1,0:T(8,128)(2,1)} %get-tuple-element.29) | copy-start | bytes 98308
  8.9 8.0 %copy-start.12 = (bf16[64,256]{1,0:T(8,128)(2,1)S(1)}, bf16[64,256]{1,0:T(8,128)(2,1)}, u32[]{:S(2)}) copy-start(bf16[64,256]{1,0:T(8,128)(2,1)} %get-tuple-element.30) | copy-start | bytes 98308
  9.0 9.2 %copy-start.11 = (bf16[64,256]{1,0:T(8,128)(2,1)S(1)}, bf16[64,256]{1,0:T(8,128)(2,1)}, u32[]{:S(2)}) copy-start(bf16[64,256]{1,0:T(8,128)(2,1)} %get-tuple-element.31) | copy-start | bytes 98308
  9.0 10.8 %copy-start.10 = (bf16[64,256]{1,0:T(8,128)(2,1)S(1)}, bf16[64,256]{1,0:T(8,128)(2,1)}, u32[]{:S(2)}) copy-start(bf16[64,256]{1,0:T(8,128)(2,1)} %get-tuple-element.32) | copy-start | bytes 98308
  9.0 11.3 %copy-start.9 = (bf16[64,256]{1,0:T(8,128)(2,1)S(1)}, bf16[64,256]{1,0:T(8,128)(2,1)}, u32[]{:S(2)}) copy-start(bf16[64,256]{1,0:T(8,128)(2,1)} %get-tuple-element.33) | copy-start | bytes 98308
  9.0 13.2 %copy-start.8 = (bf16[64,256]{1,0:T(8,128)(2,1)S(1)}, bf16[64,256]{1,0:T(8,128)(2,1)}, u32[]{:S(2)}) copy-start(bf16[64,256]{1,0:T(8,128)(2,1)} %get-tuple-element.34) | copy-start | bytes 98308
  9.0 13.9 %copy-start.7 = (bf16[64,256]{1,0:T(8,128)(2,1)S(1)}, bf16[64,256]{1,0:T(8,128)(2,1)}, u32[]{:S(2)}) copy-start(bf16[64,256]{1,0:T(8,128)(2,1)} %get-tuple-element.35) | copy-start | bytes 98308
  9.0 15.6 %copy-start.1 = (f32[8,16,16]{2,1,0:T(8,128)S(1)}, f32[8,16,16]{2,1,0:T(8,128)}, u32[]{:S(2)}) copy-start(f32[8,16,16]{2,1,0:T(8,128)} %block_inverse.1) | copy-start | bytes 24580
  9.0 15.6 %copy-start.3 = (s32[4,256]{1,0:T(4,128)S(1)}, s32[4,256]{1,0:T(4,128)}, u32[]{:S(2)}) copy-start(s32[4,256]{1,0:T(4,128)} %slots.1) | copy-start | bytes 12292
  9.0 15.5 %copy-start.4 = (f32[4,256]{1,0:T(4,128)S(1)}, f32[4,256]{1,0:T(4,128)}, u32[]{:S(2)}) copy-start(f32[4,256]{1,0:T(4,128)} %factors.1) | copy-start | bytes 12292
  9.0 15.5 %copy-start.5 = (f32[7]{0:T(128)S(1)}, f32[7]{0:T(128)}, u32[]{:S(2)}) copy-start(f32[7]{0:T(128)} %lower.1) | copy-start | bytes 88
  9.1 15.5 %copy-start.6 = (f32[7]{0:T(128)S(1)}, f32[7]{0:T(128)}, u32[]{:S(2)}) copy-start(f32[7]{0:T(128)} %upper.1) | copy-start | bytes 88
  9.1 18.6 %copy-start.2 = (bf16[64,256]{1,0:T(8,128)(2,1)S(1)}, bf16[64,256]{1,0:T(8,128)(2,1)}, u32[]{:S(2)}) copy-start(bf16[64,256]{1,0:T(8,128)(2,1)} %get-tuple-element.28.refs_0_) | copy-start | bytes 98308
  9.1 31.7 %all-to-all-start = ((bf16[8,432,256]{2,1,0:T(8,128)(2,1)}), bf16[8,432,256]{2,1,0:T(8,128)(2,1)S(1)}, u32[]{:S(2)}, u32[]{:S(2)}) async-start(bf16[8,432,256]{2,1,0:T(8,128)(2,1)} %get-tuple-element.37), calls=%async_computation | async-start | bytes 3538944 | tf_op jit(solution)/shard_map/all_to_all | solution.py:291
  14.6 7.6 %collective-permute-start = (bf16[64,256]{1,0:T(8,128)(2,1)S(1)}, bf16[64,256]{1,0:T(8,128)(2,1)S(1)}, u32[]{:S(2)}, u32[]{:S(2)}) collective-permute-start(bf16[64,256]{1,0:T(8,128)(2,1)S(1)} %copy-done.13), channel_id=1, source_target_pairs={{0,1},{1,2},{2,3},{3,4},{4,5},{5,6},{6,7},{7,0},{8,9},{9,10},{10,1... | collective-permute-start | bytes 98312 | tf_op jit(solution)/shard_map/ppermute | solution.py:293
  16.9 6.0 %collective-permute-start.1 = (bf16[64,256]{1,0:T(8,128)(2,1)S(1)}, bf16[64,256]{1,0:T(8,128)(2,1)S(1)}, u32[]{:S(2)}, u32[]{:S(2)}) collective-permute-start(bf16[64,256]{1,0:T(8,128)(2,1)S(1)} %copy-done.12), channel_id=1, source_target_pairs={{0,2},{1,3},{2,4},{3,5},{4,6},{5,7},{6,0},{7,1},{8,10},{9,11},{10,... | collective-permute-start | bytes 98312 | tf_op jit(solution)/shard_map/ppermute | solution.py:293
  18.1 9.5 %collective-permute-start.2 = (bf16[64,256]{1,0:T(8,128)(2,1)S(1)}, bf16[64,256]{1,0:T(8,128)(2,1)S(1)}, u32[]{:S(2)}, u32[]{:S(2)}) collective-permute-start(bf16[64,256]{1,0:T(8,128)(2,1)S(1)} %copy-done.11), channel_id=1, source_target_pairs={{0,3},{1,4},{2,5},{3,6},{4,7},{5,0},{6,1},{7,2},{8,11},{9,12},{10,... | collective-permute-start | bytes 98312 | tf_op jit(solution)/shard_map/ppermute | solution.py:293
  19.8 7.9 %collective-permute-start.3 = (bf16[64,256]{1,0:T(8,128)(2,1)S(1)}, bf16[64,256]{1,0:T(8,128)(2,1)S(1)}, u32[]{:S(2)}, u32[]{:S(2)}) collective-permute-start(bf16[64,256]{1,0:T(8,128)(2,1)S(1)} %copy-done.10), channel_id=1, source_target_pairs={{0,4},{1,5},{2,6},{3,7},{4,0},{5,1},{6,2},{7,3},{8,12},{9,13},{10,... | collective-permute-start | bytes 98312 | tf_op jit(solution)/shard_map/ppermute | solution.py:293
  20.3 7.4 %collective-permute-start.4 = (bf16[64,256]{1,0:T(8,128)(2,1)S(1)}, bf16[64,256]{1,0:T(8,128)(2,1)S(1)}, u32[]{:S(2)}, u32[]{:S(2)}) collective-permute-start(bf16[64,256]{1,0:T(8,128)(2,1)S(1)} %copy-done.9), channel_id=1, source_target_pairs={{0,5},{1,6},{2,7},{3,0},{4,1},{5,2},{6,3},{7,4},{8,13},{9,14},{10,... | collective-permute-start | bytes 98312 | tf_op jit(solution)/shard_map/ppermute | solution.py:293
  22.2 5.4 %collective-permute-start.5 = (bf16[64,256]{1,0:T(8,128)(2,1)S(1)}, bf16[64,256]{1,0:T(8,128)(2,1)S(1)}, u32[]{:S(2)}, u32[]{:S(2)}) collective-permute-start(bf16[64,256]{1,0:T(8,128)(2,1)S(1)} %copy-done.8), channel_id=1, source_target_pairs={{0,6},{1,7},{2,0},{3,1},{4,2},{5,3},{6,4},{7,5},{8,14},{9,15},{10,... | collective-permute-start | bytes 98312 | tf_op jit(solution)/shard_map/ppermute | solution.py:293
  22.9 4.8 %collective-permute-start.6 = (bf16[64,256]{1,0:T(8,128)(2,1)S(1)}, bf16[64,256]{1,0:T(8,128)(2,1)S(1)}, u32[]{:S(2)}, u32[]{:S(2)}) collective-permute-start(bf16[64,256]{1,0:T(8,128)(2,1)S(1)} %copy-done.7), channel_id=1, source_target_pairs={{0,7},{1,0},{2,1},{3,2},{4,3},{5,4},{6,5},{7,6},{8,15},{9,8},{10,9... | collective-permute-start | bytes 98312 | tf_op jit(solution)/shard_map/ppermute | solution.py:293
  29.0 6.4 %collective-permute-start.8 = (f32[8,256]{1,0:T(8,128)S(1)}, f32[8,256]{1,0:T(8,128)S(1)}, u32[]{:S(2)}, u32[]{:S(2)}) collective-permute-start(f32[8,256]{1,0:T(8,128)S(1)} %get-tuple-element.36), channel_id=1, source_target_pairs={{192,0},{200,8},{208,16},{216,24},{128,32},{136,40},{144,48},{152,... | collective-permute-start | bytes 24584 | tf_op jit(solution)/shard_map/ppermute | solution.py:329
  34.2 6.6 %collective-permute-start.7 = (f32[8,256]{1,0:T(8,128)S(1)}, f32[8,256]{1,0:T(8,128)S(1)}, u32[]{:S(2)}, u32[]{:S(2)}) collective-permute-start(f32[8,256]{1,0:T(8,128)S(1)} %get-tuple-element.36), channel_id=1, source_target_pairs={{224,0},{232,8},{240,16},{248,24},{160,32},{168,40},{176,48},{184,... | collective-permute-start | bytes 24584 | tf_op jit(solution)/shard_map/ppermute | solution.py:329
  43.2 17.7 %all-to-all-start.1 = ((bf16[8,192,256]{2,1,0:T(8,128)(2,1)}), bf16[8,192,256]{2,1,0:T(8,128)(2,1)S(1)}, u32[]{:S(2)}, u32[]{:S(2)}) async-start(bf16[8,192,256]{2,1,0:T(8,128)(2,1)} %get-tuple-element.39), calls=%async_computation.1 | async-start | bytes 1572864 | tf_op jit(solution)/shard_map/all_to_all | solution.py:343
  48.6 20.4 %collective-permute-start.9 = (bf16[432,256]{1,0:T(8,128)(2,1)S(1)}, bf16[432,256]{1,0:T(8,128)(2,1)S(1)}, u32[]{:S(2)}, u32[]{:S(2)}) collective-permute-start(bf16[432,256]{1,0:T(8,128)(2,1)S(1)} %get-tuple-element.41), channel_id=1, source_target_pairs={{0,224},{8,232},{16,240},{24,248},{32,160},{40,168},{48,176},{56,1... | collective-permute-start | bytes 663560 | tf_op jit(solution)/shard_map/ppermute | solution.py:344
  50.6 20.7 %collective-permute-start.10 = (bf16[432,256]{1,0:T(8,128)(2,1)S(1)}, bf16[432,256]{1,0:T(8,128)(2,1)S(1)}, u32[]{:S(2)}, u32[]{:S(2)}) collective-permute-start(bf16[432,256]{1,0:T(8,128)(2,1)S(1)} %get-tuple-element.42), channel_id=1, source_target_pairs={{0,192},{8,200},{16,208},{24,216},{32,128},{40,136},{48,144},{56,1... | collective-permute-start | bytes 663560 | tf_op jit(solution)/shard_map/ppermute | solution.py:344
  61.8 9.5 %collective-permute-start.11 = (bf16[64,256]{1,0:T(8,128)(2,1)S(1)}, bf16[64,256]{1,0:T(8,128)(2,1)S(1)}, u32[]{:S(2)}, u32[]{:S(2)}) collective-permute-start(bf16[64,256]{1,0:T(8,128)(2,1)S(1)} %get-tuple-element.43), channel_id=1, source_target_pairs={{0,224},{8,232},{16,240},{24,248},{32,160},{40,168},{48,176},{56,1... | collective-permute-start | bytes 98312 | tf_op jit(solution)/shard_map/ppermute | solution.py:354
  63.8 8.5 %collective-permute-start.12 = (bf16[64,256]{1,0:T(8,128)(2,1)S(1)}, bf16[64,256]{1,0:T(8,128)(2,1)S(1)}, u32[]{:S(2)}, u32[]{:S(2)}) collective-permute-start(bf16[64,256]{1,0:T(8,128)(2,1)S(1)} %get-tuple-element.44), channel_id=1, source_target_pairs={{0,192},{8,200},{16,208},{24,216},{32,128},{40,136},{48,144},{56,1... | collective-permute-start | bytes 98312 | tf_op jit(solution)/shard_map/ppermute | solution.py:354
  64.5 2.0 %copy-start = (f32[432,2048]{1,0:T(8,128)S(1)}, f32[432,2048]{1,0:T(8,128)}, u32[]{:S(2)}) copy-start(f32[432,2048]{1,0:T(8,128)} %get-tuple-element.25.spread) | copy-start | bytes 10616836

commit v6 on v5

--- a/solution.py
+++ b/solution.py
@@ -24,7 +24,7 @@
 EDGE = 64
 GROUP = 8
 
-SERVES = ((3, 1, 2, 0), (2, 0, 3, 1))
+SERVES = ((3, 2, 1, 0), (1, 0, 3, 2))
 
 
 def params(mebibytes):
@@ -110,7 +110,7 @@
     panel, half = row // 4, (row // 2) % 2
     for r in range(GROUP):
         member, y = r // 4, r % 4
-        served = (3 - 2 * member - half, 2 - 2 * member + half)
+        served = (3 - 2 * half - member, 2 * half + 1 - member)
         wanted = []
         for m in range(2):
             tile = (4 * (1 - panel) + served[m]) * 4 + y

time: 74.6 us -> 74.3 us (level)
    ppermute x2, waiting for transfers between devices: 5.4 us -> 3.96 us  [shards(): metas = [lax.ppermute(meta, 'ang', crossing(m, True)) for m in range(2)]]
    ppermute x4, waiting for transfers between devices: 3.36 us -> 4.53 us  [shards(): lax.ppermute(value, 'ang', crossing(m, False))]
where the time goes in v6:
time: 74.3 us; the launch traced here: 73.2 us
  starting transfers between devices  32.6 us (44%)
  Pallas kernels  20.1 us (27%)
  waiting for transfers between devices  18.3 us (25%)
  local copies, waits for them, and re-layouts  2.07 us (3%)
    ppermute x7, starting transfers between devices, shards(): lax.ppermute(chunks[shift], 'rad', [(k, (k + shift) % BLOCKS) for k in ra...  9.95 us
    all_to_all x1, waiting for transfers between devices, shards(): shared = lax.all_to_all(shared, 'rad', 0, 0)  9.8 us
    pallas_call x1, Pallas kernels, shards(): pl.pallas_call(head_kernel, in_specs=[SMEM] + [ANY] * 4, out_specs=[ANY]...  8.93 us
    ppermute x2, starting transfers between devices, shards(): metas = [lax.ppermute(meta, 'ang', crossing(m, True)) for m in range(2)]  6.37 us
    all_to_all x1, starting transfers between devices, shards(): shared = lax.all_to_all(shared, 'rad', 0, 0)  5.65 us
    all_to_all x1, starting transfers between devices, shards(): donors = lax.all_to_all(lists, 'ang', 0, 0, axis_index_groups=groups)  5.51 us
    ppermute x4, starting transfers between devices, shards(): lax.ppermute(value, 'ang', crossing(m, False))  5.07 us
    ppermute x4, waiting for transfers between devices, shards(): lax.ppermute(value, 'ang', crossing(m, False))  4.53 us
  transfers between devices with their start and end apart: 15, of which 4 were waited for; matrix products, arithmetic and copies ran while one was open for 0% of the time, Pallas kernels for 11%

profile of v6, /device:TPU:33, one launch (start us, length us, event | category | flops | bytes accessed | tf_op | source)
XLA Modules:
  0.0 73.2 jit_solution(11329423544808223278)
XLA Ops:
  0.0 8.9 %head.1 = (f32[432,2048]{1,0:T(8,128)}, bf16[8,432,256]{2,1,0:T(8,128)(2,1)}, bf16[64,256]{1,0:T(8,128)(2,1)}, bf16[64,256]{1,0:T(8,128)(2,1)}, bf16[64,256]{1,0...) custom-call(s32[1,32]{1,0:T(1,128)} %block_size.1, ...), custom_call_target="tpu_custom_call" | custom-call | tf_op jit(solution)/shard_map/head/pallas_call | solution.py:266
  9.0 0.0 copy-start.1
  9.0 0.0 copy-start.3
  9.0 0.0 copy-start.4
  9.0 0.0 copy-start.5
  9.1 0.0 copy-start.6
  9.1 5.5 %all-to-all-start = ((bf16[8,432,256]{2,1,0:T(8,128)(2,1)}), bf16[8,432,256]{2,1,0:T(8,128)(2,1)S(1)}, u32[]{:S(2)}, u32[]{:S(2)}) async-start(bf16[8,432,256]{2,1,0:T(8,128)(2,1)} %get-tuple-element.37), calls=%async_computation | async-start | bytes 3538944 | tf_op jit(solution)/shard_map/all_to_all | solution.py:291
  14.6 2.3 %collective-permute-start = (bf16[64,256]{1,0:T(8,128)(2,1)S(1)}, bf16[64,256]{1,0:T(8,128)(2,1)S(1)}, u32[]{:S(2)}, u32[]{:S(2)}) collective-permute-start(bf16[64,256]{1,0:T(8,128)(2,1)S(1)} %copy-done.13), channel_id=1, source_target_pairs={{0,1},{1,2},{2,3},{3,4},{4,5},{5,6},{6,7},{7,0},{8,9},{9,10},{10,1... | collective-permute-start | bytes 98312 | tf_op jit(solution)/shard_map/ppermute | solution.py:293
  16.9 1.2 %collective-permute-start.1 = (bf16[64,256]{1,0:T(8,128)(2,1)S(1)}, bf16[64,256]{1,0:T(8,128)(2,1)S(1)}, u32[]{:S(2)}, u32[]{:S(2)}) collective-permute-start(bf16[64,256]{1,0:T(8,128)(2,1)S(1)} %copy-done.12), channel_id=1, source_target_pairs={{0,2},{1,3},{2,4},{3,5},{4,6},{5,7},{6,0},{7,1},{8,10},{9,11},{10,... | collective-permute-start | bytes 98312 | tf_op jit(solution)/shard_map/ppermute | solution.py:293
  18.1 1.6 %collective-permute-start.2 = (bf16[64,256]{1,0:T(8,128)(2,1)S(1)}, bf16[64,256]{1,0:T(8,128)(2,1)S(1)}, u32[]{:S(2)}, u32[]{:S(2)}) collective-permute-start(bf16[64,256]{1,0:T(8,128)(2,1)S(1)} %copy-done.11), channel_id=1, source_target_pairs={{0,3},{1,4},{2,5},{3,6},{4,7},{5,0},{6,1},{7,2},{8,11},{9,12},{10,... | collective-permute-start | bytes 98312 | tf_op jit(solution)/shard_map/ppermute | solution.py:293
  19.8 0.5 collective-permute-start.3
  20.3 1.9 %collective-permute-start.4 = (bf16[64,256]{1,0:T(8,128)(2,1)S(1)}, bf16[64,256]{1,0:T(8,128)(2,1)S(1)}, u32[]{:S(2)}, u32[]{:S(2)}) collective-permute-start(bf16[64,256]{1,0:T(8,128)(2,1)S(1)} %copy-done.9), channel_id=1, source_target_pairs={{0,5},{1,6},{2,7},{3,0},{4,1},{5,2},{6,3},{7,4},{8,13},{9,14},{10,... | collective-permute-start | bytes 98312 | tf_op jit(solution)/shard_map/ppermute | solution.py:293
  22.2 0.7 collective-permute-start.5
  22.9 1.7 %collective-permute-start.6 = (bf16[64,256]{1,0:T(8,128)(2,1)S(1)}, bf16[64,256]{1,0:T(8,128)(2,1)S(1)}, u32[]{:S(2)}, u32[]{:S(2)}) collective-permute-start(bf16[64,256]{1,0:T(8,128)(2,1)S(1)} %copy-done.7), channel_id=1, source_target_pairs={{0,7},{1,0},{2,1},{3,2},{4,3},{5,4},{6,5},{7,6},{8,15},{9,8},{10,9... | collective-permute-start | bytes 98312 | tf_op jit(solution)/shard_map/ppermute | solution.py:293
  24.6 3.0 %setup.1 = (f32[16,128]{1,0:T(8,128)S(1)}, bf16[432,128]{1,0:T(8,128)(2,1)S(1)}, f32[8,256]{1,0:T(8,128)S(1)}) custom-call(f32[7]{0:T(128)S(1)} %copy-done.5, f32[7]{0:T(128)S(1)} %copy-done.6, f32[8,16,16]{2,1,0:T(8,128)S(1)} %copy-done.1, f32[8,16,16]{2,1,0:T(8,128)S(1)} %copy-done.1, s32[4,256]{1,0:T(4,128)S(1)} %copy-done.3, f32[4,256]{1,0:T(4,128)S(1)} %copy-done.4), custom_call_target="tpu_custom_call" | custom-call | tf_op jit(solution)/shard_map/setup/pallas_call | solution.py:297
  27.7 1.3 %solve.1 = (bf16[8,64,256]{2,1,0:T(8,128)(2,1)S(1)}, f32[8,256]{1,0:T(8,128)S(1)}) custom-call(f32[16,128]{1,0:T(8,128)S(1)} %get-tuple-element.26.needed, f32[8,256]{1,0:T(8,128)S(1)} %get-tuple-element.27.meta, bf16[64,256]{1,0:T(8,128)(2,1)S(1)} %copy-done.2, bf16[64,256]{1,0:T(8,128)(2,1)S(1)} %collective-permute-done.refs_1_, ...), custom_call_target="tpu_custom_call" | custom-call | tf_op jit(solution)/shard_map/solve/pallas_call | solution.py:317
  29.0 4.7 %collective-permute-start.8 = (f32[8,256]{1,0:T(8,128)S(1)}, f32[8,256]{1,0:T(8,128)S(1)}, u32[]{:S(2)}, u32[]{:S(2)}) collective-permute-start(f32[8,256]{1,0:T(8,128)S(1)} %get-tuple-element.36), channel_id=1, source_target_pairs={{160,0},{168,8},{176,16},{184,24},{128,32},{136,40},{144,48},{152,... | collective-permute-start | bytes 24584 | tf_op jit(solution)/shard_map/ppermute | solution.py:329
  33.7 1.7 %collective-permute-start.7 = (f32[8,256]{1,0:T(8,128)S(1)}, f32[8,256]{1,0:T(8,128)S(1)}, u32[]{:S(2)}, u32[]{:S(2)}) collective-permute-start(f32[8,256]{1,0:T(8,128)S(1)} %get-tuple-element.36), channel_id=1, source_target_pairs={{224,0},{232,8},{240,16},{248,24},{192,32},{200,40},{208,48},{216,... | collective-permute-start | bytes 24584 | tf_op jit(solution)/shard_map/ppermute | solution.py:329
  35.4 4.0 %collective-permute-done.7.first_meta = f32[8,256]{1,0:T(8,128)S(1)} collective-permute-done((f32[8,256]{1,0:T(8,128)S(1)}, f32[8,256]{1,0:T(8,128)S(1)}, u32[]{:S(2)}, u32[]{:S(2)}) %collective-permute-start.7) | collective-permute-done | bytes 8224 | tf_op jit(solution)/shard_map/ppermute | solution.py:329
  39.3 2.5 %partial.1 = (bf16[432,256]{1,0:T(8,128)(2,1)S(1)}, bf16[432,256]{1,0:T(8,128)(2,1)S(1)}, bf16[8,192,256]{2,1,0:T(8,128)(2,1)}) custom-call(f32[8,256]{1,0:T(8,128)S(1)} %collective-permute-done.7.first_meta, f32[8,256]{1,0:T(8,128)S(1)} %collective-permute-done.8.second_meta, bf16[8,432,256]{2,1,0:T(8,128)(2,1)S(1)} %all-to-all-done.lists, ...), custom_call_target="tpu_custom_call" | custom-call | tf_op jit(solution)/shard_map/partial/pallas_call | solution.py:330
  41.8 5.7 %all-to-all-start.1 = ((bf16[8,192,256]{2,1,0:T(8,128)(2,1)}), bf16[8,192,256]{2,1,0:T(8,128)(2,1)S(1)}, u32[]{:S(2)}, u32[]{:S(2)}) async-start(bf16[8,192,256]{2,1,0:T(8,128)(2,1)} %get-tuple-element.39), calls=%async_computation.1 | async-start | bytes 1572864 | tf_op jit(solution)/shard_map/all_to_all | solution.py:343
  47.4 2.2 %collective-permute-start.9 = (bf16[432,256]{1,0:T(8,128)(2,1)S(1)}, bf16[432,256]{1,0:T(8,128)(2,1)S(1)}, u32[]{:S(2)}, u32[]{:S(2)}) collective-permute-start(bf16[432,256]{1,0:T(8,128)(2,1)S(1)} %get-tuple-element.41), channel_id=1, source_target_pairs={{0,224},{8,232},{16,240},{24,248},{32,192},{40,200},{48,208},{56,2... | collective-permute-start | bytes 663560 | tf_op jit(solution)/shard_map/ppermute | solution.py:344
  49.7 0.3 collective-permute-start.10
  49.9 9.8 %all-to-all-done.1.shared = bf16[8,192,256]{2,1,0:T(8,128)(2,1)S(1)} async-done(((bf16[8,192,256]{2,1,0:T(8,128)(2,1)}), bf16[8,192,256]{2,1,0:T(8,128)(2,1)S(1)}, u32[]{:S(2)}, u32[]{:S(2)}) %all-to-all-start.1) | async-done | bytes 786464 | tf_op jit(solution)/shard_map/all_to_all | solution.py:343
  59.7 0.9 %own.1 = (bf16[64,256]{1,0:T(8,128)(2,1)S(1)}, bf16[64,256]{1,0:T(8,128)(2,1)S(1)}) custom-call(f32[16,128]{1,0:T(8,128)S(1)} %get-tuple-element.26.needed, bf16[8,192,256]{2,1,0:T(8,128)(2,1)S(1)} %all-to-all-done.1.shared), custom_call_target="tpu_custom_call" | custom-call | tf_op jit(solution)/shard_map/own/pallas_call | solution.py:346
  60.6 2.3 %collective-permute-start.11 = (bf16[64,256]{1,0:T(8,128)(2,1)S(1)}, bf16[64,256]{1,0:T(8,128)(2,1)S(1)}, u32[]{:S(2)}, u32[]{:S(2)}) collective-permute-start(bf16[64,256]{1,0:T(8,128)(2,1)S(1)} %get-tuple-element.43), channel_id=1, source_target_pairs={{0,224},{8,232},{16,240},{24,248},{32,192},{40,200},{48,208},{56,2... | collective-permute-start | bytes 98312 | tf_op jit(solution)/shard_map/ppermute | solution.py:354
  62.9 0.3 collective-permute-start.12
  63.2 2.0 %copy-done = f32[432,2048]{1,0:T(8,128)S(1)} copy-done((f32[432,2048]{1,0:T(8,128)S(1)}, f32[432,2048]{1,0:T(8,128)}, u32[]{:S(2)}) %copy-start) | copy-done | bytes 3538968
  65.2 2.5 %finish.1.whole = bf16[432,2048]{1,0:T(8,128)(2,1)} custom-call(f32[432,2048]{1,0:T(8,128)S(1)} %copy-done, bf16[8,192,256]{2,1,0:T(8,128)(2,1)S(1)} %all-to-all-done.1.shared, bf16[432,128]{1,0:T(8,128)(2,1)S(1)} %get-tuple-element.40.spikes), custom_call_target="tpu_custom_call" | custom-call | tf_op jit(solution)/shard_map/finish/pallas_call | solution.py:356
  67.7 3.4 %collective-permute-done.10.second = bf16[432,256]{1,0:T(8,128)(2,1)S(1)} collective-permute-done((bf16[432,256]{1,0:T(8,128)(2,1)S(1)}, bf16[432,256]{1,0:T(8,128)(2,1)S(1)}, u32[]{:S(2)}, u32[]{:S(2)}) %collective-permute-start.10) | collective-permute-done | bytes 221216 | tf_op jit(solution)/shard_map/ppermute | solution.py:344
  71.1 1.1 %collective-permute-done.12.second_coupled = bf16[64,256]{1,0:T(8,128)(2,1)S(1)} collective-permute-done((bf16[64,256]{1,0:T(8,128)(2,1)S(1)}, bf16[64,256]{1,0:T(8,128)(2,1)S(1)}, u32[]{:S(2)}, u32[]{:S(2)}) %collective-permute-start.12) | collective-permute-done | bytes 32800 | tf_op jit(solution)/shard_map/ppermute | solution.py:354
  72.3 1.0 %ghosts.1 = bf16[432,2048]{1,0:T(8,128)(2,1)} custom-call(bf16[432,2048]{1,0:T(8,128)(2,1)} %finish.1.whole, bf16[432,256]{1,0:T(8,128)(2,1)S(1)} %collective-permute-done.9.first, bf16[432,256]{1,0:T(8,128)(2,1)S(1)} %collective-permute-done.10.second, bf16[64,256]{1,0:T(8,128)(2,1)S(1)} %collective-permute-done.11.first_coupled, ...), custom_call_target="tpu_custom_call", output_to_operand_aliasing={{}: (0, {})} | custom-call | tf_op jit(solution)/shard_map/ghosts/pallas_call | solution.py:370
  (33 shorter events, 0.1 us)
Async XLA Ops:
  8.9 5.7 %copy-start.13 = (bf16[64,256]{1,0:T(8,128)(2,1)S(1)}, bf16[64,256]{1,0:T(8,128)(2,1)}, u32[]{:S(2)}) copy-start(bf16[64,256]{1,0:T(8,128)(2,1)} %get-tuple-element.29) | copy-start | bytes 98308
  8.9 8.0 %copy-start.12 = (bf16[64,256]{1,0:T(8,128)(2,1)S(1)}, bf16[64,256]{1,0:T(8,128)(2,1)}, u32[]{:S(2)}) copy-start(bf16[64,256]{1,0:T(8,128)(2,1)} %get-tuple-element.30) | copy-start | bytes 98308
  9.0 9.2 %copy-start.11 = (bf16[64,256]{1,0:T(8,128)(2,1)S(1)}, bf16[64,256]{1,0:T(8,128)(2,1)}, u32[]{:S(2)}) copy-start(bf16[64,256]{1,0:T(8,128)(2,1)} %get-tuple-element.31) | copy-start | bytes 98308
  9.0 10.8 %copy-start.10 = (bf16[64,256]{1,0:T(8,128)(2,1)S(1)}, bf16[64,256]{1,0:T(8,128)(2,1)}, u32[]{:S(2)}) copy-start(bf16[64,256]{1,0:T(8,128)(2,1)} %get-tuple-element.32) | copy-start | bytes 98308
  9.0 11.3 %copy-start.9 = (bf16[64,256]{1,0:T(8,128)(2,1)S(1)}, bf16[64,256]{1,0:T(8,128)(2,1)}, u32[]{:S(2)}) copy-start(bf16[64,256]{1,0:T(8,128)(2,1)} %get-tuple-element.33) | copy-start | bytes 98308
  9.0 13.2 %copy-start.8 = (bf16[64,256]{1,0:T(8,128)(2,1)S(1)}, bf16[64,256]{1,0:T(8,128)(2,1)}, u32[]{:S(2)}) copy-start(bf16[64,256]{1,0:T(8,128)(2,1)} %get-tuple-element.34) | copy-start | bytes 98308
  9.0 13.9 %copy-start.7 = (bf16[64,256]{1,0:T(8,128)(2,1)S(1)}, bf16[64,256]{1,0:T(8,128)(2,1)}, u32[]{:S(2)}) copy-start(bf16[64,256]{1,0:T(8,128)(2,1)} %get-tuple-element.35) | copy-start | bytes 98308
  9.0 15.6 %copy-start.1 = (f32[8,16,16]{2,1,0:T(8,128)S(1)}, f32[8,16,16]{2,1,0:T(8,128)}, u32[]{:S(2)}) copy-start(f32[8,16,16]{2,1,0:T(8,128)} %block_inverse.1) | copy-start | bytes 24580
  9.0 15.6 %copy-start.3 = (s32[4,256]{1,0:T(4,128)S(1)}, s32[4,256]{1,0:T(4,128)}, u32[]{:S(2)}) copy-start(s32[4,256]{1,0:T(4,128)} %slots.1) | copy-start | bytes 12292
  9.0 15.5 %copy-start.4 = (f32[4,256]{1,0:T(4,128)S(1)}, f32[4,256]{1,0:T(4,128)}, u32[]{:S(2)}) copy-start(f32[4,256]{1,0:T(4,128)} %factors.1) | copy-start | bytes 12292
  9.0 15.5 %copy-start.5 = (f32[7]{0:T(128)S(1)}, f32[7]{0:T(128)}, u32[]{:S(2)}) copy-start(f32[7]{0:T(128)} %lower.1) | copy-start | bytes 88
  9.1 15.5 %copy-start.6 = (f32[7]{0:T(128)S(1)}, f32[7]{0:T(128)}, u32[]{:S(2)}) copy-start(f32[7]{0:T(128)} %upper.1) | copy-start | bytes 88
  9.1 18.6 %copy-start.2 = (bf16[64,256]{1,0:T(8,128)(2,1)S(1)}, bf16[64,256]{1,0:T(8,128)(2,1)}, u32[]{:S(2)}) copy-start(bf16[64,256]{1,0:T(8,128)(2,1)} %get-tuple-element.28.refs_0_) | copy-start | bytes 98308
  9.1 30.2 %all-to-all-start = ((bf16[8,432,256]{2,1,0:T(8,128)(2,1)}), bf16[8,432,256]{2,1,0:T(8,128)(2,1)S(1)}, u32[]{:S(2)}, u32[]{:S(2)}) async-start(bf16[8,432,256]{2,1,0:T(8,128)(2,1)} %get-tuple-element.37), calls=%async_computation | async-start | bytes 3538944 | tf_op jit(solution)/shard_map/all_to_all | solution.py:291
  14.6 7.6 %collective-permute-start = (bf16[64,256]{1,0:T(8,128)(2,1)S(1)}, bf16[64,256]{1,0:T(8,128)(2,1)S(1)}, u32[]{:S(2)}, u32[]{:S(2)}) collective-permute-start(bf16[64,256]{1,0:T(8,128)(2,1)S(1)} %copy-done.13), channel_id=1, source_target_pairs={{0,1},{1,2},{2,3},{3,4},{4,5},{5,6},{6,7},{7,0},{8,9},{9,10},{10,1... | collective-permute-start | bytes 98312 | tf_op jit(solution)/shard_map/ppermute | solution.py:293
  16.9 6.0 %collective-permute-start.1 = (bf16[64,256]{1,0:T(8,128)(2,1)S(1)}, bf16[64,256]{1,0:T(8,128)(2,1)S(1)}, u32[]{:S(2)}, u32[]{:S(2)}) collective-permute-start(bf16[64,256]{1,0:T(8,128)(2,1)S(1)} %copy-done.12), channel_id=1, source_target_pairs={{0,2},{1,3},{2,4},{3,5},{4,6},{5,7},{6,0},{7,1},{8,10},{9,11},{10,... | collective-permute-start | bytes 98312 | tf_op jit(solution)/shard_map/ppermute | solution.py:293
  18.1 9.5 %collective-permute-start.2 = (bf16[64,256]{1,0:T(8,128)(2,1)S(1)}, bf16[64,256]{1,0:T(8,128)(2,1)S(1)}, u32[]{:S(2)}, u32[]{:S(2)}) collective-permute-start(bf16[64,256]{1,0:T(8,128)(2,1)S(1)} %copy-done.11), channel_id=1, source_target_pairs={{0,3},{1,4},{2,5},{3,6},{4,7},{5,0},{6,1},{7,2},{8,11},{9,12},{10,... | collective-permute-start | bytes 98312 | tf_op jit(solution)/shard_map/ppermute | solution.py:293
  19.8 7.9 %collective-permute-start.3 = (bf16[64,256]{1,0:T(8,128)(2,1)S(1)}, bf16[64,256]{1,0:T(8,128)(2,1)S(1)}, u32[]{:S(2)}, u32[]{:S(2)}) collective-permute-start(bf16[64,256]{1,0:T(8,128)(2,1)S(1)} %copy-done.10), channel_id=1, source_target_pairs={{0,4},{1,5},{2,6},{3,7},{4,0},{5,1},{6,2},{7,3},{8,12},{9,13},{10,... | collective-permute-start | bytes 98312 | tf_op jit(solution)/shard_map/ppermute | solution.py:293
  20.3 7.4 %collective-permute-start.4 = (bf16[64,256]{1,0:T(8,128)(2,1)S(1)}, bf16[64,256]{1,0:T(8,128)(2,1)S(1)}, u32[]{:S(2)}, u32[]{:S(2)}) collective-permute-start(bf16[64,256]{1,0:T(8,128)(2,1)S(1)} %copy-done.9), channel_id=1, source_target_pairs={{0,5},{1,6},{2,7},{3,0},{4,1},{5,2},{6,3},{7,4},{8,13},{9,14},{10,... | collective-permute-start | bytes 98312 | tf_op jit(solution)/shard_map/ppermute | solution.py:293
  22.2 5.4 %collective-permute-start.5 = (bf16[64,256]{1,0:T(8,128)(2,1)S(1)}, bf16[64,256]{1,0:T(8,128)(2,1)S(1)}, u32[]{:S(2)}, u32[]{:S(2)}) collective-permute-start(bf16[64,256]{1,0:T(8,128)(2,1)S(1)} %copy-done.8), channel_id=1, source_target_pairs={{0,6},{1,7},{2,0},{3,1},{4,2},{5,3},{6,4},{7,5},{8,14},{9,15},{10,... | collective-permute-start | bytes 98312 | tf_op jit(solution)/shard_map/ppermute | solution.py:293
  22.9 4.8 %collective-permute-start.6 = (bf16[64,256]{1,0:T(8,128)(2,1)S(1)}, bf16[64,256]{1,0:T(8,128)(2,1)S(1)}, u32[]{:S(2)}, u32[]{:S(2)}) collective-permute-start(bf16[64,256]{1,0:T(8,128)(2,1)S(1)} %copy-done.7), channel_id=1, source_target_pairs={{0,7},{1,0},{2,1},{3,2},{4,3},{5,4},{6,5},{7,6},{8,15},{9,8},{10,9... | collective-permute-start | bytes 98312 | tf_op jit(solution)/shard_map/ppermute | solution.py:293
  29.0 6.4 %collective-permute-start.8 = (f32[8,256]{1,0:T(8,128)S(1)}, f32[8,256]{1,0:T(8,128)S(1)}, u32[]{:S(2)}, u32[]{:S(2)}) collective-permute-start(f32[8,256]{1,0:T(8,128)S(1)} %get-tuple-element.36), channel_id=1, source_target_pairs={{160,0},{168,8},{176,16},{184,24},{128,32},{136,40},{144,48},{152,... | collective-permute-start | bytes 24584 | tf_op jit(solution)/shard_map/ppermute | solution.py:329
  33.7 5.7 %collective-permute-start.7 = (f32[8,256]{1,0:T(8,128)S(1)}, f32[8,256]{1,0:T(8,128)S(1)}, u32[]{:S(2)}, u32[]{:S(2)}) collective-permute-start(f32[8,256]{1,0:T(8,128)S(1)} %get-tuple-element.36), channel_id=1, source_target_pairs={{224,0},{232,8},{240,16},{248,24},{192,32},{200,40},{208,48},{216,... | collective-permute-start | bytes 24584 | tf_op jit(solution)/shard_map/ppermute | solution.py:329
  41.8 17.9 %all-to-all-start.1 = ((bf16[8,192,256]{2,1,0:T(8,128)(2,1)}), bf16[8,192,256]{2,1,0:T(8,128)(2,1)S(1)}, u32[]{:S(2)}, u32[]{:S(2)}) async-start(bf16[8,192,256]{2,1,0:T(8,128)(2,1)} %get-tuple-element.39), calls=%async_computation.1 | async-start | bytes 1572864 | tf_op jit(solution)/shard_map/all_to_all | solution.py:343
  47.4 20.3 %collective-permute-start.9 = (bf16[432,256]{1,0:T(8,128)(2,1)S(1)}, bf16[432,256]{1,0:T(8,128)(2,1)S(1)}, u32[]{:S(2)}, u32[]{:S(2)}) collective-permute-start(bf16[432,256]{1,0:T(8,128)(2,1)S(1)} %get-tuple-element.41), channel_id=1, source_target_pairs={{0,224},{8,232},{16,240},{24,248},{32,192},{40,200},{48,208},{56,2... | collective-permute-start | bytes 663560 | tf_op jit(solution)/shard_map/ppermute | solution.py:344
  49.7 21.5 %collective-permute-start.10 = (bf16[432,256]{1,0:T(8,128)(2,1)S(1)}, bf16[432,256]{1,0:T(8,128)(2,1)S(1)}, u32[]{:S(2)}, u32[]{:S(2)}) collective-permute-start(bf16[432,256]{1,0:T(8,128)(2,1)S(1)} %get-tuple-element.42), channel_id=1, source_target_pairs={{0,160},{8,168},{16,176},{24,184},{32,128},{40,136},{48,144},{56,1... | collective-permute-start | bytes 663560 | tf_op jit(solution)/shard_map/ppermute | solution.py:344
  60.6 10.5 %collective-permute-start.11 = (bf16[64,256]{1,0:T(8,128)(2,1)S(1)}, bf16[64,256]{1,0:T(8,128)(2,1)S(1)}, u32[]{:S(2)}, u32[]{:S(2)}) collective-permute-start(bf16[64,256]{1,0:T(8,128)(2,1)S(1)} %get-tuple-element.43), channel_id=1, source_target_pairs={{0,224},{8,232},{16,240},{24,248},{32,192},{40,200},{48,208},{56,2... | collective-permute-start | bytes 98312 | tf_op jit(solution)/shard_map/ppermute | solution.py:354
  62.9 9.3 %collective-permute-start.12 = (bf16[64,256]{1,0:T(8,128)(2,1)S(1)}, bf16[64,256]{1,0:T(8,128)(2,1)S(1)}, u32[]{:S(2)}, u32[]{:S(2)}) collective-permute-start(bf16[64,256]{1,0:T(8,128)(2,1)S(1)} %get-tuple-element.44), channel_id=1, source_target_pairs={{0,160},{8,168},{16,176},{24,184},{32,128},{40,136},{48,144},{56,1... | collective-permute-start | bytes 98312 | tf_op jit(solution)/shard_map/ppermute | solution.py:354
  63.2 2.0 %copy-start = (f32[432,2048]{1,0:T(8,128)S(1)}, f32[432,2048]{1,0:T(8,128)}, u32[]{:S(2)}) copy-start(f32[432,2048]{1,0:T(8,128)} %get-tuple-element.25.spread) | copy-start | bytes 10616836

commit v7 on v6

--- a/solution.py
+++ b/solution.py
@@ -212,11 +212,12 @@
 
 
 def finish_kernel(spread, shared, spikes, result):
-    for j in range(2):
+    for j in range(INNER // 256):
         here = slice(256 * j, 256 * (j + 1))
         coupled = shared[j, :EDGE, :]
         correction = dot(spikes[...], jnp.concatenate([coupled, coupled], axis=0))
         result[:, here] = (spread[:, here] - correction).astype(bf16)
+    result[:, INNER:] = jnp.zeros((PART_ROWS, RIM), bf16)
 
 
 def ghost_kernel(whole, first, second, first_coupled, second_coupled, spikes, result):
@@ -355,15 +356,15 @@
 
     result = pl.pallas_call(
         finish_kernel,
-        grid=(CELLS // 512,),
+        grid=(PARTS,),
         in_specs=[
-            pl.BlockSpec((ROWS, 512), lambda i: (0, i)),
-            pl.BlockSpec((2, 3 * EDGE, 256), lambda i: (i, 0, 0)),
-            whole((ROWS, 128)),
-        ],
-        out_specs=pl.BlockSpec((ROWS, 512), lambda i: (0, i)),
+            pl.BlockSpec((PART_ROWS, CELLS), lambda i: (i, 0)),
+            whole((BLOCKS, 3 * EDGE, 256)),
+            pl.BlockSpec((PART_ROWS, 128), lambda i: (i, 0)),
+        ],
+        out_specs=pl.BlockSpec((PART_ROWS, CELLS), lambda i: (i, 0)),
         out_shape=jax.ShapeDtypeStruct((ROWS, CELLS), bf16),
-        compiler_params=params(6),
+        compiler_params=params(8),
         name="finish",
     )(spread, shared, spikes)
 

time: 74.3 us -> 74.3 us (level)
  transfers between devices with their start and end apart: 15 -> 15, of which waited for: 4 -> 4; matrix products, arithmetic and copies ran while one was open for 0% -> 0% of each run, Pallas kernels for 11% -> 10%
where the time goes in v7:
time: 74.3 us; the launch traced here: 73.2 us
  starting transfers between devices  32.6 us (44%)
  Pallas kernels  19.8 us (27%)
  waiting for transfers between devices  18.6 us (25%)
  local copies, waits for them, and re-layouts  2.07 us (3%)
    ppermute x7, starting transfers between devices, shards(): lax.ppermute(chunks[shift], 'rad', [(k, (k + shift) % BLOCKS) for k in ra...  9.95 us
    all_to_all x1, waiting for transfers between devices, shards(): shared = lax.all_to_all(shared, 'rad', 0, 0)  9.8 us
    pallas_call x1, Pallas kernels, shards(): pl.pallas_call(head_kernel, in_specs=[SMEM] + [ANY] * 4, out_specs=[ANY]...  8.93 us
    ppermute x2, starting transfers between devices, shards(): metas = [lax.ppermute(meta, 'ang', crossing(m, True)) for m in range(2)]  6.37 us
    all_to_all x1, starting transfers between devices, shards(): shared = lax.all_to_all(shared, 'rad', 0, 0)  5.65 us
    all_to_all x1, starting transfers between devices, shards(): donors = lax.all_to_all(lists, 'ang', 0, 0, axis_index_groups=groups)  5.51 us
    ppermute x4, starting transfers between devices, shards(): lax.ppermute(value, 'ang', crossing(m, False))  5.07 us
    ppermute x4, waiting for transfers between devices, shards(): lax.ppermute(value, 'ang', crossing(m, False))  4.84 us
  transfers between devices with their start and end apart: 15, of which 4 were waited for; matrix products, arithmetic and copies ran while one was open for 0% of the time, Pallas kernels for 10%

profile of v7, /device:TPU:33, one launch (start us, length us, event | category | flops | bytes accessed | tf_op | source)
XLA Modules:
  0.0 73.2 jit_solution(13667246856638662288)
XLA Ops:
  0.0 8.9 %head.1 = (f32[432,2048]{1,0:T(8,128)}, bf16[8,432,256]{2,1,0:T(8,128)(2,1)}, bf16[64,256]{1,0:T(8,128)(2,1)}, bf16[64,256]{1,0:T(8,128)(2,1)}, bf16[64,256]{1,0...) custom-call(s32[1,32]{1,0:T(1,128)} %block_size.1, ...), custom_call_target="tpu_custom_call" | custom-call | tf_op jit(solution)/shard_map/head/pallas_call | solution.py:267
  9.0 0.0 copy-start.1
  9.0 0.0 copy-start.3
  9.0 0.0 copy-start.4
  9.0 0.0 copy-start.5
  9.1 0.0 copy-start.6
  9.1 5.5 %all-to-all-start = ((bf16[8,432,256]{2,1,0:T(8,128)(2,1)}), bf16[8,432,256]{2,1,0:T(8,128)(2,1)S(1)}, u32[]{:S(2)}, u32[]{:S(2)}) async-start(bf16[8,432,256]{2,1,0:T(8,128)(2,1)} %get-tuple-element.37), calls=%async_computation | async-start | bytes 3538944 | tf_op jit(solution)/shard_map/all_to_all | solution.py:292
  14.6 2.3 %collective-permute-start = (bf16[64,256]{1,0:T(8,128)(2,1)S(1)}, bf16[64,256]{1,0:T(8,128)(2,1)S(1)}, u32[]{:S(2)}, u32[]{:S(2)}) collective-permute-start(bf16[64,256]{1,0:T(8,128)(2,1)S(1)} %copy-done.13), channel_id=1, source_target_pairs={{0,1},{1,2},{2,3},{3,4},{4,5},{5,6},{6,7},{7,0},{8,9},{9,10},{10,1... | collective-permute-start | bytes 98312 | tf_op jit(solution)/shard_map/ppermute | solution.py:294
  16.9 1.2 %collective-permute-start.1 = (bf16[64,256]{1,0:T(8,128)(2,1)S(1)}, bf16[64,256]{1,0:T(8,128)(2,1)S(1)}, u32[]{:S(2)}, u32[]{:S(2)}) collective-permute-start(bf16[64,256]{1,0:T(8,128)(2,1)S(1)} %copy-done.12), channel_id=1, source_target_pairs={{0,2},{1,3},{2,4},{3,5},{4,6},{5,7},{6,0},{7,1},{8,10},{9,11},{10,... | collective-permute-start | bytes 98312 | tf_op jit(solution)/shard_map/ppermute | solution.py:294
  18.1 1.6 %collective-permute-start.2 = (bf16[64,256]{1,0:T(8,128)(2,1)S(1)}, bf16[64,256]{1,0:T(8,128)(2,1)S(1)}, u32[]{:S(2)}, u32[]{:S(2)}) collective-permute-start(bf16[64,256]{1,0:T(8,128)(2,1)S(1)} %copy-done.11), channel_id=1, source_target_pairs={{0,3},{1,4},{2,5},{3,6},{4,7},{5,0},{6,1},{7,2},{8,11},{9,12},{10,... | collective-permute-start | bytes 98312 | tf_op jit(solution)/shard_map/ppermute | solution.py:294
  19.8 0.5 collective-permute-start.3
  20.3 1.9 %collective-permute-start.4 = (bf16[64,256]{1,0:T(8,128)(2,1)S(1)}, bf16[64,256]{1,0:T(8,128)(2,1)S(1)}, u32[]{:S(2)}, u32[]{:S(2)}) collective-permute-start(bf16[64,256]{1,0:T(8,128)(2,1)S(1)} %copy-done.9), channel_id=1, source_target_pairs={{0,5},{1,6},{2,7},{3,0},{4,1},{5,2},{6,3},{7,4},{8,13},{9,14},{10,... | collective-permute-start | bytes 98312 | tf_op jit(solution)/shard_map/ppermute | solution.py:294
  22.2 0.7 collective-permute-start.5
  22.9 1.7 %collective-permute-start.6 = (bf16[64,256]{1,0:T(8,128)(2,1)S(1)}, bf16[64,256]{1,0:T(8,128)(2,1)S(1)}, u32[]{:S(2)}, u32[]{:S(2)}) collective-permute-start(bf16[64,256]{1,0:T(8,128)(2,1)S(1)} %copy-done.7), channel_id=1, source_target_pairs={{0,7},{1,0},{2,1},{3,2},{4,3},{5,4},{6,5},{7,6},{8,15},{9,8},{10,9... | collective-permute-start | bytes 98312 | tf_op jit(solution)/shard_map/ppermute | solution.py:294
  24.6 3.0 %setup.1 = (f32[16,128]{1,0:T(8,128)S(1)}, bf16[432,128]{1,0:T(8,128)(2,1)S(1)}, f32[8,256]{1,0:T(8,128)S(1)}) custom-call(f32[7]{0:T(128)S(1)} %copy-done.5, f32[7]{0:T(128)S(1)} %copy-done.6, f32[8,16,16]{2,1,0:T(8,128)S(1)} %copy-done.1, f32[8,16,16]{2,1,0:T(8,128)S(1)} %copy-done.1, s32[4,256]{1,0:T(4,128)S(1)} %copy-done.3, f32[4,256]{1,0:T(4,128)S(1)} %copy-done.4), custom_call_target="tpu_custom_call" | custom-call | tf_op jit(solution)/shard_map/setup/pallas_call | solution.py:298
  27.7 1.3 %solve.1 = (bf16[8,64,256]{2,1,0:T(8,128)(2,1)S(1)}, f32[8,256]{1,0:T(8,128)S(1)}) custom-call(f32[16,128]{1,0:T(8,128)S(1)} %get-tuple-element.26.needed, f32[8,256]{1,0:T(8,128)S(1)} %get-tuple-element.27.meta, bf16[64,256]{1,0:T(8,128)(2,1)S(1)} %copy-done.2, bf16[64,256]{1,0:T(8,128)(2,1)S(1)} %collective-permute-done.refs_1_, ...), custom_call_target="tpu_custom_call" | custom-call | tf_op jit(solution)/shard_map/solve/pallas_call | solution.py:318
  29.0 4.7 %collective-permute-start.8 = (f32[8,256]{1,0:T(8,128)S(1)}, f32[8,256]{1,0:T(8,128)S(1)}, u32[]{:S(2)}, u32[]{:S(2)}) collective-permute-start(f32[8,256]{1,0:T(8,128)S(1)} %get-tuple-element.36), channel_id=1, source_target_pairs={{160,0},{168,8},{176,16},{184,24},{128,32},{136,40},{144,48},{152,... | collective-permute-start | bytes 24584 | tf_op jit(solution)/shard_map/ppermute | solution.py:330
  33.7 1.7 %collective-permute-start.7 = (f32[8,256]{1,0:T(8,128)S(1)}, f32[8,256]{1,0:T(8,128)S(1)}, u32[]{:S(2)}, u32[]{:S(2)}) collective-permute-start(f32[8,256]{1,0:T(8,128)S(1)} %get-tuple-element.36), channel_id=1, source_target_pairs={{224,0},{232,8},{240,16},{248,24},{192,32},{200,40},{208,48},{216,... | collective-permute-start | bytes 24584 | tf_op jit(solution)/shard_map/ppermute | solution.py:330
  35.4 4.0 %collective-permute-done.7.first_meta = f32[8,256]{1,0:T(8,128)S(1)} collective-permute-done((f32[8,256]{1,0:T(8,128)S(1)}, f32[8,256]{1,0:T(8,128)S(1)}, u32[]{:S(2)}, u32[]{:S(2)}) %collective-permute-start.7) | collective-permute-done | bytes 8224 | tf_op jit(solution)/shard_map/ppermute | solution.py:330
  39.3 2.5 %partial.1 = (bf16[432,256]{1,0:T(8,128)(2,1)S(1)}, bf16[432,256]{1,0:T(8,128)(2,1)S(1)}, bf16[8,192,256]{2,1,0:T(8,128)(2,1)}) custom-call(f32[8,256]{1,0:T(8,128)S(1)} %collective-permute-done.7.first_meta, f32[8,256]{1,0:T(8,128)S(1)} %collective-permute-done.8.second_meta, bf16[8,432,256]{2,1,0:T(8,128)(2,1)S(1)} %all-to-all-done.lists, ...), custom_call_target="tpu_custom_call" | custom-call | tf_op jit(solution)/shard_map/partial/pallas_call | solution.py:331
  41.8 5.7 %all-to-all-start.1 = ((bf16[8,192,256]{2,1,0:T(8,128)(2,1)}), bf16[8,192,256]{2,1,0:T(8,128)(2,1)S(1)}, u32[]{:S(2)}, u32[]{:S(2)}) async-start(bf16[8,192,256]{2,1,0:T(8,128)(2,1)} %get-tuple-element.39), calls=%async_computation.1 | async-start | bytes 1572864 | tf_op jit(solution)/shard_map/all_to_all | solution.py:344
  47.4 2.2 %collective-permute-start.9 = (bf16[432,256]{1,0:T(8,128)(2,1)S(1)}, bf16[432,256]{1,0:T(8,128)(2,1)S(1)}, u32[]{:S(2)}, u32[]{:S(2)}) collective-permute-start(bf16[432,256]{1,0:T(8,128)(2,1)S(1)} %get-tuple-element.41), channel_id=1, source_target_pairs={{0,224},{8,232},{16,240},{24,248},{32,192},{40,200},{48,208},{56,2... | collective-permute-start | bytes 663560 | tf_op jit(solution)/shard_map/ppermute | solution.py:345
  49.7 0.3 collective-permute-start.10
  49.9 9.8 %all-to-all-done.1.shared = bf16[8,192,256]{2,1,0:T(8,128)(2,1)S(1)} async-done(((bf16[8,192,256]{2,1,0:T(8,128)(2,1)}), bf16[8,192,256]{2,1,0:T(8,128)(2,1)S(1)}, u32[]{:S(2)}, u32[]{:S(2)}) %all-to-all-start.1) | async-done | bytes 786464 | tf_op jit(solution)/shard_map/all_to_all | solution.py:344
  59.7 0.9 %own.1 = (bf16[64,256]{1,0:T(8,128)(2,1)S(1)}, bf16[64,256]{1,0:T(8,128)(2,1)S(1)}) custom-call(f32[16,128]{1,0:T(8,128)S(1)} %get-tuple-element.26.needed, bf16[8,192,256]{2,1,0:T(8,128)(2,1)S(1)} %all-to-all-done.1.shared), custom_call_target="tpu_custom_call" | custom-call | tf_op jit(solution)/shard_map/own/pallas_call | solution.py:347
  60.6 2.3 %collective-permute-start.11 = (bf16[64,256]{1,0:T(8,128)(2,1)S(1)}, bf16[64,256]{1,0:T(8,128)(2,1)S(1)}, u32[]{:S(2)}, u32[]{:S(2)}) collective-permute-start(bf16[64,256]{1,0:T(8,128)(2,1)S(1)} %get-tuple-element.43), channel_id=1, source_target_pairs={{0,224},{8,232},{16,240},{24,248},{32,192},{40,200},{48,208},{56,2... | collective-permute-start | bytes 98312 | tf_op jit(solution)/shard_map/ppermute | solution.py:355
  62.9 0.3 collective-permute-start.12
  63.2 2.0 %copy-done = f32[432,2048]{1,0:T(8,128)S(1)} copy-done((f32[432,2048]{1,0:T(8,128)S(1)}, f32[432,2048]{1,0:T(8,128)}, u32[]{:S(2)}) %copy-start) | copy-done | bytes 3538968
  65.2 2.2 %finish.1.whole = bf16[432,2048]{1,0:T(8,128)(2,1)} custom-call(f32[432,2048]{1,0:T(8,128)S(1)} %copy-done, bf16[8,192,256]{2,1,0:T(8,128)(2,1)S(1)} %all-to-all-done.1.shared, bf16[432,128]{1,0:T(8,128)(2,1)S(1)} %get-tuple-element.40.spikes), custom_call_target="tpu_custom_call" | custom-call | tf_op jit(solution)/shard_map/finish/pallas_call | solution.py:357
  67.4 3.7 %collective-permute-done.10.second = bf16[432,256]{1,0:T(8,128)(2,1)S(1)} collective-permute-done((bf16[432,256]{1,0:T(8,128)(2,1)S(1)}, bf16[432,256]{1,0:T(8,128)(2,1)S(1)}, u32[]{:S(2)}, u32[]{:S(2)}) %collective-permute-start.10) | collective-permute-done | bytes 221216 | tf_op jit(solution)/shard_map/ppermute | solution.py:345
  71.1 1.1 %collective-permute-done.12.second_coupled = bf16[64,256]{1,0:T(8,128)(2,1)S(1)} collective-permute-done((bf16[64,256]{1,0:T(8,128)(2,1)S(1)}, bf16[64,256]{1,0:T(8,128)(2,1)S(1)}, u32[]{:S(2)}, u32[]{:S(2)}) %collective-permute-start.12) | collective-permute-done | bytes 32800 | tf_op jit(solution)/shard_map/ppermute | solution.py:355
  72.3 1.0 %ghosts.1 = bf16[432,2048]{1,0:T(8,128)(2,1)} custom-call(bf16[432,2048]{1,0:T(8,128)(2,1)} %finish.1.whole, bf16[432,256]{1,0:T(8,128)(2,1)S(1)} %collective-permute-done.9.first, bf16[432,256]{1,0:T(8,128)(2,1)S(1)} %collective-permute-done.10.second, bf16[64,256]{1,0:T(8,128)(2,1)S(1)} %collective-permute-done.11.first_coupled, ...), custom_call_target="tpu_custom_call", output_to_operand_aliasing={{}: (0, {})} | custom-call | tf_op jit(solution)/shard_map/ghosts/pallas_call | solution.py:371
  (33 shorter events, 0.1 us)
Async XLA Ops:
  8.9 5.7 %copy-start.13 = (bf16[64,256]{1,0:T(8,128)(2,1)S(1)}, bf16[64,256]{1,0:T(8,128)(2,1)}, u32[]{:S(2)}) copy-start(bf16[64,256]{1,0:T(8,128)(2,1)} %get-tuple-element.29) | copy-start | bytes 98308
  8.9 8.0 %copy-start.12 = (bf16[64,256]{1,0:T(8,128)(2,1)S(1)}, bf16[64,256]{1,0:T(8,128)(2,1)}, u32[]{:S(2)}) copy-start(bf16[64,256]{1,0:T(8,128)(2,1)} %get-tuple-element.30) | copy-start | bytes 98308
  9.0 9.2 %copy-start.11 = (bf16[64,256]{1,0:T(8,128)(2,1)S(1)}, bf16[64,256]{1,0:T(8,128)(2,1)}, u32[]{:S(2)}) copy-start(bf16[64,256]{1,0:T(8,128)(2,1)} %get-tuple-element.31) | copy-start | bytes 98308
  9.0 10.8 %copy-start.10 = (bf16[64,256]{1,0:T(8,128)(2,1)S(1)}, bf16[64,256]{1,0:T(8,128)(2,1)}, u32[]{:S(2)}) copy-start(bf16[64,256]{1,0:T(8,128)(2,1)} %get-tuple-element.32) | copy-start | bytes 98308
  9.0 11.3 %copy-start.9 = (bf16[64,256]{1,0:T(8,128)(2,1)S(1)}, bf16[64,256]{1,0:T(8,128)(2,1)}, u32[]{:S(2)}) copy-start(bf16[64,256]{1,0:T(8,128)(2,1)} %get-tuple-element.33) | copy-start | bytes 98308
  9.0 13.2 %copy-start.8 = (bf16[64,256]{1,0:T(8,128)(2,1)S(1)}, bf16[64,256]{1,0:T(8,128)(2,1)}, u32[]{:S(2)}) copy-start(bf16[64,256]{1,0:T(8,128)(2,1)} %get-tuple-element.34) | copy-start | bytes 98308
  9.0 13.9 %copy-start.7 = (bf16[64,256]{1,0:T(8,128)(2,1)S(1)}, bf16[64,256]{1,0:T(8,128)(2,1)}, u32[]{:S(2)}) copy-start(bf16[64,256]{1,0:T(8,128)(2,1)} %get-tuple-element.35) | copy-start | bytes 98308
  9.0 15.6 %copy-start.1 = (f32[8,16,16]{2,1,0:T(8,128)S(1)}, f32[8,16,16]{2,1,0:T(8,128)}, u32[]{:S(2)}) copy-start(f32[8,16,16]{2,1,0:T(8,128)} %block_inverse.1) | copy-start | bytes 24580
  9.0 15.6 %copy-start.3 = (s32[4,256]{1,0:T(4,128)S(1)}, s32[4,256]{1,0:T(4,128)}, u32[]{:S(2)}) copy-start(s32[4,256]{1,0:T(4,128)} %slots.1) | copy-start | bytes 12292
  9.0 15.5 %copy-start.4 = (f32[4,256]{1,0:T(4,128)S(1)}, f32[4,256]{1,0:T(4,128)}, u32[]{:S(2)}) copy-start(f32[4,256]{1,0:T(4,128)} %factors.1) | copy-start | bytes 12292
  9.0 15.5 %copy-start.5 = (f32[7]{0:T(128)S(1)}, f32[7]{0:T(128)}, u32[]{:S(2)}) copy-start(f32[7]{0:T(128)} %lower.1) | copy-start | bytes 88
  9.1 15.5 %copy-start.6 = (f32[7]{0:T(128)S(1)}, f32[7]{0:T(128)}, u32[]{:S(2)}) copy-start(f32[7]{0:T(128)} %upper.1) | copy-start | bytes 88
  9.1 18.6 %copy-start.2 = (bf16[64,256]{1,0:T(8,128)(2,1)S(1)}, bf16[64,256]{1,0:T(8,128)(2,1)}, u32[]{:S(2)}) copy-start(bf16[64,256]{1,0:T(8,128)(2,1)} %get-tuple-element.28.refs_0_) | copy-start | bytes 98308
  9.1 30.2 %all-to-all-start = ((bf16[8,432,256]{2,1,0:T(8,128)(2,1)}), bf16[8,432,256]{2,1,0:T(8,128)(2,1)S(1)}, u32[]{:S(2)}, u32[]{:S(2)}) async-start(bf16[8,432,256]{2,1,0:T(8,128)(2,1)} %get-tuple-element.37), calls=%async_computation | async-start | bytes 3538944 | tf_op jit(solution)/shard_map/all_to_all | solution.py:292
  14.6 7.6 %collective-permute-start = (bf16[64,256]{1,0:T(8,128)(2,1)S(1)}, bf16[64,256]{1,0:T(8,128)(2,1)S(1)}, u32[]{:S(2)}, u32[]{:S(2)}) collective-permute-start(bf16[64,256]{1,0:T(8,128)(2,1)S(1)} %copy-done.13), channel_id=1, source_target_pairs={{0,1},{1,2},{2,3},{3,4},{4,5},{5,6},{6,7},{7,0},{8,9},{9,10},{10,1... | collective-permute-start | bytes 98312 | tf_op jit(solution)/shard_map/ppermute | solution.py:294
  16.9 6.0 %collective-permute-start.1 = (bf16[64,256]{1,0:T(8,128)(2,1)S(1)}, bf16[64,256]{1,0:T(8,128)(2,1)S(1)}, u32[]{:S(2)}, u32[]{:S(2)}) collective-permute-start(bf16[64,256]{1,0:T(8,128)(2,1)S(1)} %copy-done.12), channel_id=1, source_target_pairs={{0,2},{1,3},{2,4},{3,5},{4,6},{5,7},{6,0},{7,1},{8,10},{9,11},{10,... | collective-permute-start | bytes 98312 | tf_op jit(solution)/shard_map/ppermute | solution.py:294
  18.1 9.5 %collective-permute-start.2 = (bf16[64,256]{1,0:T(8,128)(2,1)S(1)}, bf16[64,256]{1,0:T(8,128)(2,1)S(1)}, u32[]{:S(2)}, u32[]{:S(2)}) collective-permute-start(bf16[64,256]{1,0:T(8,128)(2,1)S(1)} %copy-done.11), channel_id=1, source_target_pairs={{0,3},{1,4},{2,5},{3,6},{4,7},{5,0},{6,1},{7,2},{8,11},{9,12},{10,... | collective-permute-start | bytes 98312 | tf_op jit(solution)/shard_map/ppermute | solution.py:294
  19.8 7.9 %collective-permute-start.3 = (bf16[64,256]{1,0:T(8,128)(2,1)S(1)}, bf16[64,256]{1,0:T(8,128)(2,1)S(1)}, u32[]{:S(2)}, u32[]{:S(2)}) collective-permute-start(bf16[64,256]{1,0:T(8,128)(2,1)S(1)} %copy-done.10), channel_id=1, source_target_pairs={{0,4},{1,5},{2,6},{3,7},{4,0},{5,1},{6,2},{7,3},{8,12},{9,13},{10,... | collective-permute-start | bytes 98312 | tf_op jit(solution)/shard_map/ppermute | solution.py:294
  20.3 7.4 %collective-permute-start.4 = (bf16[64,256]{1,0:T(8,128)(2,1)S(1)}, bf16[64,256]{1,0:T(8,128)(2,1)S(1)}, u32[]{:S(2)}, u32[]{:S(2)}) collective-permute-start(bf16[64,256]{1,0:T(8,128)(2,1)S(1)} %copy-done.9), channel_id=1, source_target_pairs={{0,5},{1,6},{2,7},{3,0},{4,1},{5,2},{6,3},{7,4},{8,13},{9,14},{10,... | collective-permute-start | bytes 98312 | tf_op jit(solution)/shard_map/ppermute | solution.py:294
  22.2 5.4 %collective-permute-start.5 = (bf16[64,256]{1,0:T(8,128)(2,1)S(1)}, bf16[64,256]{1,0:T(8,128)(2,1)S(1)}, u32[]{:S(2)}, u32[]{:S(2)}) collective-permute-start(bf16[64,256]{1,0:T(8,128)(2,1)S(1)} %copy-done.8), channel_id=1, source_target_pairs={{0,6},{1,7},{2,0},{3,1},{4,2},{5,3},{6,4},{7,5},{8,14},{9,15},{10,... | collective-permute-start | bytes 98312 | tf_op jit(solution)/shard_map/ppermute | solution.py:294
  22.9 4.8 %collective-permute-start.6 = (bf16[64,256]{1,0:T(8,128)(2,1)S(1)}, bf16[64,256]{1,0:T(8,128)(2,1)S(1)}, u32[]{:S(2)}, u32[]{:S(2)}) collective-permute-start(bf16[64,256]{1,0:T(8,128)(2,1)S(1)} %copy-done.7), channel_id=1, source_target_pairs={{0,7},{1,0},{2,1},{3,2},{4,3},{5,4},{6,5},{7,6},{8,15},{9,8},{10,9... | collective-permute-start | bytes 98312 | tf_op jit(solution)/shard_map/ppermute | solution.py:294
  29.0 6.4 %collective-permute-start.8 = (f32[8,256]{1,0:T(8,128)S(1)}, f32[8,256]{1,0:T(8,128)S(1)}, u32[]{:S(2)}, u32[]{:S(2)}) collective-permute-start(f32[8,256]{1,0:T(8,128)S(1)} %get-tuple-element.36), channel_id=1, source_target_pairs={{160,0},{168,8},{176,16},{184,24},{128,32},{136,40},{144,48},{152,... | collective-permute-start | bytes 24584 | tf_op jit(solution)/shard_map/ppermute | solution.py:330
  33.7 5.7 %collective-permute-start.7 = (f32[8,256]{1,0:T(8,128)S(1)}, f32[8,256]{1,0:T(8,128)S(1)}, u32[]{:S(2)}, u32[]{:S(2)}) collective-permute-start(f32[8,256]{1,0:T(8,128)S(1)} %get-tuple-element.36), channel_id=1, source_target_pairs={{224,0},{232,8},{240,16},{248,24},{192,32},{200,40},{208,48},{216,... | collective-permute-start | bytes 24584 | tf_op jit(solution)/shard_map/ppermute | solution.py:330
  41.8 17.9 %all-to-all-start.1 = ((bf16[8,192,256]{2,1,0:T(8,128)(2,1)}), bf16[8,192,256]{2,1,0:T(8,128)(2,1)S(1)}, u32[]{:S(2)}, u32[]{:S(2)}) async-start(bf16[8,192,256]{2,1,0:T(8,128)(2,1)} %get-tuple-element.39), calls=%async_computation.1 | async-start | bytes 1572864 | tf_op jit(solution)/shard_map/all_to_all | solution.py:344
  47.4 20.0 %collective-permute-start.9 = (bf16[432,256]{1,0:T(8,128)(2,1)S(1)}, bf16[432,256]{1,0:T(8,128)(2,1)S(1)}, u32[]{:S(2)}, u32[]{:S(2)}) collective-permute-start(bf16[432,256]{1,0:T(8,128)(2,1)S(1)} %get-tuple-element.41), channel_id=1, source_target_pairs={{0,224},{8,232},{16,240},{24,248},{32,192},{40,200},{48,208},{56,2... | collective-permute-start | bytes 663560 | tf_op jit(solution)/shard_map/ppermute | solution.py:345
  49.7 21.5 %collective-permute-start.10 = (bf16[432,256]{1,0:T(8,128)(2,1)S(1)}, bf16[432,256]{1,0:T(8,128)(2,1)S(1)}, u32[]{:S(2)}, u32[]{:S(2)}) collective-permute-start(bf16[432,256]{1,0:T(8,128)(2,1)S(1)} %get-tuple-element.42), channel_id=1, source_target_pairs={{0,160},{8,168},{16,176},{24,184},{32,128},{40,136},{48,144},{56,1... | collective-permute-start | bytes 663560 | tf_op jit(solution)/shard_map/ppermute | solution.py:345
  60.6 10.5 %collective-permute-start.11 = (bf16[64,256]{1,0:T(8,128)(2,1)S(1)}, bf16[64,256]{1,0:T(8,128)(2,1)S(1)}, u32[]{:S(2)}, u32[]{:S(2)}) collective-permute-start(bf16[64,256]{1,0:T(8,128)(2,1)S(1)} %get-tuple-element.43), channel_id=1, source_target_pairs={{0,224},{8,232},{16,240},{24,248},{32,192},{40,200},{48,208},{56,2... | collective-permute-start | bytes 98312 | tf_op jit(solution)/shard_map/ppermute | solution.py:355
  62.9 9.3 %collective-permute-start.12 = (bf16[64,256]{1,0:T(8,128)(2,1)S(1)}, bf16[64,256]{1,0:T(8,128)(2,1)S(1)}, u32[]{:S(2)}, u32[]{:S(2)}) collective-permute-start(bf16[64,256]{1,0:T(8,128)(2,1)S(1)} %get-tuple-element.44), channel_id=1, source_target_pairs={{0,160},{8,168},{16,176},{24,184},{32,128},{40,136},{48,144},{56,1... | collective-permute-start | bytes 98312 | tf_op jit(solution)/shard_map/ppermute | solution.py:355
  63.2 2.0 %copy-start = (f32[432,2048]{1,0:T(8,128)S(1)}, f32[432,2048]{1,0:T(8,128)}, u32[]{:S(2)}) copy-start(f32[432,2048]{1,0:T(8,128)} %get-tuple-element.25.spread) | copy-start | bytes 10616836
